TPU v7x, 256 devices: a whole 4x4x8 slice. The times are simulated.
256 devices in a mesh: group: 2 (over y_hi), fsdp: 16 (over y_lo, x, core), tp: 8 (over z).
Axes of the slice: x: 4, y: 4 (y_hi: 2, y_lo: 2; y = y_hi * 2 + y_lo), z: 8, core: 2. Of those that a mesh axis runs over, the one named last changes fastest.
Arguments:
- hidden: bfloat16 [2, 12288, 8192], P('group', 'fsdp', 'tp'), may hold values from -6 to 6
- cotangent: bfloat16 [12288, 2, 1024], P('fsdp', None, 'tp'), may hold values from -6 to 6
- queries: bfloat16 [12288, 8192], P('fsdp', 'tp'), may hold values from -160 to 160, as said below
- kv_cache: bfloat16 [6144, 2, 16, 1024], P('fsdp', None, None, 'tp'), may hold values from -7 to 7
- lengths: int32 [6144], P('fsdp'), may hold values from 2 to 16, as said below
- master: float32 [1024, 2, 8192], P('fsdp', None, 'tp'), may hold values from -4 to 4
- moment1: float32 [1024, 2, 8192], P('fsdp', None, 'tp'), may hold values from -1.5 to 1.5
- moment2: float32 [1024, 2, 8192], P('fsdp', None, 'tp'), may hold values from 0.002 to 0.02
Outputs:
- results: bfloat16 [2, 12288, 8192], P('group', 'fsdp', 'tp')
- new_master: float32 [1024, 2, 8192], P('fsdp', None, 'tp')
- new_first: float32 [1024, 2, 8192], P('fsdp', None, 'tp')
- new_second: float32 [1024, 2, 8192], P('fsdp', None, 'tp')
Inputs may be any that keep to these rules, and one draw needn't show every extreme that they name: `queries`: token 2 * r + s is step s of rollout row r. `lengths`: the first of every 384 rows has all 16 positions in use.
All inputs are finite; a program needn't handle non-finite values.
Results may differ from a plain program's by a relative error of at most 0.0052.
Values may be sent and summed in bfloat16 or wider, within the bound.
No kernel may reach another device: no remote copies, remote signals or barrier semaphores. Data moves between devices by JAX's collectives and lax.ppermute only.
A program may use at most 192 MiB of HBM per device.

v0:
```python
import math

import jax
import jax.numpy as jnp
from jax import lax
from jax.sharding import PartitionSpec as P

D = 8192
HD = 128
STEPS = 2
OPT_STEP = 100


first_decay = 0.9
second_decay = 0.95
learn_rate = 0.15
weight_decay = 0.1
small_term = 1e-08


def passed_along(block, axis, distance):
    devices = range(lax.axis_size(axis))
    route = [(i - distance, i) for i in devices if i - distance in devices]
    return lax.ppermute(block, axis, route)


def attend(queries, kv_cache, fresh, lengths):
    row_count = queries.shape[0] // STEPS
    cached_len = kv_cache.shape[2]
    kv_heads = fresh.shape[2] // HD
    groups = queries.shape[1] // fresh.shape[2]
    query = queries.reshape(row_count, STEPS, kv_heads, groups, HD)
    keys_old = kv_cache[:, 0].reshape(row_count, cached_len, kv_heads, HD)
    values_old = kv_cache[:, 1].reshape(row_count, cached_len, kv_heads, HD)
    keys_new = fresh[:, 0].reshape(row_count, STEPS, kv_heads, HD)
    values_new = fresh[:, 1].reshape(row_count, STEPS, kv_heads, HD)
    root = 1.0 / math.sqrt(HD)
    old_scores = (
        jnp.einsum("rskgd,rpkd->rskgp", query, keys_old, preferred_element_type=jnp.float32) * root
    )
    new_scores = (
        jnp.einsum("rskgd,rjkd->rskgj", query, keys_new, preferred_element_type=jnp.float32) * root
    )
    old_mask = (jnp.arange(cached_len, dtype=jnp.int32)[None, :] < lengths[:, None])[
        :, None, None, None, :
    ]
    new_mask = (jnp.arange(STEPS)[None, :] <= jnp.arange(STEPS)[:, None])[None, :, None, None, :]
    top = jnp.maximum(
        jnp.max(jnp.where(old_mask, old_scores, -jnp.inf), axis=-1, keepdims=True),
        jnp.max(jnp.where(new_mask, new_scores, -jnp.inf), axis=-1, keepdims=True),
    )
    old_exp = jnp.where(old_mask, jnp.exp(old_scores - top), 0.0)
    new_exp = jnp.where(new_mask, jnp.exp(new_scores - top), 0.0)
    total = jnp.sum(old_exp, axis=-1, keepdims=True) + jnp.sum(new_exp, axis=-1, keepdims=True)
    old_probs = (old_exp / total).astype(jnp.bfloat16)
    new_probs = (new_exp / total).astype(jnp.bfloat16)
    mixed = jnp.einsum(
        "rskgp,rpkd->rskgd", old_probs, values_old, preferred_element_type=jnp.float32
    )
    mixed = mixed + jnp.einsum(
        "rskgj,rjkd->rskgd", new_probs, values_new, preferred_element_type=jnp.float32
    )
    return mixed.astype(jnp.bfloat16).reshape(row_count * STEPS, queries.shape[1])


def on_device(hidden, cotangent, queries, kv_cache, lengths, master, moment1, moment2):
    half_index = lax.axis_index("group")
    rows_in = hidden[0]
    scale = 1.0 / math.sqrt(D)
    gathered_cot = lax.all_gather(cotangent, "tp", axis=2, tiled=True)
    old_weights = master.astype(jnp.bfloat16)
    columns = gathered_cot
    input_grad = (
        jnp.einsum(
            "tgn,ngc->tc",
            columns,
            lax.all_gather(old_weights, "fsdp", axis=0, tiled=True),
            preferred_element_type=jnp.float32,
        )
        * scale
    )
    columns = gathered_cot
    gradient = (
        lax.psum_scatter(
            jnp.einsum("tgn,tc->ngc", columns, rows_in, preferred_element_type=jnp.float32),
            "fsdp",
            scatter_dimension=0,
            tiled=True,
        )
        * scale
    )
    mirrored = passed_along(gradient, "group", 1)
    gradient = jnp.where(half_index == 0, gradient, mirrored)
    new_first = first_decay * moment1 + (1.0 - first_decay) * gradient
    new_second = second_decay * moment2 + (1.0 - second_decay) * gradient * gradient
    first_hat = new_first / (1.0 - first_decay**OPT_STEP)
    second_hat = new_second / (1.0 - second_decay**OPT_STEP)
    new_master = master - learn_rate * (
        first_hat / (jnp.sqrt(second_hat) + small_term) + weight_decay * master
    )
    serving = new_master.astype(jnp.bfloat16)
    partial_kv = jnp.einsum(
        "tc,ngc->tgn",
        rows_in,
        lax.all_gather(serving, "fsdp", axis=0, tiled=True),
        preferred_element_type=jnp.float32,
    )
    head_width = cotangent.shape[2]
    summed = lax.psum(partial_kv, "tp")
    own_kv = lax.dynamic_slice_in_dim(summed, lax.axis_index("tp") * head_width, head_width, 2)
    fresh = (own_kv * scale).astype(jnp.bfloat16)
    attention = attend(queries, kv_cache, fresh, lengths)
    block = jnp.where(half_index == 0, input_grad.astype(jnp.bfloat16), attention)
    return (block[None], new_master, new_first, new_second)


def solution(mesh):
    in_specs = (
        P("group", "fsdp", "tp"),
        P("fsdp", None, "tp"),
        P("fsdp", "tp"),
        P("fsdp", None, None, "tp"),
        P("fsdp"),
        P("fsdp", None, "tp"),
        P("fsdp", None, "tp"),
        P("fsdp", None, "tp"),
    )
    out_specs = (
        P("group", "fsdp", "tp"),
        P("fsdp", None, "tp"),
        P("fsdp", None, "tp"),
        P("fsdp", None, "tp"),
    )
    return jax.shard_map(
        on_device, mesh=mesh, in_specs=in_specs, out_specs=out_specs, check_vma=False
    )
```

profile of v0, /device:TPU:121, one launch (start us, length us, event | category | flops | bytes accessed | tf_op | source)
XLA Modules:
  0.0 508.2 jit_solution(4512937427150035072)
XLA Ops:
  7.2 0.0 all-gather.4.cloned.1.call-start
  7.2 1.9 copy.53
  9.1 0.0 all-gather.4.cloned.1.call-update
  9.2 0.0 all-reduce.6.cloned.1.call-start
  9.2 51.5 %all-gather.4.cloned.1.call-done = bf16[768,2,1024]{2,0,1:T(8,128)(2,1)} async-done(((bf16[768,2,128]{2,0,1:T(8,128)(2,1)}), bf16[768,2,1024]{2,0,1:T(8,128)(2,1)}) %all-gather.4.cloned.1.call-update) | async-done | bytes 3145744 | tf_op jit(solution)/shard_map/all_gather | solution.py:70
  60.7 7.5 %convolution_bitcast_fusion = f32[1024,2,1024]{0,2,1:T(8,128)} fusion(bf16[768,2,1024]{2,0,1:T(8,128)(2,1)} %all-gather.4.cloned.1.call-done, bf16[1,768,1024]{2,1,0:T(8,128)(2,1)S(1)} %copy-done), kind=kOutput, calls=%fused_computation.2 | convolution fusion | flops 3221225472 | bytes 13107200 | tf_op jit(solution)/shard_map/tgn,tc->ngc/dot_general | solution.py:85
  68.2 13.4 %copy.58 = f32[1024,2,1024]{2,1,0:T(2,128)} copy(f32[1024,2,1024]{0,2,1:T(8,128)} %convolution_bitcast_fusion) | data formatting | bytes 16777216 | tf_op jit(solution)/shard_map/tgn,tc->ngc/transpose | solution.py:85
  81.6 0.0 all-reduce.6.cloned.1.call-update
  81.7 0.0 all-gather.8.cloned.1.call-start
  81.7 0.6 copy-done.13
  82.3 0.6 dynamic-slice
  83.5 148.4 %all-reduce.6.cloned.1.call-done = f32[1024,2,1024]{2,1,0:T(2,128)} async-done(((f32[1024,2,1024]{2,1,0:T(2,128)}), f32[1024,2,1024]{2,1,0:T(2,128)}) %all-reduce.6.cloned.1.call-update) | async-done | bytes 8388624
  231.9 1.1 constant_dynamic-slice_fusion
  233.0 1.0 copy_multiply_fusion.1
  234.0 1.3 collective-permute-start
  235.3 13.7 %collective-permute-done = f32[64,2,1024]{2,0,1:T(8,128)} collective-permute-done((f32[64,2,1024]{2,0,1:T(8,128)}, f32[64,2,1024]{2,0,1:T(8,128)}, u32[]{:S(2)}, u32[]{:S(2)}) %collective-permute-start) | collective-permute-done | bytes 524320 | tf_op jit(solution)/shard_map/ppermute | solution.py:24
  249.0 3.2 fusion.34
  252.2 1.0 copy.63
  253.2 0.0 all-gather.8.cloned.1.call-update
  253.2 0.0 all-reduce.4.cloned.1.call-start
  253.2 42.5 %all-gather.8.cloned.1.call-done = bf16[1024,2,1024]{2,1,0:T(2,128)(2,1)} async-done(((bf16[64,2,1024]{2,1,0:T(2,128)(2,1)}), bf16[1024,2,1024]{2,1,0:T(2,128)(2,1)}) %all-gather.8.cloned.1.call-update) | async-done | bytes 4194320 | tf_op jit(solution)/shard_map/all_gather | solution.py:105
  295.7 8.8 %fusion.8 = f32[768,2,1024]{0,2,1:T(8,128)} fusion(bf16[1024,2,1024]{2,1,0:T(2,128)(2,1)} %all-gather.8.cloned.1.call-done, bf16[1,768,1024]{2,1,0:T(8,128)(2,1)S(1)} %copy-done), kind=kOutput, calls=%fused_computation.15 | convolution fusion | flops 3221225472 | bytes 12058624 | tf_op jit(solution)/shard_map/tc,ngc->tgn/dot_general | solution.py:102
  304.5 0.0 all-reduce.4.cloned.1.call-update
  304.5 0.2 all-gather.6.cloned.1.call-start
  304.7 0.9 copy.99
  305.6 0.0 all-gather.6.cloned.1.call-update
  305.6 0.3 copy-done.6
  306.0 1.6 copy.79
  307.6 0.1 iota_compare_fusion
  307.7 3.2 fusion.4
  311.0 1.2 copy.68
  312.2 1.2 copy.69
  313.4 1.2 copy.70
  314.6 138.0 %all-reduce.4.cloned.1.call-done = f32[768,2,1024]{0,2,1:T(8,128)} async-done(((f32[768,2,1024]{0,2,1:T(8,128)}), f32[768,2,1024]{0,2,1:T(8,128)}) %all-reduce.4.cloned.1.call-update) | async-done | bytes 6291472 | tf_op jit(solution)/shard_map/psum | solution.py:109
  452.6 1.2 multiply_convert_fusion
  453.8 0.8 fusion.37
  454.6 1.7 copy.65
  456.3 1.7 copy.67
  458.1 8.8 %select_reduce_fusion = (f32[384,2,8]{2,1,0:T(2,128)S(1)}, f32[384,2,1,8,2]{3,4,1,0,2:T(2,128)S(1)}) fusion(pred[2,2]{1,0:T(4,128)(4,1)S(1)} %iota_compare_fusion.1, bf16[384,2,128,1]{2,1,3,0:T(2,128)(2,1)} %bitcast.111, bf16[384,2,8,128]{3,2,1,0:T(8,128)(2,1)} %bitcast.108), kind=kOutput, calls=%fused_computation.33 | convolution fusion | flops 3176448 | bytes 1843204 | tf_op jit(solution)/shard_map/rskgd,rjkd->rskgj/dot_general | solution.py:42
  466.9 0.2 max.8
  467.1 1.7 fusion.30
  468.8 2.4 bitcast_reduce_fusion
  471.2 0.2 add.41
  471.4 1.3 fusion.28
  472.7 0.6 copy-done.7
  473.3 4.0 fusion.2
  477.3 16.1 %all-gather.6.cloned.1.call-done = bf16[1024,2,1024]{2,0,1:T(8,128)(2,1)} async-done(((bf16[64,2,1024]{2,0,1:T(8,128)(2,1)}), bf16[1024,2,1024]{2,0,1:T(8,128)(2,1)}) %all-gather.6.cloned.1.call-update) | async-done | bytes 4194320 | tf_op jit(solution)/shard_map/all_gather | solution.py:77
  493.4 8.2 %fusion.11 = bf16[1,768,1024]{2,1,0:T(8,128)(2,1)} fusion(bf16[96,8,8,128]{3,2,1,0:T(8,128)(2,1)} %bitcast.112, pred[]{:T(512)S(6)} %eq.4, bf16[768,2,1024]{2,0,1:T(8,128)(2,1)} %all-gather.4.cloned.1.call-done, bf16[1024,2,1024]{2,0,1:T(8,128)(2,1)} %all-gather.6.cloned.1.call-done), kind=kOutput, calls=%fused_computation.17 | convolution fusion | flops 3223584768 | bytes 10485761 | tf_op jit(solution)/shard_map/tgn,ngc->tc/dot_general | solution.py:74
  (26 shorter events, 0.1 us)
Async XLA Ops:
  7.2 53.5 %copy-start = (bf16[1,768,1024]{2,1,0:T(8,128)(2,1)S(1)}, bf16[1,768,1024]{2,1,0:T(8,128)(2,1)}, u32[]{:S(2)}) copy-start(bf16[1,768,1024]{2,1,0:T(8,128)(2,1)} %param.8) | copy-start | bytes 4718596
  7.2 53.5 %all-gather.4.cloned.1.call-start = ((), (), s32[]{:S(2)}) async-start(), calls=%async_computation | async-start | bytes 3538944 | tf_op jit(solution)/shard_map/all_gather | solution.py:70
  9.2 222.8 %all-reduce.6.cloned.1.call-start = ((), (), s32[]{:S(2)}) async-start(), calls=%async_computation.4 | async-start | bytes 16777216
  81.6 0.7 copy-start.13
  81.6 167.4 %copy-start.2 = (f32[64,2,1024]{2,1,0:T(2,128)S(1)}, f32[64,2,1024]{2,1,0:T(2,128)}, u32[]{:S(2)}) copy-start(f32[64,2,1024]{2,1,0:T(2,128)} %param.13) | copy-start | bytes 1572868
  81.6 167.4 %copy-start.8 = (f32[64,2,1024]{2,1,0:T(2,128)S(1)}, f32[64,2,1024]{2,1,0:T(2,128)}, u32[]{:S(2)}) copy-start(f32[64,2,1024]{2,1,0:T(2,128)} %param.14) | copy-start | bytes 1572868
  81.7 214.0 %all-gather.8.cloned.1.call-start = ((), (), s32[]{:S(2)}) async-start(), calls=%async_computation.2 | async-start | bytes 4456448 | tf_op jit(solution)/shard_map/all_gather | solution.py:105
  234.0 15.0 %collective-permute-start = (f32[64,2,1024]{2,0,1:T(8,128)}, f32[64,2,1024]{2,0,1:T(8,128)}, u32[]{:S(2)}, u32[]{:S(2)}) collective-permute-start(f32[64,2,1024]{2,0,1:T(8,128)} %copy_multiply_fusion.1), channel_id=1, source_target_pairs={{0,128},{1,129},{2,130},{3,131},{4,132},{5,133},{6,134},{7,135},{8... | collective-permute-start | bytes 1572872 | tf_op jit(solution)/shard_map/ppermute | solution.py:24
  253.2 199.4 %all-reduce.4.cloned.1.call-start = ((), (), s32[]{:S(2)}) async-start(), calls=%async_computation.3 | async-start | bytes 12582912 | tf_op jit(solution)/shard_map/psum | solution.py:109
  304.5 1.5 copy-start.6
  304.5 3.1 copy-start.12
  304.5 188.9 %all-gather.6.cloned.1.call-start = ((), (), s32[]{:S(2)}) async-start(), calls=%async_computation.1 | async-start | bytes 4456448 | tf_op jit(solution)/shard_map/all_gather | solution.py:77
  307.7 3.3 copy-start.9
  307.7 3.3 copy-start.5
  307.7 4.5 copy-start.4
  307.7 5.7 %copy-start.3 = (f32[64,2,1024]{2,0,1:T(8,128)S(1)}, f32[64,2,1024]{2,0,1:T(8,128)}, u32[]{:S(2)}) copy-start(f32[64,2,1024]{2,0,1:T(8,128)} %get-tuple-element.19) | copy-start | bytes 1572868
  458.1 10.7 %copy-start.10 = (pred[384,16]{1,0:T(8,128)(4,1)S(1)}, pred[384,16]{1,0:T(8,128)(4,1)}, u32[]{:S(2)}) copy-start(pred[384,16]{1,0:T(8,128)(4,1)} %copy-done.9) | copy-start | bytes 18436
  467.1 4.3 copy-start.11
  471.4 1.9 copy-start.7
  493.4 8.2 %copy-start.1 = (bf16[1,768,1024]{2,1,0:T(8,128)(2,1)S(1)}, bf16[1,768,1024]{2,1,0:T(8,128)(2,1)}, u32[]{:S(2)}) copy-start(bf16[1,768,1024]{2,1,0:T(8,128)(2,1)} %param.8) | copy-start | bytes 4718596
Sparse Core Ops, SparseCore 0:
  10.3 50.3 all-gather.3
  81.8 150.1 all-reduce.5
  253.3 42.3 all-gather.7
  304.6 147.9 all-reduce.3
  454.2 39.1 all-gather.5
where the time goes:
time: 512 us; the launch traced here: 508 us
  waiting for transfers between devices  410 us (80%)
  matrix products  41.8 us (8%)
  local copies, waits for them, and re-layouts  29.9 us (6%)
  between operations  14.6 us (3%)
  other arithmetic  9.94 us (2%)
    unnamed x6, waiting for transfers between devices  148 us
    psum x1, waiting for transfers between devices, on_device(): summed = lax.psum(partial_kv, 'tp')  138 us
    all_gather x1, waiting for transfers between devices, on_device(): gathered_cot = lax.all_gather(cotangent, 'tp', axis=2, tiled=True)  51.5 us
    all_gather x1, waiting for transfers between devices, on_device(): lax.all_gather(serving, 'fsdp', axis=0, tiled=True)  42.5 us
    all_gather x1, waiting for transfers between devices, on_device(): lax.all_gather(old_weights, 'fsdp', axis=0, tiled=True)  16.1 us
    ppermute x1, waiting for transfers between devices, passed_along(): return lax.ppermute(block, axis, route)  13.7 us
    transpose x1, local copies, waits for them, and re-layouts, on_device(): jnp.einsum('tgn,tc->ngc', columns, rows_in, preferred_element_type=jnp.fl...  13.4 us
    unnamed x36, local copies, waits for them, and re-layouts  11.2 us
  transfers between devices with their start and end apart: 6, of which 6 were waited for; matrix products, arithmetic and copies ran while one was open for 7% of the time, Pallas kernels for 0%

commit v1 on v0

v1 whole, which is shorter than its diff:
```python
import math

import jax
import jax.numpy as jnp
from jax import lax
from jax.experimental import pallas as pl
from jax.experimental.pallas import tpu as pltpu
from jax.sharding import PartitionSpec as P

D = 8192
HD = 128
STEPS = 2
OPT_STEP = 100

first_decay = 0.9
second_decay = 0.95
learn_rate = 0.15
weight_decay = 0.1
small_term = 1e-08

N_TP = 8
N_FSDP = 16
SPAN = 16
MASKED = -1e30
OFFSETS = (0, -1, 1, -2, 2, -3, 3, 4)
SAME_CORE = [list(range(0, N_FSDP, 2)), list(range(1, N_FSDP, 2))]


def sibling(block, group):
    pairs = [(group * N_FSDP + f, group * N_FSDP + (f ^ 1)) for f in range(N_FSDP)]
    return lax.ppermute(block, ("group", "fsdp"), pairs)


def along_z(block, group, step):
    pairs = [(group * N_TP + z, group * N_TP + (z + step) % N_TP) for z in range(N_TP)]
    return lax.ppermute(block, ("group", "tp"), pairs)


def final_kernel(place, *refs):
    count = N_TP + 1
    hids, refs = refs[:count], refs[count:]
    w, w_other, queries, cache, reach_of = refs[:5]
    cots, refs = refs[5 : 5 + N_TP], refs[5 + N_TP :]
    cot_other, old, out = refs[:3]
    (
        hid_v, w_v, q_v, c_v, fresh_v, out_v, limit_v, cot_v, old_v,
        hid_sem, w_sem, q_sem, c_sem, out_sem, cot_sem, old_sem,
    ) = refs[3:]
    tokens, features = q_v.shape
    half = tokens // 2
    heads = features // HD
    per = 8

    @pl.when(place[0] == 0)
    def _():
        z, core = place[1], place[2]
        loads = [pltpu.make_async_copy(old, old_v, old_sem)]
        for r in range(N_TP):
            loads.append(
                pltpu.make_async_copy(
                    cots[r].at[:, pl.ds(0, tokens)], cot_v.at[r, pl.ds(0, HD)], cot_sem.at[r]
                )
            )
        loads.append(
            pltpu.make_async_copy(cot_other, cot_v.at[:, pl.ds(HD, HD)], cot_sem.at[N_TP])
        )
        for load in loads:
            load.start()
        for load in loads:
            load.wait()
        stores = []
        for first in range(0, tokens, 128):
            at = slice(first, first + 128)
            total = None
            for r, offset in enumerate(OFFSETS):
                plane = lax.rem(z + (offset + N_TP), N_TP)
                rows = jnp.concatenate(
                    [old_v[2 * plane + core], old_v[2 * plane + 1 - core]], axis=0
                )
                part = lax.dot_general(
                    cot_v[r, :, at],
                    rows,
                    (((0,), (0,)), ((), ())),
                    preferred_element_type=jnp.float32,
                )
                total = part if total is None else total + part
            out_v[at] = (total * (1.0 / math.sqrt(D))).astype(jnp.bfloat16)
            rows = pl.ds(first, 128)
            store = pltpu.make_async_copy(out_v.at[rows], out.at[rows], out_sem.at[first // 128])
            store.start()
            stores.append(store)
        for store in stores:
            store.wait()

    @pl.when(place[0] != 0)
    def _():
        z, core = place[1], place[2]
        loads = [
            pltpu.make_async_copy(v, w_v.at[i], w_sem.at[i]) for i, v in enumerate((w, w_other))
        ]
        for r in range(N_TP - 1):
            loads.append(pltpu.make_async_copy(hids[r], hid_v.at[r], hid_sem.at[r]))
        for i in range(2):
            r = N_TP - 1 + i
            rows = hid_v.at[N_TP - 1, pl.ds(i * half, half)]
            loads.append(pltpu.make_async_copy(hids[r], rows, hid_sem.at[r]))
        loads.append(pltpu.make_async_copy(queries, q_v, q_sem))
        loads.append(pltpu.make_async_copy(cache, c_v, c_sem))
        for load in loads:
            load.start()

        loads[0].wait()
        loads[1].wait()
        total = None
        for r, offset in enumerate(OFFSETS):
            loads[2 + r].wait()
            if r == N_TP - 1:
                loads[3 + r].wait()
            plane = lax.rem(z + (offset + N_TP), N_TP)
            rows = [w_v[i, q, plane] for i in range(2) for q in range(N_TP)]
            part = lax.dot_general(
                hid_v[r],
                jnp.concatenate(rows, axis=0),
                (((1,), (1,)), ((), ())),
                preferred_element_type=jnp.float32,
            )
            total = part if total is None else total + part
        total = total * (1.0 / math.sqrt(D))
        for i in range(2):
            own = total[:, i * 64 : (i + 1) * 64]
            other = total[:, HD + i * 64 : HD + (i + 1) * 64]
            fresh_v[i] = jnp.where(
                core == 0,
                jnp.concatenate([own, other], axis=1),
                jnp.concatenate([other, own], axis=1),
            ).astype(jnp.bfloat16)
        loads[-2].wait()
        loads[-1].wait()

        width = 128 + SPAN
        root = 1.0 / math.sqrt(HD)
        key_at = lax.broadcasted_iota(jnp.int32, (width, heads * SPAN), 0)
        token = lax.broadcasted_iota(jnp.int32, (width, heads * SPAN), 1) % SPAN
        new = key_at - 128
        owner = jnp.where(key_at < 128, key_at // 16, new // STEPS)
        limit = jnp.where(key_at < 128, key_at % 16, 0)
        limit = jnp.where(owner == token // STEPS, jnp.where(new <= token, limit, 99), 99)
        limit_v[...] = limit.astype(jnp.float32)

        stores = []
        for first in range(0, tokens // SPAN, per):
            ids = range(first, first + per)
            scores = []
            for i in ids:
                at = slice(i * SPAN, (i + 1) * SPAN)
                query = jnp.concatenate(
                    [q_v[at, h * HD : (h + 1) * HD] for h in range(heads)], axis=0
                )
                keys = c_v[i * 8 : (i + 1) * 8, 0].reshape(128, HD)
                keys = jnp.concatenate([keys, fresh_v[0, at]], axis=0)
                scores.append(
                    lax.dot_general(
                        keys, query, (((1,), (1,)), ((), ())), preferred_element_type=jnp.float32
                    )
                )
            probs = []
            for i, score in zip(ids, scores):
                seen = limit_v[...] < reach_of[i : i + 1, :]
                score = jnp.where(seen, score * root, MASKED)
                score = jnp.exp(score - jnp.max(score, axis=0, keepdims=True))
                inverse = 1.0 / jnp.sum(score, axis=0, keepdims=True)
                probs.append((score * inverse).astype(jnp.bfloat16))
            for i, prob in zip(ids, probs):
                at = slice(i * SPAN, (i + 1) * SPAN)
                values = c_v[i * 8 : (i + 1) * 8, 1].reshape(128, HD)
                values = jnp.concatenate([values, fresh_v[1, at]], axis=0)
                mixed = lax.dot_general(
                    prob, values, (((0,), (0,)), ((), ())), preferred_element_type=jnp.float32
                ).astype(jnp.bfloat16)
                for h in range(heads):
                    out_v[at, h * HD : (h + 1) * HD] = mixed[h * SPAN : (h + 1) * SPAN]
            rows = pl.ds(first * SPAN, per * SPAN)
            store = pltpu.make_async_copy(out_v.at[rows], out.at[rows], out_sem.at[first // per])
            store.start()
            stores.append(store)
        for store in stores:
            store.wait()


def final(place, hids, w, w_other, queries, cache, lengths, cots, cot_other, old):
    rows = cache.shape[0]
    tokens, features = queries.shape
    reach_of = jnp.repeat(lengths.astype(jnp.float32).reshape(rows // 8, 8), STEPS, axis=1)
    reach_of = jnp.tile(reach_of, (1, features // HD))
    anywhere = pl.BlockSpec(memory_space=pl.ANY)
    in_specs = [pl.BlockSpec(memory_space=pltpu.SMEM)] + [anywhere] * (len(hids) + 4)
    in_specs += [pl.BlockSpec(memory_space=pltpu.VMEM)] + [anywhere] * (len(cots) + 2)
    return pl.pallas_call(
        final_kernel,
        in_specs=in_specs,
        out_specs=anywhere,
        out_shape=jax.ShapeDtypeStruct((tokens, features), jnp.bfloat16),
        scratch_shapes=[
            pltpu.VMEM((N_TP, tokens, features), jnp.bfloat16),
            pltpu.VMEM((2,) + w.shape, jnp.bfloat16),
            pltpu.VMEM((tokens, features), jnp.bfloat16),
            pltpu.VMEM(cache.shape, jnp.bfloat16),
            pltpu.VMEM((2, tokens, HD), jnp.bfloat16),
            pltpu.VMEM((tokens, features), jnp.bfloat16),
            pltpu.VMEM((128 + SPAN, 128), jnp.float32),
            pltpu.VMEM((N_TP, 2 * HD, tokens), jnp.bfloat16),
            pltpu.VMEM(old.shape, jnp.bfloat16),
            pltpu.SemaphoreType.DMA((N_TP + 1,)),
            pltpu.SemaphoreType.DMA((2,)),
            pltpu.SemaphoreType.DMA,
            pltpu.SemaphoreType.DMA,
            pltpu.SemaphoreType.DMA((6,)),
            pltpu.SemaphoreType.DMA((N_TP + 1,)),
            pltpu.SemaphoreType.DMA,
        ],
        compiler_params=pltpu.CompilerParams(vmem_limit_bytes=40 * 1024 * 1024),
        cost_estimate=pl.CostEstimate(
            flops=2 * tokens * D * 2 * HD, bytes_accessed=24 * 2**20, transcendentals=0
        ),
    )(place, *hids, w, w_other, queries, cache, reach_of, *cots, cot_other, old)


def after(block, *others):
    return lax.optimization_barrier((block, *others))[0]


def on_device(hidden, cotangent, queries, kv_cache, lengths, master, moment1, moment2):
    half_index = lax.axis_index("group")
    z = lax.axis_index("tp")
    f = lax.axis_index("fsdp")
    core = f % 2
    rows_in = hidden[0]
    tokens, features = rows_in.shape
    half = tokens // 2
    scale = 1.0 / math.sqrt(D)

    def placed(buffer, block, index):
        return lax.dynamic_update_slice(buffer, block[None], (index % N_TP, 0, 0))

    cot = jnp.transpose(cotangent, (1, 2, 0))
    own = lax.dynamic_slice_in_dim(cot, core * 64, 64, 1)
    other = lax.dynamic_slice_in_dim(cot, (1 - core) * 64, 64, 1)
    cot = jnp.concatenate([own, sibling(other, 0)], axis=2).reshape(128, 2 * tokens)
    own_hidden = after(rows_in, cot[:1, :1])
    hid_chip = jnp.concatenate([rows_in, sibling(own_hidden, 0)], axis=0)

    def products(block):
        product = jnp.dot(block, hid_chip, preferred_element_type=jnp.float32)
        return product.astype(jnp.bfloat16)

    cots = [cot]
    up = down = cot
    hids = [rows_in]
    h_up = along_z(own_hidden, 1, 1)
    h_down = along_z(own_hidden, 1, -1)
    sums = [(products(cot), z)]
    for s in range(1, 4):
        up = along_z(up, 0, 1)
        down = along_z(down, 0, -1)
        if s > 1:
            up, down = after(up, sums[-1][0]), after(down, sums[-1][0])
        if s == 2:
            up, down, h_up, h_down = lax.optimization_barrier((up, down, h_up, h_down))
            hids += [h_up, h_down]
            h_up = along_z(h_up, 1, 1)
            h_down = along_z(h_down, 1, -1)
        cots += [up, down]
        pair = products(jnp.concatenate([up, down], axis=0))
        sums += [(pair[:128], z - s), (pair[128:], z + s)]
    up, down, _ = lax.optimization_barrier((up, down, sums[-1][0]))
    up, down = along_z(up[:64], 0, 1), along_z(down[64:], 0, -1)
    up, down, h_up, h_down = lax.optimization_barrier((up, down, h_up, h_down))
    hids += [h_up, h_down]
    h_up = along_z(h_up, 1, 1)
    h_down = along_z(h_down, 1, -1)
    last = jnp.concatenate([up, down], axis=0)
    cots.append(last)
    sums.append((products(last), z + 4))

    partial = jnp.zeros((N_TP, 128, features), jnp.bfloat16)
    for block, index in sums:
        partial = placed(partial, block, index)
    gathered = lax.all_to_all(partial, "fsdp", 0, 0, axis_index_groups=SAME_CORE)
    cot_other = jnp.stack([block[:, tokens:] for block in cots])
    gathered, cot_other = lax.optimization_barrier((gathered, cot_other))

    gradient = jnp.sum(gathered.astype(jnp.float32), axis=0) * scale
    gradient = jnp.transpose(gradient.reshape(2, 64, features), (1, 0, 2))

    def updated(gradient):
        new_first = first_decay * moment1 + (1.0 - first_decay) * gradient
        new_second = second_decay * moment2 + (1.0 - second_decay) * gradient * gradient
        first_hat = new_first / (1.0 - first_decay**OPT_STEP)
        second_hat = new_second / (1.0 - second_decay**OPT_STEP)
        new_master = master - learn_rate * (
            first_hat / (jnp.sqrt(second_hat) + small_term) + weight_decay * master
        )
        return new_master, new_first, new_second

    serving = jnp.transpose(updated(gradient)[0], (1, 0, 2)).astype(jnp.bfloat16)
    serving = serving.reshape(N_TP, 16, features)

    pieces = lax.all_to_all(serving, "fsdp", 0, 0, axis_index_groups=SAME_CORE)
    pieces = lax.all_to_all(pieces, "tp", 0, 0)
    h_up, h_down, pieces = lax.optimization_barrier((h_up, h_down, pieces))
    hids += [h_up, h_down]
    h_up = along_z(h_up[:half], 1, 1)
    h_down = along_z(h_down[half:], 1, -1)
    hids += [h_up, h_down]
    gradient_late = after(gradient, pieces)
    pieces = lax.ppermute(pieces, "group", [(0, 1)])
    mirrored = lax.ppermute(gradient_late, "group", [(0, 1)])
    cot_other = after(cot_other, pieces)
    w = lax.all_to_all(
        jnp.broadcast_to(pieces[None], (8,) + pieces.shape),
        "fsdp",
        0,
        0,
        axis_index_groups=SAME_CORE,
    )
    cot_other = sibling(cot_other, 0)

    gradient = jnp.where(half_index == 0, gradient, mirrored)
    new_master, new_first, new_second = updated(gradient)
    w, new_master, new_first, new_second, *last_hids = lax.optimization_barrier(
        (w, new_master, new_first, new_second, *hids[-2:])
    )
    hids[-2:] = last_hids
    w_other = lax.ppermute(w, "fsdp", [(i, i ^ 1) for i in range(N_FSDP)])

    old = jnp.transpose(master, (1, 0, 2)).astype(jnp.bfloat16).reshape(128, features)
    old = lax.all_gather(old, "fsdp", axis=0)
    place = jnp.stack([half_index, z, core]).astype(jnp.int32)
    block = final(place, hids, w, w_other, queries, kv_cache, lengths, cots, cot_other, old)
    return (block[None], new_master, new_first, new_second)


def solution(mesh):
    in_specs = (
        P("group", "fsdp", "tp"),
        P("fsdp", None, "tp"),
        P("fsdp", "tp"),
        P("fsdp", None, None, "tp"),
        P("fsdp"),
        P("fsdp", None, "tp"),
        P("fsdp", None, "tp"),
        P("fsdp", None, "tp"),
    )
    out_specs = (
        P("group", "fsdp", "tp"),
        P("fsdp", None, "tp"),
        P("fsdp", None, "tp"),
        P("fsdp", None, "tp"),
    )
    return jax.shard_map(
        on_device, mesh=mesh, in_specs=in_specs, out_specs=out_specs, check_vma=False
    )
```

time: 512 us -> 248 us (0.48)
  waiting for transfers between devices: 410 us -> 80.6 us
  starting transfers between devices: 1.67 us -> 60.4 us
  matrix products: 41.8 us -> 13.1 us
  Pallas kernels: 0 us -> 15.3 us
  blocking collectives: 0 us -> 9.35 us
  other arithmetic: 9.94 us -> 15.3 us
    unnamed x6 -> x1, waiting for transfers between devices: 148 us -> 0.02 us
    psum x1 -> x0, waiting for transfers between devices: 138 us -> none  [on_device(): summed = lax.psum(partial_kv, 'tp')]
    all_gather x3 -> x1, waiting for transfers between devices: 110 us -> 0.01 us  [on_device(): old = lax.all_gather(old, 'fsdp', axis=0)]
    ppermute x1 -> x22, waiting for transfers between devices: 13.7 us -> 64.1 us  [the longest x16 34.6 us: along_z(): return lax.ppermute(block, ('group', 'tp'), pairs)]
    ppermute x1 -> x22, starting transfers between devices: 1.28 us -> 44.8 us  [the longest x16 34.5 us: along_z(): return lax.ppermute(block, ('group', 'tp'), pairs)]
    dot_general x7 -> x5, matrix products: 41.8 us -> 13.1 us  [products(): product = jnp.dot(block, hid_chip, preferred_element_type=jnp.float32)]
    all_to_all x0 -> x3, waiting for transfers between devices: none -> 16.5 us  [the longest x1 11.3 us: on_device(): lax.all_to_all(partial, 'fsdp', 0, 0, axis_index_groups=SAME_CORE)]
    all_to_all x0 -> x3, starting transfers between devices: none -> 15.5 us  [the longest x1 5.2 us: on_device(): lax.all_to_all(partial, 'fsdp', 0, 0, axis_index_groups=SAME_CORE)]
  transfers between devices with their start and end apart: 6 -> 26, of which waited for: 6 -> 8; matrix products, arithmetic and copies ran while one was open for 7% -> 24% of each run, Pallas kernels for 0% -> 0%
where the time goes in v1:
time: 248 us; the launch traced here: 244 us
  waiting for transfers between devices  80.6 us (32%)
  starting transfers between devices  60.4 us (24%)
  local copies, waits for them, and re-layouts  35 us (14%)
  other arithmetic  15.3 us (6%)
  Pallas kernels  15.3 us (6%)
  between operations  14.6 us (6%)
  matrix products  13.1 us (5%)
  blocking collectives  9.35 us (4%)
    ppermute x16, waiting for transfers between devices, along_z(): return lax.ppermute(block, ('group', 'tp'), pairs)  34.6 us
    ppermute x16, starting transfers between devices, along_z(): return lax.ppermute(block, ('group', 'tp'), pairs)  34.5 us
    ppermute x1, waiting for transfers between devices, on_device(): mirrored = lax.ppermute(gradient_late, 'group', [(0, 1)])  22 us
    unnamed x33, local copies, waits for them, and re-layouts  18.3 us
    pallas_call x1, Pallas kernels, final(): pl.pallas_call(final_kernel, in_specs=in_specs, out_specs=anywhere, out_s...  15.3 us
    dot_general x5, matrix products, products(): product = jnp.dot(block, hid_chip, preferred_element_type=jnp.float32)  13.1 us
    all_to_all x1, waiting for transfers between devices, on_device(): lax.all_to_all(partial, 'fsdp', 0, 0, axis_index_groups=SAME_CORE)  11.3 us
    all_to_all x1, blocking collectives, on_device(): pieces = lax.all_to_all(serving, 'fsdp', 0, 0, axis_index_groups=SAME_CORE)  9.35 us
  transfers between devices with their start and end apart: 26, of which 8 were waited for; matrix products, arithmetic and copies ran while one was open for 24% of the time, Pallas kernels for 0%

profile of v1, /device:TPU:121, one launch (start us, length us, event | category | flops | bytes accessed | tf_op | source)
XLA Modules:
  0.0 243.7 jit_solution(3706012814129919096)
XLA Ops:
  7.2 1.8 collective-permute-start.4
  9.0 1.9 collective-permute-start.7
  11.0 4.8 %collective-permute-start.6 = (bf16[768,1024]{1,0:T(8,128)(2,1)}, bf16[768,1024]{1,0:T(8,128)(2,1)}, u32[]{:S(2)}, u32[]{:S(2)}) collective-permute-start(bf16[768,1024]{1,0:T(8,128)(2,1)} %bitcast.80), channel_id=1, source_target_pairs={{128,129},{129,130},{130,131},{131,132},{132,133},{133,134},{134,1... | collective-permute-start | bytes 4718600 | tf_op jit(solution)/shard_map/ppermute | solution.py:36
  15.7 2.0 dynamic-slice_bitcast_fusion.1
  18.5 7.7 %pad_maximum_fusion.1 = bf16[2,64,1536]{1,0,2:T(2,128)(2,1)} fusion(bf16[2,64,768]{1,0,2:T(2,128)(2,1)S(1)} %collective-permute-done, bf16[2,64,768]{1,0,2:T(2,128)(2,1)S(1)} %get-tuple-element.69), kind=kLoop, calls=%fused_computation.11 | loop fusion | flops 196608 | bytes 786432 | tf_op jit(solution)/shard_map/concatenate | solution.py:248
  26.2 2.2 copy.26
  28.4 1.4 collective-permute-start.3
  29.9 1.4 collective-permute-start.1
  31.3 1.4 collective-permute-start.5
  32.7 1.4 collective-permute-start.2
  36.3 2.6 %convolution_convert_fusion.2 = bf16[256,1024]{1,0:T(8,128)(2,1)S(1)} fusion(bf16[128,1536]{1,0:T(8,128)(2,1)} %collective-permute-done.3.refs_16_, bf16[128,1536]{1,0:T(8,128)(2,1)} %collective-permute-done.1.refs_15_, bf16[768,1024]{1,0:T(8,128)(2,1)} %collective-permute-done.4, bf16[768,1024]{1,0:T(8,128)(2,1)S(1)} %bitcast.81), kind=kOutput, calls=%fused_computation.4 | convolution fusion | flops 813432832 | bytes 4456448 | tf_op jit(solution)/shard_map/dot_general | solution.py:253
  39.0 9.0 %collective-permute-done.7.refs_2_ = bf16[768,1024]{1,0:T(8,128)(2,1)S(1)} collective-permute-done((bf16[768,1024]{1,0:T(8,128)(2,1)}, bf16[768,1024]{1,0:T(8,128)(2,1)S(1)}, u32[]{:S(2)}, u32[]{:S(2)}) %collective-permute-start.7) | collective-permute-done | bytes 1572896 | tf_op jit(solution)/shard_map/ppermute | solution.py:36
  50.7 2.6 %convolution_convert_fusion.1 = bf16[256,1024]{1,0:T(8,128)(2,1)S(1)} fusion(bf16[128,1536]{1,0:T(8,128)(2,1)} %collective-permute-done.5.refs_18_, bf16[128,1536]{1,0:T(8,128)(2,1)} %collective-permute-done.2.refs_17_, bf16[768,1024]{1,0:T(8,128)(2,1)} %collective-permute-done.4, bf16[768,1024]{1,0:T(8,128)(2,1)S(1)} %bitcast.82), kind=kOutput, calls=%fused_computation.3 | convolution fusion | flops 813432832 | bytes 4456448 | tf_op jit(solution)/shard_map/dot_general | solution.py:253
  53.3 5.1 %collective-permute-start.12 = (bf16[768,1024]{1,0:T(8,128)(2,1)}, bf16[768,1024]{1,0:T(8,128)(2,1)}, u32[]{:S(2)}, u32[]{:S(2)}) collective-permute-start(bf16[768,1024]{1,0:T(8,128)(2,1)} %collective-permute-done.6.refs_1_), channel_id=1, source_target_pairs={{128,129},{129,130},{130,131},{131,132},{132,133},{133,134},{134,1... | collective-permute-start | bytes 4718600 | tf_op jit(solution)/shard_map/ppermute | solution.py:36
  58.5 1.9 collective-permute-start.13
  60.4 1.7 broadcast_in_dim.39
  62.1 2.7 %fusion.1 = bf16[8,128,1024]{2,1,0:T(8,128)(2,1)} fusion(bf16[8,128,1024]{2,1,0:T(8,128)(2,1)} %broadcast_in_dim.39, s32[]{:T(128)S(6)} %select_n.81, bf16[128,1536]{1,0:T(8,128)(2,1)S(1)} %bitcast.75, bf16[768,1024]{1,0:T(8,128)(2,1)} %collective-permute-done.4, bf16[768,1024]{1,0:T(8,128)(2,1)S(1)} %bitcast.83), kind=kOutput, calls=%fused_computation.8 | convolution fusion | flops 409075712 | bytes 3801092 | tf_op jit(solution)/shard_map/dot_general | solution.py:253
  69.1 2.4 convolution_convert_fusion
  73.0 17.8 %collective-permute-done.12.refs_3_ = bf16[768,1024]{1,0:T(8,128)(2,1)} collective-permute-done((bf16[768,1024]{1,0:T(8,128)(2,1)}, bf16[768,1024]{1,0:T(8,128)(2,1)}, u32[]{:S(2)}, u32[]{:S(2)}) %collective-permute-start.12) | collective-permute-done | bytes 1572896 | tf_op jit(solution)/shard_map/ppermute | solution.py:36
  90.8 4.8 %collective-permute-done.13.refs_4_ = bf16[768,1024]{1,0:T(8,128)(2,1)} collective-permute-done((bf16[768,1024]{1,0:T(8,128)(2,1)S(1)}, bf16[768,1024]{1,0:T(8,128)(2,1)}, u32[]{:S(2)}, u32[]{:S(2)}) %collective-permute-start.13) | collective-permute-done | bytes 1572896 | tf_op jit(solution)/shard_map/ppermute | solution.py:36
  95.7 2.7 %fusion.3 = bf16[8,128,1024]{2,1,0:T(8,128)(2,1)} fusion(bf16[8,128,1024]{2,1,0:T(8,128)(2,1)} %bitcast_dynamic-update-slice_fusion, s32[]{:T(128)S(6)} %select_n.95, bf16[128,1536]{1,0:T(8,128)(2,1)S(1)} %constant_dynamic-update-slice_fusion.refs_21_, bf16[768,1024]{1,0:T(8,128)(2,1)} %collective-permute-done.4, bf16[768,1024]{1,0:T(8,128)(2,1)S(1)} %bitcast.85), kind=kOutput, calls=%fused_computation.10 | convolution fusion | flops 409075712 | bytes 3801092 | tf_op jit(solution)/shard_map/dot_general | solution.py:253
  98.4 5.2 %all-to-all-start = ((bf16[8,128,1024]{2,1,0:T(8,128)(2,1)}), bf16[8,128,1024]{2,1,0:T(8,128)(2,1)}, u32[]{:S(2)}, u32[]{:S(2)}) async-start(bf16[8,128,1024]{2,1,0:T(8,128)(2,1)} %fusion.3), calls=%async_computation | async-start | bytes 4194304 | tf_op jit(solution)/shard_map/all_to_all | solution.py:288
  104.3 1.6 fusion.25
  105.9 1.6 fusion.24
  107.5 1.6 bitcast_dynamic-update-slice_fusion.6
  109.1 1.6 bitcast_dynamic-update-slice_fusion.5
  112.1 1.9 collective-permute-start.14
  114.1 3.5 %collective-permute-start.15 = (bf16[768,1024]{1,0:T(8,128)(2,1)}, bf16[768,1024]{1,0:T(8,128)(2,1)}, u32[]{:S(2)}, u32[]{:S(2)}) collective-permute-start(bf16[768,1024]{1,0:T(8,128)(2,1)} %collective-permute-done.13.refs_4_), channel_id=1, source_target_pairs={{128,135},{129,128},{130,129},{131,130},{132,131},{133,132},{134,1... | collective-permute-start | bytes 4718600 | tf_op jit(solution)/shard_map/ppermute | solution.py:36
  118.3 11.3 %all-to-all-done = bf16[8,128,1024]{2,1,0:T(8,128)(2,1)} async-done(((bf16[8,128,1024]{2,1,0:T(8,128)(2,1)}), bf16[8,128,1024]{2,1,0:T(8,128)(2,1)}, u32[]{:S(2)}, u32[]{:S(2)}) %all-to-all-start) | async-done | bytes 2097184 | tf_op jit(solution)/shard_map/all_to_all | solution.py:288
  129.5 2.1 convert_reduce_fusion
  132.6 9.3 %all_to_all.20 = bf16[8,16,1024]{2,1,0:T(8,128)(2,1)} all-to-all(bf16[8,16,1024]{2,1,0:T(8,128)(2,1)S(1)} %bitcast.91), channel_id=1, replica_groups={{0,16,32,48,64,80,96,112},{8,24,40,56,72,88,104,120},{1,17,33,49,65,81,..., dimensions={0} | all-to-all | bytes 524288 | tf_op jit(solution)/shard_map/all_to_all | solution.py:308
  141.9 5.1 %all-to-all-start.2 = ((bf16[8,16,1024]{2,1,0:T(8,128)(2,1)}), bf16[8,16,1024]{2,1,0:T(8,128)(2,1)}, u32[]{:S(2)}, u32[]{:S(2)}) async-start(bf16[8,16,1024]{2,1,0:T(8,128)(2,1)} %all_to_all.20), calls=%async_computation.2 | async-start | bytes 524288 | tf_op jit(solution)/shard_map/all_to_all | solution.py:309
  147.1 2.9 %collective-permute-done.15.refs_6_ = bf16[768,1024]{1,0:T(8,128)(2,1)} collective-permute-done((bf16[768,1024]{1,0:T(8,128)(2,1)}, bf16[768,1024]{1,0:T(8,128)(2,1)}, u32[]{:S(2)}, u32[]{:S(2)}) %collective-permute-start.15) | collective-permute-done | bytes 1572896 | tf_op jit(solution)/shard_map/ppermute | solution.py:36
  149.9 5.2 %all-to-all-done.2 = bf16[8,16,1024]{2,1,0:T(8,128)(2,1)} async-done(((bf16[8,16,1024]{2,1,0:T(8,128)(2,1)}), bf16[8,16,1024]{2,1,0:T(8,128)(2,1)}, u32[]{:S(2)}, u32[]{:S(2)}) %all-to-all-start.2) | async-done | bytes 262176 | tf_op jit(solution)/shard_map/all_to_all | solution.py:309
  156.5 7.5 %collective-permute-done.16 = bf16[8,16,1024]{2,1,0:T(8,128)(2,1)S(1)} collective-permute-done((bf16[8,16,1024]{2,1,0:T(8,128)(2,1)}, bf16[8,16,1024]{2,1,0:T(8,128)(2,1)S(1)}, u32[]{:S(2)}, u32[]{:S(2)}) %collective-permute-start.16) | collective-permute-done | bytes 262176 | tf_op jit(solution)/shard_map/ppermute | solution.py:316
  164.0 1.7 broadcast_in_dim.48
  165.7 5.2 %all-to-all-start.3 = ((bf16[8,8,16,1024]{3,2,1,0:T(8,128)(2,1)}), bf16[8,8,16,1024]{3,2,1,0:T(8,128)(2,1)}, u32[]{:S(2)}, u32[]{:S(2)}) async-start(bf16[8,8,16,1024]{3,2,1,0:T(8,128)(2,1)} %broadcast_in_dim.48), calls=%async_computation.3 | async-start | bytes 4194304 | tf_op jit(solution)/shard_map/all_to_all | solution.py:319
  173.1 2.1 slice.72
  175.2 4.9 %collective-permute-start.19 = (bf16[384,1024]{1,0:T(8,128)(2,1)}, bf16[384,1024]{1,0:T(8,128)(2,1)}, u32[]{:S(2)}, u32[]{:S(2)}) collective-permute-start(bf16[384,1024]{1,0:T(8,128)(2,1)} %slice.72), channel_id=1, source_target_pairs={{128,135},{129,128},{130,129},{131,130},{132,131},{133,132},{134,1... | collective-permute-start | bytes 2359304 | tf_op jit(solution)/shard_map/ppermute | solution.py:36
  180.1 1.9 collective-permute-start.18
  182.0 22.0 %collective-permute-done.17 = f32[64,2,1024]{2,0,1:T(8,128)} collective-permute-done((f32[64,2,1024]{2,0,1:T(8,128)}, f32[64,2,1024]{2,0,1:T(8,128)}, u32[]{:S(2)}, u32[]{:S(2)}) %collective-permute-start.17) | collective-permute-done | bytes 524320 | tf_op jit(solution)/shard_map/ppermute | solution.py:317
  204.1 3.3 %multiply_subtract_fusion = (f32[64,2,1024]{2,0,1:T(8,128)}, f32[64,2,1024]{2,0,1:T(8,128)}, f32[64,2,1024]{2,0,1:T(8,128)}) fusion(f32[64,2,1024]{2,1,0:T(2,128)} %param.13, f32[64,2,1024]{2,0,1:T(8,128)} %bitcast.89, f32[64,2,1024]{2,0,1:T(8,128)} %collective-permute-done.17, pred[]{:T(512)S(6)} %eq.13, f32[64,2,1024]{2,1,0:T(2,128)} %param.14, ...), kind=kLoop, calls=%fused_computation.32 | loop fusion | flops 2097152 | bytes 4194305 | tf_op jit(solution)/shard_map/sub | solution.py:300
  207.4 3.4 %collective-permute-start.20 = (bf16[8,8,16,1024]{3,2,1,0:T(8,128)(2,1)}, bf16[8,8,16,1024]{3,2,1,0:T(8,128)(2,1)}, u32[]{:S(2)}, u32[]{:S(2)}) collective-permute-start(bf16[8,8,16,1024]{3,2,1,0:T(8,128)(2,1)} %all-to-all-done.3.refs_9_), channel_id=1, source_target_pairs={{0,8},{8,0},{16,24},{24,16},{32,40},{40,32},{48,56},{56,48},{64,72... | collective-permute-start | bytes 6291464 | tf_op jit(solution)/shard_map/ppermute | solution.py:334
  210.8 1.8 collective-permute-start.21
  212.9 2.3 copy.35
  215.2 2.2 copy.36
  220.1 1.4 copy-done.4
  221.5 15.3 %shard_map.111 = bf16[768,1024]{1,0:T(8,128)(2,1)} custom-call(s32[3]{0:T(128)S(1)} %pad_add_fusion.place, bf16[768,1024]{1,0:T(8,128)(2,1)S(1)} %bitcast.86, bf16[768,1024]{1,0:T(8,128)(2,1)} %collective-permute-done.6.refs_1_, bf16[768,1024]{1,0:T(8,128)(2,1)S(1)} %copy-done.4, bf16[768,1024]{1,0:T(8,128)(2,1)} %collective-permute-done.12.refs_3_, ...), custom_call_target="tpu_custom_call" | custom-call | flops 3221225472 | bytes 25165824 | tf_op jit(solution)/shard_map/pallas_call | solution.py:198
  (75 shorter events, 21.3 us)
Async XLA Ops:
  7.2 211.5 %all-gather.2.cloned.1.call-start = ((), (), s32[]{:S(2)}) async-start(), calls=%async_computation.4 | async-start | bytes 4456448 | tf_op jit(solution)/shard_map/all_gather | solution.py:337
  7.2 29.1 %collective-permute-start.4 = (bf16[768,1024]{1,0:T(8,128)(2,1)}, bf16[768,1024]{1,0:T(8,128)(2,1)}, u32[]{:S(2)}, u32[]{:S(2)}) collective-permute-start(bf16[768,1024]{1,0:T(8,128)(2,1)} %bitcast.78), channel_id=1, source_target_pairs={{0,8},{8,0},{16,24},{24,16},{32,40},{40,32},{48,56},{56,48},{64,72... | collective-permute-start | bytes 4718600 | tf_op jit(solution)/shard_map/ppermute | solution.py:31
  9.0 39.0 %collective-permute-start.7 = (bf16[768,1024]{1,0:T(8,128)(2,1)}, bf16[768,1024]{1,0:T(8,128)(2,1)S(1)}, u32[]{:S(2)}, u32[]{:S(2)}) collective-permute-start(bf16[768,1024]{1,0:T(8,128)(2,1)} %bitcast.79), channel_id=1, source_target_pairs={{128,135},{129,128},{130,129},{131,130},{132,131},{133,132},{134,1... | collective-permute-start | bytes 4718600 | tf_op jit(solution)/shard_map/ppermute | solution.py:36
  11.0 38.2 %collective-permute-start.6 = (bf16[768,1024]{1,0:T(8,128)(2,1)}, bf16[768,1024]{1,0:T(8,128)(2,1)}, u32[]{:S(2)}, u32[]{:S(2)}) collective-permute-start(bf16[768,1024]{1,0:T(8,128)(2,1)} %bitcast.80), channel_id=1, source_target_pairs={{128,129},{129,130},{130,131},{131,132},{132,133},{133,134},{134,1... | collective-permute-start | bytes 4718600 | tf_op jit(solution)/shard_map/ppermute | solution.py:36
  17.8 0.7 collective-permute-start
  18.5 17.8 %copy-start = (bf16[1,768,1024]{2,1,0:T(8,128)(2,1)S(1)}, bf16[1,768,1024]{2,1,0:T(8,128)(2,1)}, u32[]{:S(2)}) copy-start(bf16[1,768,1024]{2,1,0:T(8,128)(2,1)} %param.8) | copy-start | bytes 4718596
  28.4 2.9 %collective-permute-start.3 = (bf16[128,1536]{1,0:T(8,128)(2,1)S(1)}, bf16[128,1536]{1,0:T(8,128)(2,1)}, u32[]{:S(2)}, u32[]{:S(2)}) collective-permute-start(bf16[128,1536]{1,0:T(8,128)(2,1)S(1)} %bitcast.73), channel_id=1, source_target_pairs={{0,7},{1,0},{2,1},{3,2},{4,3},{5,4},{6,5},{7,6},{8,15},{9,8},{10,9... | collective-permute-start | bytes 1179656 | tf_op jit(solution)/shard_map/ppermute | solution.py:36
  29.9 2.8 %collective-permute-start.1 = (bf16[128,1536]{1,0:T(8,128)(2,1)S(1)}, bf16[128,1536]{1,0:T(8,128)(2,1)}, u32[]{:S(2)}, u32[]{:S(2)}) collective-permute-start(bf16[128,1536]{1,0:T(8,128)(2,1)S(1)} %bitcast.74), channel_id=1, source_target_pairs={{0,1},{1,2},{2,3},{3,4},{4,5},{5,6},{6,7},{7,0},{8,9},{9,10},{10,1... | collective-permute-start | bytes 1179656 | tf_op jit(solution)/shard_map/ppermute | solution.py:36
  31.3 7.6 %collective-permute-start.5 = (bf16[128,1536]{1,0:T(8,128)(2,1)}, bf16[128,1536]{1,0:T(8,128)(2,1)}, u32[]{:S(2)}, u32[]{:S(2)}) collective-permute-start(bf16[128,1536]{1,0:T(8,128)(2,1)} %collective-permute-done.3.refs_16_), channel_id=1, source_target_pairs={{0,7},{1,0},{2,1},{3,2},{4,3},{5,4},{6,5},{7,6},{8,15},{9,8},{10,9... | collective-permute-start | bytes 1179656 | tf_op jit(solution)/shard_map/ppermute | solution.py:36
  32.7 6.2 %collective-permute-start.2 = (bf16[128,1536]{1,0:T(8,128)(2,1)}, bf16[128,1536]{1,0:T(8,128)(2,1)}, u32[]{:S(2)}, u32[]{:S(2)}) collective-permute-start(bf16[128,1536]{1,0:T(8,128)(2,1)} %collective-permute-done.1.refs_15_), channel_id=1, source_target_pairs={{0,1},{1,2},{2,3},{3,4},{4,5},{5,6},{6,7},{7,0},{8,9},{9,10},{10,1... | collective-permute-start | bytes 1179656 | tf_op jit(solution)/shard_map/ppermute | solution.py:36
  48.0 1.1 copy-start.2
  49.1 9.3 %copy-start.3 = (bf16[768,1024]{1,0:T(8,128)(2,1)S(1)}, bf16[768,1024]{1,0:T(8,128)(2,1)}, u32[]{:S(2)}) copy-start(bf16[768,1024]{1,0:T(8,128)(2,1)} %copy-done.2) | copy-start | bytes 4718596
  49.1 18.5 %collective-permute-start.8 = (bf16[128,1536]{1,0:T(8,128)(2,1)}, bf16[128,1536]{1,0:T(8,128)(2,1)S(1)}, u32[]{:S(2)}, u32[]{:S(2)}) collective-permute-start(bf16[128,1536]{1,0:T(8,128)(2,1)} %collective-permute-done.2.refs_17_), channel_id=1, source_target_pairs={{0,1},{1,2},{2,3},{3,4},{4,5},{5,6},{6,7},{7,0},{8,9},{9,10},{10,1... | collective-permute-start | bytes 1179656 | tf_op jit(solution)/shard_map/ppermute | solution.py:36
  50.0 17.7 %collective-permute-start.9 = (bf16[128,1536]{1,0:T(8,128)(2,1)}, bf16[128,1536]{1,0:T(8,128)(2,1)S(1)}, u32[]{:S(2)}, u32[]{:S(2)}) collective-permute-start(bf16[128,1536]{1,0:T(8,128)(2,1)} %collective-permute-done.5.refs_18_), channel_id=1, source_target_pairs={{0,7},{1,0},{2,1},{3,2},{4,3},{5,4},{6,5},{7,6},{8,15},{9,8},{10,9... | collective-permute-start | bytes 1179656 | tf_op jit(solution)/shard_map/ppermute | solution.py:36
  53.3 37.5 %collective-permute-start.12 = (bf16[768,1024]{1,0:T(8,128)(2,1)}, bf16[768,1024]{1,0:T(8,128)(2,1)}, u32[]{:S(2)}, u32[]{:S(2)}) collective-permute-start(bf16[768,1024]{1,0:T(8,128)(2,1)} %collective-permute-done.6.refs_1_), channel_id=1, source_target_pairs={{128,129},{129,130},{130,131},{131,132},{132,133},{133,134},{134,1... | collective-permute-start | bytes 4718600 | tf_op jit(solution)/shard_map/ppermute | solution.py:36
  58.5 37.2 %collective-permute-start.13 = (bf16[768,1024]{1,0:T(8,128)(2,1)S(1)}, bf16[768,1024]{1,0:T(8,128)(2,1)}, u32[]{:S(2)}, u32[]{:S(2)}) collective-permute-start(bf16[768,1024]{1,0:T(8,128)(2,1)S(1)} %copy-done.3), channel_id=1, source_target_pairs={{128,135},{129,128},{130,129},{131,130},{132,131},{133,132},{134,1... | collective-permute-start | bytes 4718600 | tf_op jit(solution)/shard_map/ppermute | solution.py:36
  67.7 5.3 %collective-permute-start.11 = (bf16[64,1536]{1,0:T(8,128)(2,1)S(1)}, bf16[64,1536]{1,0:T(8,128)(2,1)S(1)}, u32[]{:S(2)}, u32[]{:S(2)}) collective-permute-start(bf16[64,1536]{1,0:T(8,128)(2,1)S(1)} %slice.59), channel_id=1, source_target_pairs={{0,7},{1,0},{2,1},{3,2},{4,3},{5,4},{6,5},{7,6},{8,15},{9,8},{10,9... | collective-permute-start | bytes 589832 | tf_op jit(solution)/shard_map/ppermute | solution.py:36
  68.4 4.6 %collective-permute-start.10 = (bf16[64,1536]{1,0:T(8,128)(2,1)S(1)}, bf16[64,1536]{1,0:T(8,128)(2,1)S(1)}, u32[]{:S(2)}, u32[]{:S(2)}) collective-permute-start(bf16[64,1536]{1,0:T(8,128)(2,1)S(1)} %slice.58), channel_id=1, source_target_pairs={{0,1},{1,2},{2,3},{3,4},{4,5},{5,6},{6,7},{7,0},{8,9},{9,10},{10,1... | collective-permute-start | bytes 589832 | tf_op jit(solution)/shard_map/ppermute | solution.py:36
  98.4 31.2 %all-to-all-start = ((bf16[8,128,1024]{2,1,0:T(8,128)(2,1)}), bf16[8,128,1024]{2,1,0:T(8,128)(2,1)}, u32[]{:S(2)}, u32[]{:S(2)}) async-start(bf16[8,128,1024]{2,1,0:T(8,128)(2,1)} %fusion.3), calls=%async_computation | async-start | bytes 4194304 | tf_op jit(solution)/shard_map/all_to_all | solution.py:288
  112.1 34.9 %collective-permute-start.14 = (bf16[768,1024]{1,0:T(8,128)(2,1)}, bf16[768,1024]{1,0:T(8,128)(2,1)S(1)}, u32[]{:S(2)}, u32[]{:S(2)}) collective-permute-start(bf16[768,1024]{1,0:T(8,128)(2,1)} %collective-permute-done.12.refs_3_), channel_id=1, source_target_pairs={{128,129},{129,130},{130,131},{131,132},{132,133},{133,134},{134,1... | collective-permute-start | bytes 4718600 | tf_op jit(solution)/shard_map/ppermute | solution.py:36
  114.1 35.9 %collective-permute-start.15 = (bf16[768,1024]{1,0:T(8,128)(2,1)}, bf16[768,1024]{1,0:T(8,128)(2,1)}, u32[]{:S(2)}, u32[]{:S(2)}) collective-permute-start(bf16[768,1024]{1,0:T(8,128)(2,1)} %collective-permute-done.13.refs_4_), channel_id=1, source_target_pairs={{128,135},{129,128},{130,129},{131,130},{132,131},{133,132},{134,1... | collective-permute-start | bytes 4718600 | tf_op jit(solution)/shard_map/ppermute | solution.py:36
  129.5 2.2 copy-start.5
  129.5 2.2 copy-start.8
  129.5 2.2 copy-start.9
  131.7 0.8 copy-start.6
  141.9 13.3 %all-to-all-start.2 = ((bf16[8,16,1024]{2,1,0:T(8,128)(2,1)}), bf16[8,16,1024]{2,1,0:T(8,128)(2,1)}, u32[]{:S(2)}, u32[]{:S(2)}) async-start(bf16[8,16,1024]{2,1,0:T(8,128)(2,1)} %all_to_all.20), calls=%async_computation.2 | async-start | bytes 524288 | tf_op jit(solution)/shard_map/all_to_all | solution.py:309
  155.2 8.8 %collective-permute-start.16 = (bf16[8,16,1024]{2,1,0:T(8,128)(2,1)}, bf16[8,16,1024]{2,1,0:T(8,128)(2,1)S(1)}, u32[]{:S(2)}, u32[]{:S(2)}) collective-permute-start(bf16[8,16,1024]{2,1,0:T(8,128)(2,1)} %all-to-all-done.2), channel_id=1, source_target_pairs={{0,128},{1,129},{2,130},{3,131},{4,132},{5,133},{6,134},{7,135},{8... | collective-permute-start | bytes 786440 | tf_op jit(solution)/shard_map/ppermute | solution.py:316
  165.7 41.7 %all-to-all-start.3 = ((bf16[8,8,16,1024]{3,2,1,0:T(8,128)(2,1)}), bf16[8,8,16,1024]{3,2,1,0:T(8,128)(2,1)}, u32[]{:S(2)}, u32[]{:S(2)}) async-start(bf16[8,8,16,1024]{3,2,1,0:T(8,128)(2,1)} %broadcast_in_dim.48), calls=%async_computation.3 | async-start | bytes 4194304 | tf_op jit(solution)/shard_map/all_to_all | solution.py:319
  170.9 33.2 %collective-permute-start.17 = (f32[64,2,1024]{2,0,1:T(8,128)}, f32[64,2,1024]{2,0,1:T(8,128)}, u32[]{:S(2)}, u32[]{:S(2)}) collective-permute-start(f32[64,2,1024]{2,0,1:T(8,128)} %bitcast.88), channel_id=1, source_target_pairs={{0,128},{1,129},{2,130},{3,131},{4,132},{5,133},{6,134},{7,135},{8... | collective-permute-start | bytes 1572872 | tf_op jit(solution)/shard_map/ppermute | solution.py:317
  175.2 32.2 %collective-permute-start.19 = (bf16[384,1024]{1,0:T(8,128)(2,1)}, bf16[384,1024]{1,0:T(8,128)(2,1)}, u32[]{:S(2)}, u32[]{:S(2)}) collective-permute-start(bf16[384,1024]{1,0:T(8,128)(2,1)} %slice.72), channel_id=1, source_target_pairs={{128,135},{129,128},{130,129},{131,130},{132,131},{133,132},{134,1... | collective-permute-start | bytes 2359304 | tf_op jit(solution)/shard_map/ppermute | solution.py:36
  180.1 27.3 %collective-permute-start.18 = (bf16[384,1024]{1,0:T(8,128)(2,1)}, bf16[384,1024]{1,0:T(8,128)(2,1)}, u32[]{:S(2)}, u32[]{:S(2)}) collective-permute-start(bf16[384,1024]{1,0:T(8,128)(2,1)} %slice.71), channel_id=1, source_target_pairs={{128,129},{129,130},{130,131},{131,132},{132,133},{133,134},{134,1... | collective-permute-start | bytes 2359304 | tf_op jit(solution)/shard_map/ppermute | solution.py:36
  182.0 30.6 %copy-start.10 = (s32[384]{0:T(512)S(1)}, s32[384]{0:T(512)}, u32[]{:S(2)}) copy-start(s32[384]{0:T(512)} %param.12) | copy-start | bytes 4612
  207.4 11.3 %collective-permute-start.20 = (bf16[8,8,16,1024]{3,2,1,0:T(8,128)(2,1)}, bf16[8,8,16,1024]{3,2,1,0:T(8,128)(2,1)}, u32[]{:S(2)}, u32[]{:S(2)}) collective-permute-start(bf16[8,8,16,1024]{3,2,1,0:T(8,128)(2,1)} %all-to-all-done.3.refs_9_), channel_id=1, source_target_pairs={{0,8},{8,0},{16,24},{24,16},{32,40},{40,32},{48,56},{56,48},{64,72... | collective-permute-start | bytes 6291464 | tf_op jit(solution)/shard_map/ppermute | solution.py:334
  210.8 7.9 %collective-permute-start.21 = (bf16[8,128,768]{2,1,0:T(8,128)(2,1)}, bf16[8,128,768]{2,1,0:T(8,128)(2,1)}, u32[]{:S(2)}, u32[]{:S(2)}) collective-permute-start(bf16[8,128,768]{2,1,0:T(8,128)(2,1)} %fusion.23), channel_id=1, source_target_pairs={{0,8},{8,0},{16,24},{24,16},{32,40},{40,32},{48,56},{56,48},{64,72... | collective-permute-start | bytes 4718600 | tf_op jit(solution)/shard_map/ppermute | solution.py:31
  212.8 4.6 %copy-start.7 = (f32[64,2,1024]{2,0,1:T(8,128)S(1)}, f32[64,2,1024]{2,0,1:T(8,128)}, u32[]{:S(2)}) copy-start(f32[64,2,1024]{2,0,1:T(8,128)} %get-tuple-element.65) | copy-start | bytes 1572868
  218.7 1.4 copy-start.1
  220.1 1.4 copy-start.4
Sparse Core Ops, SparseCore 0:
  36.3 53.5 all-gather.1

commit v2 on v1

--- a/solution.py
+++ b/solution.py
@@ -1,3 +1,4 @@
+import functools
 import math
 
 import jax
@@ -23,6 +24,10 @@
 SPAN = 16
 MASKED = -1e30
 OFFSETS = (0, -1, 1, -2, 2, -3, 3, 4)
+HID_PARTS = (
+    (0, None), (1, None), (2, None), (3, None), (4, None),
+    (5, None), (6, None), (7, 0), (7, 1),
+)
 SAME_CORE = [list(range(0, N_FSDP, 2)), list(range(1, N_FSDP, 2))]
 
 
@@ -38,9 +43,9 @@
 
 def final_kernel(place, *refs):
     count = N_TP + 1
-    hids, refs = refs[:count], refs[count:]
+    hids, refs = refs[: len(HID_PARTS)], refs[len(HID_PARTS) :]
     w, w_other, queries, cache, reach_of = refs[:5]
-    cots, refs = refs[5 : 5 + N_TP], refs[5 + N_TP :]
+    cots, refs = refs[5 : 5 + count], refs[5 + count :]
     cot_other, old, out = refs[:3]
     (
         hid_v, w_v, q_v, c_v, fresh_v, out_v, limit_v, cot_v, old_v,
@@ -55,14 +60,16 @@
     def _():
         z, core = place[1], place[2]
         loads = [pltpu.make_async_copy(old, old_v, old_sem)]
-        for r in range(N_TP):
+        for i in range(count):
+            if i < N_TP - 1:
+                rows = cot_v.at[i, pl.ds(0, HD)]
+            else:
+                rows = cot_v.at[N_TP - 1, pl.ds((i - N_TP + 1) * 64, 64)]
             loads.append(
-                pltpu.make_async_copy(
-                    cots[r].at[:, pl.ds(0, tokens)], cot_v.at[r, pl.ds(0, HD)], cot_sem.at[r]
-                )
+                pltpu.make_async_copy(cots[i].at[:, pl.ds(0, tokens)], rows, cot_sem.at[i])
             )
         loads.append(
-            pltpu.make_async_copy(cot_other, cot_v.at[:, pl.ds(HD, HD)], cot_sem.at[N_TP])
+            pltpu.make_async_copy(cot_other, cot_v.at[:, pl.ds(HD, HD)], cot_sem.at[count])
         )
         for load in loads:
             load.start()
@@ -98,26 +105,30 @@
         loads = [
             pltpu.make_async_copy(v, w_v.at[i], w_sem.at[i]) for i, v in enumerate((w, w_other))
         ]
-        for r in range(N_TP - 1):
-            loads.append(pltpu.make_async_copy(hids[r], hid_v.at[r], hid_sem.at[r]))
-        for i in range(2):
-            r = N_TP - 1 + i
-            rows = hid_v.at[N_TP - 1, pl.ds(i * half, half)]
-            loads.append(pltpu.make_async_copy(hids[r], rows, hid_sem.at[r]))
+        for i, (r, part) in enumerate(HID_PARTS):
+            to = hid_v.at[r] if part is None else hid_v.at[r, pl.ds(part * half, half)]
+            loads.append(pltpu.make_async_copy(hids[i], to, hid_sem.at[i]))
         loads.append(pltpu.make_async_copy(queries, q_v, q_sem))
         loads.append(pltpu.make_async_copy(cache, c_v, c_sem))
-        for load in loads:
+        started = 5
+        for load in loads[:started]:
             load.start()
 
-        loads[0].wait()
-        loads[1].wait()
         total = None
+        arrived = -1
         for r, offset in enumerate(OFFSETS):
-            loads[2 + r].wait()
-            if r == N_TP - 1:
-                loads[3 + r].wait()
+            needed = 1 + max(i for i, v in enumerate(HID_PARTS, 1) if v[0] == r)
+            while arrived < needed:
+                arrived += 1
+                loads[arrived].wait()
+                if started < len(loads):
+                    loads[started].start()
+                    started += 1
             plane = lax.rem(z + (offset + N_TP), N_TP)
-            rows = [w_v[i, q, plane] for i in range(2) for q in range(N_TP)]
+            flipped = lax.rem(plane + 4, N_TP)
+            rows = [
+                v for i in range(2) for v in (w_v[i, plane, :64], w_v[i, flipped, 64:])
+            ]
             part = lax.dot_general(
                 hid_v[r],
                 jnp.concatenate(rows, axis=0),
@@ -187,11 +198,8 @@
             store.wait()
 
 
-def final(place, hids, w, w_other, queries, cache, lengths, cots, cot_other, old):
-    rows = cache.shape[0]
+def final(place, hids, w, w_other, queries, cache, reach_of, cots, cot_other, old):
     tokens, features = queries.shape
-    reach_of = jnp.repeat(lengths.astype(jnp.float32).reshape(rows // 8, 8), STEPS, axis=1)
-    reach_of = jnp.tile(reach_of, (1, features // HD))
     anywhere = pl.BlockSpec(memory_space=pl.ANY)
     in_specs = [pl.BlockSpec(memory_space=pltpu.SMEM)] + [anywhere] * (len(hids) + 4)
     in_specs += [pl.BlockSpec(memory_space=pltpu.VMEM)] + [anywhere] * (len(cots) + 2)
@@ -210,19 +218,150 @@
             pltpu.VMEM((128 + SPAN, 128), jnp.float32),
             pltpu.VMEM((N_TP, 2 * HD, tokens), jnp.bfloat16),
             pltpu.VMEM(old.shape, jnp.bfloat16),
-            pltpu.SemaphoreType.DMA((N_TP + 1,)),
+            pltpu.SemaphoreType.DMA((len(HID_PARTS),)),
             pltpu.SemaphoreType.DMA((2,)),
             pltpu.SemaphoreType.DMA,
             pltpu.SemaphoreType.DMA,
             pltpu.SemaphoreType.DMA((6,)),
-            pltpu.SemaphoreType.DMA((N_TP + 1,)),
+            pltpu.SemaphoreType.DMA((N_TP + 2,)),
             pltpu.SemaphoreType.DMA,
         ],
-        compiler_params=pltpu.CompilerParams(vmem_limit_bytes=40 * 1024 * 1024),
+        compiler_params=pltpu.CompilerParams(vmem_limit_bytes=56 * 1024 * 1024),
         cost_estimate=pl.CostEstimate(
             flops=2 * tokens * D * 2 * HD, bytes_accessed=24 * 2**20, transcendentals=0
         ),
     )(place, *hids, w, w_other, queries, cache, reach_of, *cots, cot_other, old)
+
+
+def split_kernel(place, cot, own, other, turned):
+    @pl.when(place[0] == 0)
+    def _():
+        core = place[2]
+        for g in range(2):
+            turned[...] = cot[:, g * HD : (g + 1) * HD].T
+            rows = slice(g * 64, (g + 1) * 64)
+            own[rows] = turned[pl.ds(pl.multiple_of(core * 64, 64), 64)]
+            other[rows] = turned[pl.ds(pl.multiple_of((1 - core) * 64, 64), 64)]
+
+
+def split(place, cot):
+    turned = jax.ShapeDtypeStruct((HD, cot.shape[0]), cot.dtype)
+    return pl.pallas_call(
+        split_kernel,
+        in_specs=[
+            pl.BlockSpec(memory_space=pltpu.SMEM),
+            pl.BlockSpec(memory_space=pltpu.VMEM),
+        ],
+        out_specs=[pl.BlockSpec(memory_space=pltpu.VMEM)] * 2,
+        out_shape=[turned, turned],
+        scratch_shapes=[pltpu.VMEM(turned.shape, turned.dtype)],
+        compiler_params=pltpu.CompilerParams(vmem_limit_bytes=8 * 1024 * 1024),
+    )(place, cot)
+
+
+def product_kernel(place, *refs, ids, halves, first):
+    count = len(ids)
+    blocks, refs = refs[: count * halves], refs[count * halves :]
+    hid_own, hid_other = refs[:2]
+    refs = refs[2:] if first else refs[4:]
+    partial, cot_other, block_v, hid_v, out_v, block_sem, hid_sem, out_sem, cot_sem = refs
+    tokens, features = hid_own.shape
+    rows = HD // halves
+
+    @pl.when(place[0] == 0)
+    def _():
+        z = place[1]
+        loads = [
+            pltpu.make_async_copy(v, hid_v.at[pl.ds(i * tokens, tokens)], hid_sem.at[i])
+            for i, v in enumerate((hid_own, hid_other))
+        ]
+        stores = []
+        for i, block in enumerate(blocks):
+            at = pl.ds(i * rows, rows)
+            loads.append(pltpu.make_async_copy(block, block_v.at[at], block_sem.at[i]))
+            part = cot_other.at[ids[i // halves], pl.ds(i % halves * rows, rows)]
+            stores.append(
+                pltpu.make_async_copy(block.at[:, pl.ds(tokens, tokens)], part, cot_sem.at[i])
+            )
+        for copy in loads + stores:
+            copy.start()
+        for load in loads:
+            load.wait()
+        for n in range(0, features, 256):
+            part = jnp.dot(
+                block_v[...], hid_v[:, n : n + 256], preferred_element_type=jnp.float32
+            )
+            out_v[:, n : n + 256] = part.astype(jnp.bfloat16)
+        for i, r in enumerate(ids):
+            plane = lax.rem(z + (OFFSETS[r] + N_TP), N_TP)
+            store = pltpu.make_async_copy(
+                out_v.at[pl.ds(i * HD, HD)], partial.at[plane], out_sem.at[i]
+            )
+            store.start()
+            stores.append(store)
+        for store in stores:
+            store.wait()
+
+
+def product(place, ids, blocks, hid_own, hid_other, before=()):
+    first = not before
+    tokens, features = hid_own.shape
+    operands = (place, *blocks, hid_own, hid_other, *before)
+    rows = len(ids) * HD
+    return pl.pallas_call(
+        functools.partial(
+            product_kernel, ids=ids, halves=len(blocks) // len(ids), first=first
+        ),
+        in_specs=[pl.BlockSpec(memory_space=pltpu.SMEM)]
+        + [pl.BlockSpec(memory_space=pl.ANY)] * (len(operands) - 1),
+        out_specs=[pl.BlockSpec(memory_space=pl.ANY)] * 2,
+        out_shape=[
+            jax.ShapeDtypeStruct((N_TP, HD, features), jnp.bfloat16),
+            jax.ShapeDtypeStruct((N_TP, HD, tokens), jnp.bfloat16),
+        ],
+        input_output_aliases={} if first else {len(operands) - 2: 0, len(operands) - 1: 1},
+        scratch_shapes=[
+            pltpu.VMEM((rows, 2 * tokens), jnp.bfloat16),
+            pltpu.VMEM((2 * tokens, features), jnp.bfloat16),
+            pltpu.VMEM((rows, features), jnp.bfloat16),
+            pltpu.SemaphoreType.DMA((len(blocks),)),
+            pltpu.SemaphoreType.DMA((2,)),
+            pltpu.SemaphoreType.DMA((len(ids),)),
+            pltpu.SemaphoreType.DMA((len(blocks),)),
+        ],
+        compiler_params=pltpu.CompilerParams(vmem_limit_bytes=16 * 1024 * 1024),
+        cost_estimate=pl.CostEstimate(
+            flops=4 * rows * tokens * features, bytes_accessed=12 * 2**20, transcendentals=0
+        ),
+    )(*operands)
+
+
+def adam(gradient, master, moment1, moment2):
+    new_first = first_decay * moment1 + (1.0 - first_decay) * gradient
+    new_second = second_decay * moment2 + (1.0 - second_decay) * gradient * gradient
+    first_hat = new_first / (1.0 - first_decay**OPT_STEP)
+    second_hat = new_second / (1.0 - second_decay**OPT_STEP)
+    new_master = master - learn_rate * (
+        first_hat / (jnp.sqrt(second_hat) + small_term) + weight_decay * master
+    )
+    return new_master, new_first, new_second
+
+
+def adam_kernel(place, gradient, mirrored, master, moment1, moment2, *outs):
+    chosen = jnp.where(place[0] == 0, gradient[...], mirrored[...])
+    for out, value in zip(outs, adam(chosen, master[...], moment1[...], moment2[...])):
+        out[...] = value
+
+
+def adam_outputs(place, *arrays):
+    return pl.pallas_call(
+        adam_kernel,
+        in_specs=[pl.BlockSpec(memory_space=pltpu.SMEM)]
+        + [pl.BlockSpec(memory_space=pltpu.VMEM)] * 5,
+        out_specs=[pl.BlockSpec(memory_space=pltpu.VMEM)] * 3,
+        out_shape=[jax.ShapeDtypeStruct(arrays[0].shape, jnp.float32)] * 3,
+        compiler_params=pltpu.CompilerParams(vmem_limit_bytes=16 * 1024 * 1024),
+    )(place, *arrays)
 
 
 def after(block, *others):
@@ -239,83 +378,59 @@
     half = tokens // 2
     scale = 1.0 / math.sqrt(D)
 
-    def placed(buffer, block, index):
-        return lax.dynamic_update_slice(buffer, block[None], (index % N_TP, 0, 0))
-
-    cot = jnp.transpose(cotangent, (1, 2, 0))
-    own = lax.dynamic_slice_in_dim(cot, core * 64, 64, 1)
-    other = lax.dynamic_slice_in_dim(cot, (1 - core) * 64, 64, 1)
-    cot = jnp.concatenate([own, sibling(other, 0)], axis=2).reshape(128, 2 * tokens)
-    own_hidden = after(rows_in, cot[:1, :1])
-    hid_chip = jnp.concatenate([rows_in, sibling(own_hidden, 0)], axis=0)
-
-    def products(block):
-        product = jnp.dot(block, hid_chip, preferred_element_type=jnp.float32)
-        return product.astype(jnp.bfloat16)
+    place = jnp.stack([half_index, z, core]).astype(jnp.int32)
+
+    own, other = split(place, cotangent.reshape(tokens, 2 * HD))
+    cot = jnp.concatenate([own, sibling(other, 0)], axis=1)
 
     cots = [cot]
-    up = down = cot
+    own_hidden = after(rows_in, cot)
     hids = [rows_in]
-    h_up = along_z(own_hidden, 1, 1)
-    h_down = along_z(own_hidden, 1, -1)
-    sums = [(products(cot), z)]
-    for s in range(1, 4):
-        up = along_z(up, 0, 1)
-        down = along_z(down, 0, -1)
-        if s > 1:
-            up, down = after(up, sums[-1][0]), after(down, sums[-1][0])
-        if s == 2:
-            up, down, h_up, h_down = lax.optimization_barrier((up, down, h_up, h_down))
-            hids += [h_up, h_down]
-            h_up = along_z(h_up, 1, 1)
-            h_down = along_z(h_down, 1, -1)
-        cots += [up, down]
-        pair = products(jnp.concatenate([up, down], axis=0))
-        sums += [(pair[:128], z - s), (pair[128:], z + s)]
-    up, down, _ = lax.optimization_barrier((up, down, sums[-1][0]))
+    h_up, h_down = along_z(own_hidden, 1, 1), along_z(own_hidden, 1, -1)
+    up, down = along_z(cot, 0, 1), along_z(cot, 0, -1)
+    cots += [up, down]
+    hid_other = sibling(after(rows_in, up, down), 0)
+    up, down = along_z(up, 0, 1), along_z(down, 0, -1)
+    cots += [up, down]
+    up, down = after(up, h_up, h_down), after(down, h_up, h_down)
+    hids += [h_up, h_down]
+    h_up, h_down = along_z(h_up, 1, 1), along_z(h_down, 1, -1)
+    up, down = along_z(up, 0, 1), along_z(down, 0, -1)
+    cots += [up, down]
+    sums = product(place, (0, 1, 2, 3, 4), cots[:5], rows_in, hid_other)
+    up, down = after(up, sums[0]), after(down, sums[0])
     up, down = along_z(up[:64], 0, 1), along_z(down[64:], 0, -1)
-    up, down, h_up, h_down = lax.optimization_barrier((up, down, h_up, h_down))
+    sums = product(place, (5, 6), cots[5:], rows_in, hid_other, sums)
+    old = jnp.transpose(master, (1, 0, 2)).astype(jnp.bfloat16).reshape(128, features)
+    old = lax.all_gather(old, "fsdp", axis=0)
+    sums = (after(sums[0], up, down, old), sums[1])
+    partial, cot_other = product(place, (7,), (up, down), rows_in, hid_other, sums)
+    cots += [up, down]
+    gathered = lax.all_to_all(partial, "fsdp", 0, 0, axis_index_groups=SAME_CORE)
+    gathered, h_up, h_down = lax.optimization_barrier((gathered, h_up, h_down))
     hids += [h_up, h_down]
-    h_up = along_z(h_up, 1, 1)
-    h_down = along_z(h_down, 1, -1)
-    last = jnp.concatenate([up, down], axis=0)
-    cots.append(last)
-    sums.append((products(last), z + 4))
-
-    partial = jnp.zeros((N_TP, 128, features), jnp.bfloat16)
-    for block, index in sums:
-        partial = placed(partial, block, index)
-    gathered = lax.all_to_all(partial, "fsdp", 0, 0, axis_index_groups=SAME_CORE)
-    cot_other = jnp.stack([block[:, tokens:] for block in cots])
-    gathered, cot_other = lax.optimization_barrier((gathered, cot_other))
-
+    h_up, h_down = along_z(h_up, 1, 1), along_z(h_down, 1, -1)
     gradient = jnp.sum(gathered.astype(jnp.float32), axis=0) * scale
     gradient = jnp.transpose(gradient.reshape(2, 64, features), (1, 0, 2))
 
-    def updated(gradient):
-        new_first = first_decay * moment1 + (1.0 - first_decay) * gradient
-        new_second = second_decay * moment2 + (1.0 - second_decay) * gradient * gradient
-        first_hat = new_first / (1.0 - first_decay**OPT_STEP)
-        second_hat = new_second / (1.0 - second_decay**OPT_STEP)
-        new_master = master - learn_rate * (
-            first_hat / (jnp.sqrt(second_hat) + small_term) + weight_decay * master
-        )
-        return new_master, new_first, new_second
-
-    serving = jnp.transpose(updated(gradient)[0], (1, 0, 2)).astype(jnp.bfloat16)
-    serving = serving.reshape(N_TP, 16, features)
-
-    pieces = lax.all_to_all(serving, "fsdp", 0, 0, axis_index_groups=SAME_CORE)
-    pieces = lax.all_to_all(pieces, "tp", 0, 0)
-    h_up, h_down, pieces = lax.optimization_barrier((h_up, h_down, pieces))
+    serving = jnp.transpose(adam(gradient, master, moment1, moment2)[0], (1, 0, 2)).astype(jnp.bfloat16)
+    serving = serving.reshape(128, features)
+
+    def across(rows, flip):
+        pairs = [
+            ((p * 2 + c) * N_TP + plane, (N_FSDP + (plane ^ flip) * 2 + c) * N_TP + p)
+            for p in range(8)
+            for c in range(2)
+            for plane in range(N_TP)
+        ]
+        return lax.ppermute(rows, ("group", "fsdp", "tp"), pairs)
+
+    keys, values = across(serving[:64], 0), across(serving[64:], 4)
     hids += [h_up, h_down]
-    h_up = along_z(h_up[:half], 1, 1)
-    h_down = along_z(h_down[half:], 1, -1)
-    hids += [h_up, h_down]
-    gradient_late = after(gradient, pieces)
-    pieces = lax.ppermute(pieces, "group", [(0, 1)])
-    mirrored = lax.ppermute(gradient_late, "group", [(0, 1)])
-    cot_other = after(cot_other, pieces)
+    far_first, far_second = along_z(h_up[:half], 1, 1), along_z(h_down[half:], 1, -1)
+    hids += [far_first, far_second]
+    cot_other = after(cot_other, keys)
+    pieces = jnp.concatenate([keys, values], axis=0)
     w = lax.all_to_all(
         jnp.broadcast_to(pieces[None], (8,) + pieces.shape),
         "fsdp",
@@ -324,20 +439,18 @@
         axis_index_groups=SAME_CORE,
     )
     cot_other = sibling(cot_other, 0)
-
-    gradient = jnp.where(half_index == 0, gradient, mirrored)
-    new_master, new_first, new_second = updated(gradient)
-    w, new_master, new_first, new_second, *last_hids = lax.optimization_barrier(
-        (w, new_master, new_first, new_second, *hids[-2:])
-    )
-    hids[-2:] = last_hids
+    reach_of = jnp.repeat(lengths.astype(jnp.float32).reshape(-1, 8), STEPS, axis=1)
+    reach_of = jnp.tile(reach_of, (1, queries.shape[1] // HD))
+    w, reach_of, gradient, far_first, far_second = lax.optimization_barrier(
+        (w, reach_of, gradient, far_first, far_second)
+    )
+    hids[-2:] = [far_first, far_second]
+    mirrored = lax.ppermute(gradient, "group", [(0, 1)])
     w_other = lax.ppermute(w, "fsdp", [(i, i ^ 1) for i in range(N_FSDP)])
-
-    old = jnp.transpose(master, (1, 0, 2)).astype(jnp.bfloat16).reshape(128, features)
-    old = lax.all_gather(old, "fsdp", axis=0)
-    place = jnp.stack([half_index, z, core]).astype(jnp.int32)
-    block = final(place, hids, w, w_other, queries, kv_cache, lengths, cots, cot_other, old)
-    return (block[None], new_master, new_first, new_second)
+    block = final(place, hids, w, w_other, queries, kv_cache, reach_of, cots, cot_other, old)
+    mirrored, block = lax.optimization_barrier((mirrored, block))
+    outs = adam_outputs(place, gradient, mirrored, master, moment1, moment2)
+    return (block[None], *outs)
 
 
 def solution(mesh):

time: 248 us -> 223 us (0.90); the launches traced: 244 us -> 222 us
  local copies, waits for them, and re-layouts: 35 us -> 16.5 us
  waiting for transfers between devices: 80.6 us -> 96.9 us
  matrix products: 13.1 us -> 0 us
  other arithmetic: 15.3 us -> 5.17 us
  blocking collectives: 9.35 us -> 0 us
  starting transfers between devices: 60.4 us -> 67.3 us
  Pallas kernels: 15.3 us -> 21 us
    ppermute x16, waiting for transfers between devices: 34.6 us -> 73.1 us  [along_z(): return lax.ppermute(block, ('group', 'tp'), pairs)]
    ppermute x2 -> x3, waiting for transfers between devices: 29.5 us -> 11.8 us  [the longest x2 11.8 us: across(): return lax.ppermute(rows, ('group', 'fsdp', 'tp'), pairs)]
    all_to_all x1, starting transfers between devices: 5.19 us -> 20.9 us  [on_device(): lax.all_to_all(jnp.broadcast_to(pieces[None], (8,) + pieces.shape), 'fsdp...]
    dot_general x5 -> x0, matrix products: 13.1 us -> none  [products(): product = jnp.dot(block, hid_chip, preferred_element_type=jnp.float32)]
    all_to_all x1, waiting for transfers between devices: 0.01 us -> 11.6 us  [on_device(): lax.all_to_all(jnp.broadcast_to(pieces[None], (8,) + pieces.shape), 'fsdp...]
    all_to_all x1, waiting for transfers between devices: 11.3 us -> 0.01 us  [on_device(): lax.all_to_all(partial, 'fsdp', 0, 0, axis_index_groups=SAME_CORE)]
    unnamed x33 -> x62, local copies, waits for them, and re-layouts: 18.3 us -> 8.34 us
    all_to_all x1 -> x0, blocking collectives: 9.35 us -> none  [on_device(): pieces = lax.all_to_all(serving, 'fsdp', 0, 0, axis_index_groups=SAME_CORE)]
  transfers between devices with their start and end apart: 26 -> 26, of which waited for: 8 -> 9; matrix products, arithmetic and copies ran while one was open for 24% -> 4% of each run, Pallas kernels for 0% -> 8%
where the time goes in v2:
time: 223 us; the launch traced here: 222 us
  waiting for transfers between devices  96.9 us (43%)
  starting transfers between devices  67.3 us (30%)
  Pallas kernels  21 us (9%)
  local copies, waits for them, and re-layouts  16.5 us (7%)
  between operations  14.7 us (7%)
  other arithmetic  5.17 us (2%)
    ppermute x16, waiting for transfers between devices, along_z(): return lax.ppermute(block, ('group', 'tp'), pairs)  73.1 us
    ppermute x16, starting transfers between devices, along_z(): return lax.ppermute(block, ('group', 'tp'), pairs)  31.3 us
    all_to_all x1, starting transfers between devices, on_device(): lax.all_to_all(jnp.broadcast_to(pieces[None], (8,) + pieces.shape), 'fsdp...  20.9 us
    pallas_call x1, Pallas kernels, final(): pl.pallas_call(final_kernel, in_specs=in_specs, out_specs=anywhere, out_s...  16.1 us
    ppermute x2, waiting for transfers between devices, across(): return lax.ppermute(rows, ('group', 'fsdp', 'tp'), pairs)  11.8 us
    all_to_all x1, waiting for transfers between devices, on_device(): lax.all_to_all(jnp.broadcast_to(pieces[None], (8,) + pieces.shape), 'fsdp...  11.6 us
    unnamed x62, local copies, waits for them, and re-layouts  8.34 us
    all_to_all x1, starting transfers between devices, on_device(): lax.all_to_all(partial, 'fsdp', 0, 0, axis_index_groups=SAME_CORE)  5.33 us
  transfers between devices with their start and end apart: 26, of which 9 were waited for; matrix products, arithmetic and copies ran while one was open for 4% of the time, Pallas kernels for 8%

profile of v2, /device:TPU:121, one launch (start us, length us, event | category | flops | bytes accessed | tf_op | source)
XLA Modules:
  0.0 221.6 jit_solution(7586587794989934249)
XLA Ops:
  7.2 1.3 convert_bitcast_fusion
  8.5 0.8 copy.31
  10.8 0.7 collective-permute-start.1
  11.5 0.7 collective-permute-start.6
  12.2 4.8 %collective-permute-start.3 = (bf16[768,1024]{1,0:T(8,128)(2,1)S(1)}, bf16[768,1024]{1,0:T(8,128)(2,1)S(1)}, u32[]{:S(2)}, u32[]{:S(2)}) collective-permute-start(bf16[768,1024]{1,0:T(8,128)(2,1)S(1)} %bitcast.29), channel_id=1, source_target_pairs={{128,129},{129,130},{130,131},{131,132},{132,133},{133,134},{134,1... | collective-permute-start | bytes 4718600 | tf_op jit(solution)/shard_map/ppermute | solution.py:41
  16.9 1.9 collective-permute-start.4
  18.9 0.8 collective-permute-start.8
  19.7 0.7 collective-permute-start.7
  20.4 0.7 collective-permute-start.2
  21.1 28.9 %collective-permute-done.3.refs_1_ = bf16[768,1024]{1,0:T(8,128)(2,1)S(1)} collective-permute-done((bf16[768,1024]{1,0:T(8,128)(2,1)S(1)}, bf16[768,1024]{1,0:T(8,128)(2,1)S(1)}, u32[]{:S(2)}, u32[]{:S(2)}) %collective-permute-start.3) | collective-permute-done | bytes 1572896 | tf_op jit(solution)/shard_map/ppermute | solution.py:41
  50.0 5.0 %collective-permute-done.4.refs_2_ = bf16[768,1024]{1,0:T(8,128)(2,1)S(1)} collective-permute-done((bf16[768,1024]{1,0:T(8,128)(2,1)S(1)}, bf16[768,1024]{1,0:T(8,128)(2,1)S(1)}, u32[]{:S(2)}, u32[]{:S(2)}) %collective-permute-start.4) | collective-permute-done | bytes 1572896 | tf_op jit(solution)/shard_map/ppermute | solution.py:41
  55.7 0.7 collective-permute-start.5
  56.4 0.7 shard_map.112
  59.3 1.1 copy-done.1
  60.4 0.7 copy-done.12
  61.8 1.4 copy-done.2
  63.2 0.9 copy-done.13
  64.1 0.9 copy-done.15
  65.7 1.1 copy-done.3
  66.8 5.3 %all-to-all-start = ((bf16[8,128,1024]{2,1,0:T(8,128)(2,1)}), bf16[8,128,1024]{2,1,0:T(8,128)(2,1)}, u32[]{:S(2)}, u32[]{:S(2)}) async-start(bf16[8,128,1024]{2,1,0:T(8,128)(2,1)} %get-tuple-element.46), calls=%async_computation | async-start | bytes 4194304 | tf_op jit(solution)/shard_map/all_to_all | solution.py:409
  72.2 2.1 collective-permute-start.12
  74.2 3.4 %collective-permute-start.13 = (bf16[768,1024]{1,0:T(8,128)(2,1)}, bf16[768,1024]{1,0:T(8,128)(2,1)}, u32[]{:S(2)}, u32[]{:S(2)}) collective-permute-start(bf16[768,1024]{1,0:T(8,128)(2,1)} %copy-done.26), channel_id=1, source_target_pairs={{128,135},{129,128},{130,129},{131,130},{132,131},{133,132},{134,1... | collective-permute-start | bytes 4718600 | tf_op jit(solution)/shard_map/ppermute | solution.py:41
  77.6 30.2 %collective-permute-done.12.refs_3_ = bf16[768,1024]{1,0:T(8,128)(2,1)} collective-permute-done((bf16[768,1024]{1,0:T(8,128)(2,1)S(1)}, bf16[768,1024]{1,0:T(8,128)(2,1)}, u32[]{:S(2)}, u32[]{:S(2)}) %collective-permute-start.12) | collective-permute-done | bytes 1572896 | tf_op jit(solution)/shard_map/ppermute | solution.py:41
  107.8 3.4 %collective-permute-done.13.refs_4_ = bf16[768,1024]{1,0:T(8,128)(2,1)} collective-permute-done((bf16[768,1024]{1,0:T(8,128)(2,1)}, bf16[768,1024]{1,0:T(8,128)(2,1)}, u32[]{:S(2)}, u32[]{:S(2)}) %collective-permute-start.13) | collective-permute-done | bytes 1572896 | tf_op jit(solution)/shard_map/ppermute | solution.py:41
  111.1 2.0 convert_reduce_fusion
  113.2 1.9 collective-permute-start.16
  115.1 3.4 %collective-permute-start.18 = (bf16[768,1024]{1,0:T(8,128)(2,1)}, bf16[768,1024]{1,0:T(8,128)(2,1)}, u32[]{:S(2)}, u32[]{:S(2)}) collective-permute-start(bf16[768,1024]{1,0:T(8,128)(2,1)} %collective-permute-done.13.refs_4_), channel_id=1, source_target_pairs={{128,135},{129,128},{130,129},{131,130},{132,131},{133,132},{134,1... | collective-permute-start | bytes 4718600 | tf_op jit(solution)/shard_map/ppermute | solution.py:41
  118.5 1.7 fusion.3
  120.7 1.3 collective-permute-start.14
  122.1 1.3 collective-permute-start.15
  123.4 9.2 %collective-permute-done.14 = bf16[64,1024]{1,0:T(8,128)(2,1)S(1)} collective-permute-done((bf16[64,1024]{1,0:T(8,128)(2,1)S(1)}, bf16[64,1024]{1,0:T(8,128)(2,1)S(1)}, u32[]{:S(2)}, u32[]{:S(2)}) %collective-permute-start.14) | collective-permute-done | bytes 131104 | tf_op jit(solution)/shard_map/ppermute | solution.py:426
  132.5 2.6 %collective-permute-done.15 = bf16[64,1024]{1,0:T(8,128)(2,1)S(1)} collective-permute-done((bf16[64,1024]{1,0:T(8,128)(2,1)S(1)}, bf16[64,1024]{1,0:T(8,128)(2,1)S(1)}, u32[]{:S(2)}, u32[]{:S(2)}) %collective-permute-start.15) | collective-permute-done | bytes 131104 | tf_op jit(solution)/shard_map/ppermute | solution.py:426
  135.2 1.7 broadcast_in_dim.12
  136.8 20.9 %all-to-all-start.1 = ((bf16[8,128,1024]{2,1,0:T(8,128)(2,1)}), bf16[8,128,1024]{2,1,0:T(8,128)(2,1)}, u32[]{:S(2)}, u32[]{:S(2)}) async-start(bf16[8,128,1024]{2,1,0:T(8,128)(2,1)} %broadcast_in_dim.12), calls=%async_computation.1 | async-start | bytes 4194304 | tf_op jit(solution)/shard_map/all_to_all | solution.py:434
  157.8 1.2 copy-done.23
  159.0 0.9 slice.34
  159.9 6.5 %collective-permute-start.17 = (bf16[384,1024]{1,0:T(8,128)(2,1)}, bf16[384,1024]{1,0:T(8,128)(2,1)}, u32[]{:S(2)}, u32[]{:S(2)}) collective-permute-start(bf16[384,1024]{1,0:T(8,128)(2,1)} %slice.34), channel_id=1, source_target_pairs={{128,129},{129,130},{130,131},{131,132},{132,133},{133,134},{134,1... | collective-permute-start | bytes 2359304 | tf_op jit(solution)/shard_map/ppermute | solution.py:41
  166.5 2.1 slice.35
  168.5 1.9 collective-permute-start.19
  170.6 1.5 copy.44
  172.1 11.6 %all-to-all-done.1.refs_9_ = bf16[8,128,1024]{2,1,0:T(8,128)(2,1)} async-done(((bf16[8,128,1024]{2,1,0:T(8,128)(2,1)}), bf16[8,128,1024]{2,1,0:T(8,128)(2,1)}, u32[]{:S(2)}, u32[]{:S(2)}) %all-to-all-start.1) | async-done | bytes 2097184 | tf_op jit(solution)/shard_map/all_to_all | solution.py:434
  183.7 5.6 %collective-permute-done.19.refs_8_ = bf16[384,1024]{1,0:T(8,128)(2,1)} collective-permute-done((bf16[384,1024]{1,0:T(8,128)(2,1)}, bf16[384,1024]{1,0:T(8,128)(2,1)}, u32[]{:S(2)}, u32[]{:S(2)}) %collective-permute-start.19) | collective-permute-done | bytes 786464 | tf_op jit(solution)/shard_map/ppermute | solution.py:41
  189.4 2.6 %collective-permute-start.21 = (bf16[8,128,1024]{2,1,0:T(8,128)(2,1)}, bf16[8,128,1024]{2,1,0:T(8,128)(2,1)}, u32[]{:S(2)}, u32[]{:S(2)}) collective-permute-start(bf16[8,128,1024]{2,1,0:T(8,128)(2,1)} %all-to-all-done.1.refs_9_), channel_id=1, source_target_pairs={{0,8},{8,0},{16,24},{24,16},{32,40},{40,32},{48,56},{56,48},{64,72... | collective-permute-start | bytes 6291464 | tf_op jit(solution)/shard_map/ppermute | solution.py:449
  192.0 1.8 collective-permute-start.22
  193.8 1.3 collective-permute-start.20
  195.1 0.7 copy.34.refs_13_
  196.1 16.1 %shard_map.115 = bf16[768,1024]{1,0:T(8,128)(2,1)} custom-call(s32[3]{0:T(128)} %copy-done.20, bf16[768,1024]{1,0:T(8,128)(2,1)} %bitcast.28, bf16[768,1024]{1,0:T(8,128)(2,1)} %copy-done.24, bf16[768,1024]{1,0:T(8,128)(2,1)} %copy-done.26, bf16[768,1024]{1,0:T(8,128)(2,1)} %collective-permute-done.12.refs_3_, ...), custom_call_target="tpu_custom_call" | custom-call | flops 3221225472 | bytes 25165824 | tf_op jit(solution)/shard_map/pallas_call | solution.py:206
  212.3 2.4 %shard_map.116 = (f32[64,2,1024]{2,1,0:T(2,128)}, f32[64,2,1024]{2,1,0:T(2,128)}, f32[64,2,1024]{2,1,0:T(2,128)}) custom-call(s32[3]{0:T(128)S(1)} %copy-done.21, f32[64,2,1024]{2,1,0:T(2,128)S(1)} %bitcast.36, f32[64,2,1024]{2,1,0:T(2,128)} %collective-permute-done.20.mirrored, f32[64,2,1024]{2,1,0:T(2,128)S(1)} %copy-done.5, ...), custom_call_target="tpu_custom_call" | custom-call | tf_op jit(solution)/shard_map/pallas_call | solution.py:357
  (94 shorter events, 6.6 us)
Async XLA Ops:
  7.2 2.1 copy-start.27
  7.2 54.6 %all-gather.2.cloned.1.call-start = ((), (), s32[]{:S(2)}) async-start(), calls=%async_computation.2 | async-start | bytes 4456448 | tf_op jit(solution)/shard_map/all_gather | solution.py:405
  8.5 3.7 %copy-start = (bf16[1,768,1024]{2,1,0:T(8,128)(2,1)S(1)}, bf16[1,768,1024]{2,1,0:T(8,128)(2,1)}, u32[]{:S(2)}) copy-start(bf16[1,768,1024]{2,1,0:T(8,128)(2,1)} %param.8) | copy-start | bytes 4718596
  9.5 52.3 %copy-start.20 = (s32[3]{0:T(128)}, s32[3]{0:T(128)S(1)}, u32[]{:S(2)}) copy-start(s32[3]{0:T(128)S(1)} %pad_add_fusion.place) | copy-start | bytes 40
  10.0 0.7 collective-permute-start
  10.8 46.4 %copy-start.11 = (bf16[128,1536]{1,0:T(8,128)(2,1)}, bf16[128,1536]{1,0:T(8,128)(2,1)S(1)}, u32[]{:S(2)}) copy-start(bf16[128,1536]{1,0:T(8,128)(2,1)S(1)} %constant_dynamic-update-slice_fusion.refs_0_.refs_14_) | copy-start | bytes 1179652
  10.8 8.1 %collective-permute-start.1 = (bf16[128,1536]{1,0:T(8,128)(2,1)S(1)}, bf16[128,1536]{1,0:T(8,128)(2,1)S(1)}, u32[]{:S(2)}, u32[]{:S(2)}) collective-permute-start(bf16[128,1536]{1,0:T(8,128)(2,1)S(1)} %constant_dynamic-update-slice_fusion.refs_0_.refs_14_), channel_id=1, source_target_pairs={{0,1},{1,2},{2,3},{3,4},{4,5},{5,6},{6,7},{7,0},{8,9},{9,10},{10,1... | collective-permute-start | bytes 1179656 | tf_op jit(solution)/shard_map/ppermute | solution.py:41
  11.5 7.4 %collective-permute-start.6 = (bf16[128,1536]{1,0:T(8,128)(2,1)S(1)}, bf16[128,1536]{1,0:T(8,128)(2,1)S(1)}, u32[]{:S(2)}, u32[]{:S(2)}) collective-permute-start(bf16[128,1536]{1,0:T(8,128)(2,1)S(1)} %constant_dynamic-update-slice_fusion.refs_0_.refs_14_), channel_id=1, source_target_pairs={{0,7},{1,0},{2,1},{3,2},{4,3},{5,4},{6,5},{7,6},{8,15},{9,8},{10,9... | collective-permute-start | bytes 1179656 | tf_op jit(solution)/shard_map/ppermute | solution.py:41
  12.2 37.8 %collective-permute-start.3 = (bf16[768,1024]{1,0:T(8,128)(2,1)S(1)}, bf16[768,1024]{1,0:T(8,128)(2,1)S(1)}, u32[]{:S(2)}, u32[]{:S(2)}) collective-permute-start(bf16[768,1024]{1,0:T(8,128)(2,1)S(1)} %bitcast.29), channel_id=1, source_target_pairs={{128,129},{129,130},{130,131},{131,132},{132,133},{133,134},{134,1... | collective-permute-start | bytes 4718600 | tf_op jit(solution)/shard_map/ppermute | solution.py:41
  16.9 38.0 %collective-permute-start.4 = (bf16[768,1024]{1,0:T(8,128)(2,1)S(1)}, bf16[768,1024]{1,0:T(8,128)(2,1)S(1)}, u32[]{:S(2)}, u32[]{:S(2)}) collective-permute-start(bf16[768,1024]{1,0:T(8,128)(2,1)S(1)} %bitcast.30), channel_id=1, source_target_pairs={{128,135},{129,128},{130,129},{131,130},{132,131},{133,132},{134,1... | collective-permute-start | bytes 4718600 | tf_op jit(solution)/shard_map/ppermute | solution.py:41
  18.9 38.3 %copy-start.16 = (bf16[128,1536]{1,0:T(8,128)(2,1)}, bf16[128,1536]{1,0:T(8,128)(2,1)S(1)}, u32[]{:S(2)}) copy-start(bf16[128,1536]{1,0:T(8,128)(2,1)S(1)} %collective-permute-done.1.refs_1_.refs_15_) | copy-start | bytes 1179652
  18.9 38.3 %copy-start.17 = (bf16[128,1536]{1,0:T(8,128)(2,1)}, bf16[128,1536]{1,0:T(8,128)(2,1)S(1)}, u32[]{:S(2)}) copy-start(bf16[128,1536]{1,0:T(8,128)(2,1)S(1)} %collective-permute-done.6.refs_2_.refs_16_) | copy-start | bytes 1179652
  18.9 37.5 %collective-permute-start.8 = (bf16[768,1024]{1,0:T(8,128)(2,1)S(1)}, bf16[768,1024]{1,0:T(8,128)(2,1)S(1)}, u32[]{:S(2)}, u32[]{:S(2)}) collective-permute-start(bf16[768,1024]{1,0:T(8,128)(2,1)S(1)} %bitcast.31), channel_id=1, source_target_pairs={{0,8},{8,0},{16,24},{24,16},{32,40},{40,32},{48,56},{56,48},{64,72... | collective-permute-start | bytes 4718600 | tf_op jit(solution)/shard_map/ppermute | solution.py:36
  19.7 1.4 collective-permute-start.7
  20.4 35.3 %collective-permute-start.2 = (bf16[128,1536]{1,0:T(8,128)(2,1)S(1)}, bf16[128,1536]{1,0:T(8,128)(2,1)S(1)}, u32[]{:S(2)}, u32[]{:S(2)}) collective-permute-start(bf16[128,1536]{1,0:T(8,128)(2,1)S(1)} %collective-permute-done.1.refs_1_.refs_15_), channel_id=1, source_target_pairs={{0,1},{1,2},{2,3},{3,4},{4,5},{5,6},{6,7},{7,0},{8,9},{9,10},{10,1... | collective-permute-start | bytes 1179656 | tf_op jit(solution)/shard_map/ppermute | solution.py:41
  21.1 36.1 %copy-start.18 = (bf16[128,1536]{1,0:T(8,128)(2,1)}, bf16[128,1536]{1,0:T(8,128)(2,1)S(1)}, u32[]{:S(2)}) copy-start(bf16[128,1536]{1,0:T(8,128)(2,1)S(1)} %collective-permute-done.7.refs_4_.refs_18_) | copy-start | bytes 1179652
  50.0 6.4 %copy-start.24 = (bf16[768,1024]{1,0:T(8,128)(2,1)}, bf16[768,1024]{1,0:T(8,128)(2,1)S(1)}, u32[]{:S(2)}) copy-start(bf16[768,1024]{1,0:T(8,128)(2,1)S(1)} %collective-permute-done.3.refs_1_) | copy-start | bytes 4718596
  55.0 1.4 copy-start.26
  55.0 2.2 collective-permute-start.10
  55.7 1.5 copy-start.19
  55.7 1.5 collective-permute-start.5
  57.2 2.1 copy-start.6
  57.2 2.1 copy-start.7
  57.2 3.2 %collective-permute-start.11 = (bf16[64,1536]{1,0:T(8,128)(2,1)S(1)}, bf16[64,1536]{1,0:T(8,128)(2,1)S(1)}, u32[]{:S(2)}, u32[]{:S(2)}) collective-permute-start(bf16[64,1536]{1,0:T(8,128)(2,1)S(1)} %slice.25), channel_id=1, source_target_pairs={{0,7},{1,0},{2,1},{3,2},{4,3},{5,4},{6,5},{7,6},{8,15},{9,8},{10,9... | collective-permute-start | bytes 589832 | tf_op jit(solution)/shard_map/ppermute | solution.py:41
  57.9 3.2 %collective-permute-start.9 = (bf16[64,1536]{1,0:T(8,128)(2,1)S(1)}, bf16[64,1536]{1,0:T(8,128)(2,1)S(1)}, u32[]{:S(2)}, u32[]{:S(2)}) collective-permute-start(bf16[64,1536]{1,0:T(8,128)(2,1)S(1)} %slice.24), channel_id=1, source_target_pairs={{0,1},{1,2},{2,3},{3,4},{4,5},{5,6},{6,7},{7,0},{8,9},{9,10},{10,1... | collective-permute-start | bytes 589832 | tf_op jit(solution)/shard_map/ppermute | solution.py:41
  61.8 1.4 copy-start.2
  66.8 5.3 %copy-start.25 = (bf16[768,1024]{1,0:T(8,128)(2,1)S(1)}, bf16[768,1024]{1,0:T(8,128)(2,1)}, u32[]{:S(2)}) copy-start(bf16[768,1024]{1,0:T(8,128)(2,1)} %copy-done.24) | copy-start | bytes 4718596
  66.8 44.3 %all-to-all-start = ((bf16[8,128,1024]{2,1,0:T(8,128)(2,1)}), bf16[8,128,1024]{2,1,0:T(8,128)(2,1)}, u32[]{:S(2)}, u32[]{:S(2)}) async-start(bf16[8,128,1024]{2,1,0:T(8,128)(2,1)} %get-tuple-element.46), calls=%async_computation | async-start | bytes 4194304 | tf_op jit(solution)/shard_map/all_to_all | solution.py:409
  72.1 46.4 %copy-start.5 = (f32[64,2,1024]{2,1,0:T(2,128)S(1)}, f32[64,2,1024]{2,1,0:T(2,128)}, u32[]{:S(2)}) copy-start(f32[64,2,1024]{2,1,0:T(2,128)} %master.1) | copy-start | bytes 1572868
  72.1 46.4 %copy-start.8 = (f32[64,2,1024]{2,1,0:T(2,128)S(1)}, f32[64,2,1024]{2,1,0:T(2,128)}, u32[]{:S(2)}) copy-start(f32[64,2,1024]{2,1,0:T(2,128)} %moment2.1) | copy-start | bytes 1572868
  72.2 46.4 %copy-start.9 = (f32[64,2,1024]{2,1,0:T(2,128)S(1)}, f32[64,2,1024]{2,1,0:T(2,128)}, u32[]{:S(2)}) copy-start(f32[64,2,1024]{2,1,0:T(2,128)} %moment1.1) | copy-start | bytes 1572868
  72.2 35.6 %collective-permute-start.12 = (bf16[768,1024]{1,0:T(8,128)(2,1)S(1)}, bf16[768,1024]{1,0:T(8,128)(2,1)}, u32[]{:S(2)}, u32[]{:S(2)}) collective-permute-start(bf16[768,1024]{1,0:T(8,128)(2,1)S(1)} %copy-done.25), channel_id=1, source_target_pairs={{128,129},{129,130},{130,131},{131,132},{132,133},{133,134},{134,1... | collective-permute-start | bytes 4718600 | tf_op jit(solution)/shard_map/ppermute | solution.py:41
  74.2 36.9 %collective-permute-start.13 = (bf16[768,1024]{1,0:T(8,128)(2,1)}, bf16[768,1024]{1,0:T(8,128)(2,1)}, u32[]{:S(2)}, u32[]{:S(2)}) collective-permute-start(bf16[768,1024]{1,0:T(8,128)(2,1)} %copy-done.26), channel_id=1, source_target_pairs={{128,135},{129,128},{130,129},{131,130},{132,131},{133,132},{134,1... | collective-permute-start | bytes 4718600 | tf_op jit(solution)/shard_map/ppermute | solution.py:41
  113.2 7.5 %copy-start.22 = (f32[128,1024]{1,0:T(8,128)}, f32[128,1024]{1,0:T(8,128)S(1)}, u32[]{:S(2)}) copy-start(f32[128,1024]{1,0:T(8,128)S(1)} %broadcast_multiply_fusion) | copy-start | bytes 1572868
  113.2 44.6 %collective-permute-start.16 = (bf16[768,1024]{1,0:T(8,128)(2,1)}, bf16[768,1024]{1,0:T(8,128)(2,1)S(1)}, u32[]{:S(2)}, u32[]{:S(2)}) collective-permute-start(bf16[768,1024]{1,0:T(8,128)(2,1)} %collective-permute-done.12.refs_3_), channel_id=1, source_target_pairs={{128,129},{129,130},{130,131},{131,132},{132,133},{133,134},{134,1... | collective-permute-start | bytes 4718600 | tf_op jit(solution)/shard_map/ppermute | solution.py:41
  115.1 51.3 %collective-permute-start.18 = (bf16[768,1024]{1,0:T(8,128)(2,1)}, bf16[768,1024]{1,0:T(8,128)(2,1)}, u32[]{:S(2)}, u32[]{:S(2)}) collective-permute-start(bf16[768,1024]{1,0:T(8,128)(2,1)} %collective-permute-done.13.refs_4_), channel_id=1, source_target_pairs={{128,135},{129,128},{130,129},{131,130},{132,131},{133,132},{134,1... | collective-permute-start | bytes 4718600 | tf_op jit(solution)/shard_map/ppermute | solution.py:41
  120.7 11.8 %collective-permute-start.14 = (bf16[64,1024]{1,0:T(8,128)(2,1)S(1)}, bf16[64,1024]{1,0:T(8,128)(2,1)S(1)}, u32[]{:S(2)}, u32[]{:S(2)}) collective-permute-start(bf16[64,1024]{1,0:T(8,128)(2,1)S(1)} %bitcast.44), channel_id=1, source_target_pairs={{0,128},{1,144},{2,160},{3,176},{4,192},{5,208},{6,224},{7,240},{8... | collective-permute-start | bytes 393224 | tf_op jit(solution)/shard_map/ppermute | solution.py:426
  122.1 13.1 %collective-permute-start.15 = (bf16[64,1024]{1,0:T(8,128)(2,1)S(1)}, bf16[64,1024]{1,0:T(8,128)(2,1)S(1)}, u32[]{:S(2)}, u32[]{:S(2)}) collective-permute-start(bf16[64,1024]{1,0:T(8,128)(2,1)S(1)} %bitcast.45), channel_id=1, source_target_pairs={{0,192},{1,208},{2,224},{3,240},{4,128},{5,144},{6,160},{7,176},{8... | collective-permute-start | bytes 393224 | tf_op jit(solution)/shard_map/ppermute | solution.py:426
  136.8 46.9 %all-to-all-start.1 = ((bf16[8,128,1024]{2,1,0:T(8,128)(2,1)}), bf16[8,128,1024]{2,1,0:T(8,128)(2,1)}, u32[]{:S(2)}, u32[]{:S(2)}) async-start(bf16[8,128,1024]{2,1,0:T(8,128)(2,1)} %broadcast_in_dim.12), calls=%async_computation.1 | async-start | bytes 4194304 | tf_op jit(solution)/shard_map/all_to_all | solution.py:434
  157.8 12.7 %copy-start.28 = (s32[384]{0:T(512)S(1)}, s32[384]{0:T(512)}, u32[]{:S(2)}) copy-start(s32[384]{0:T(512)} %param.12) | copy-start | bytes 4612
  159.9 32.1 %copy-start.4 = (bf16[8,128,768]{2,1,0:T(8,128)(2,1)S(1)}, bf16[8,128,768]{2,1,0:T(8,128)(2,1)}, u32[]{:S(2)}) copy-start(bf16[8,128,768]{2,1,0:T(8,128)(2,1)} %copy-done.3) | copy-start | bytes 4718596
  159.9 23.8 %collective-permute-start.17 = (bf16[384,1024]{1,0:T(8,128)(2,1)}, bf16[384,1024]{1,0:T(8,128)(2,1)}, u32[]{:S(2)}, u32[]{:S(2)}) collective-permute-start(bf16[384,1024]{1,0:T(8,128)(2,1)} %slice.34), channel_id=1, source_target_pairs={{128,129},{129,130},{130,131},{131,132},{132,133},{133,134},{134,1... | collective-permute-start | bytes 2359304 | tf_op jit(solution)/shard_map/ppermute | solution.py:41
  168.5 20.8 %collective-permute-start.19 = (bf16[384,1024]{1,0:T(8,128)(2,1)}, bf16[384,1024]{1,0:T(8,128)(2,1)}, u32[]{:S(2)}, u32[]{:S(2)}) collective-permute-start(bf16[384,1024]{1,0:T(8,128)(2,1)} %slice.35), channel_id=1, source_target_pairs={{128,135},{129,128},{130,129},{131,130},{132,131},{133,132},{134,1... | collective-permute-start | bytes 2359304 | tf_op jit(solution)/shard_map/ppermute | solution.py:41
  189.4 6.8 %collective-permute-start.21 = (bf16[8,128,1024]{2,1,0:T(8,128)(2,1)}, bf16[8,128,1024]{2,1,0:T(8,128)(2,1)}, u32[]{:S(2)}, u32[]{:S(2)}) collective-permute-start(bf16[8,128,1024]{2,1,0:T(8,128)(2,1)} %all-to-all-done.1.refs_9_), channel_id=1, source_target_pairs={{0,8},{8,0},{16,24},{24,16},{32,40},{40,32},{48,56},{56,48},{64,72... | collective-permute-start | bytes 6291464 | tf_op jit(solution)/shard_map/ppermute | solution.py:449
  192.0 3.8 %collective-permute-start.22 = (bf16[8,128,768]{2,1,0:T(8,128)(2,1)S(1)}, bf16[8,128,768]{2,1,0:T(8,128)(2,1)}, u32[]{:S(2)}, u32[]{:S(2)}) collective-permute-start(bf16[8,128,768]{2,1,0:T(8,128)(2,1)S(1)} %copy-done.4), channel_id=1, source_target_pairs={{0,8},{8,0},{16,24},{24,16},{32,40},{40,32},{48,56},{56,48},{64,72... | collective-permute-start | bytes 4718600 | tf_op jit(solution)/shard_map/ppermute | solution.py:36
  193.8 18.5 %collective-permute-start.20 = (f32[64,2,1024]{2,1,0:T(2,128)S(1)}, f32[64,2,1024]{2,1,0:T(2,128)}, u32[]{:S(2)}, u32[]{:S(2)}) collective-permute-start(f32[64,2,1024]{2,1,0:T(2,128)S(1)} %bitcast.35), channel_id=1, source_target_pairs={{0,128},{1,129},{2,130},{3,131},{4,132},{5,133},{6,134},{7,135},{8... | collective-permute-start | bytes 1572872 | tf_op jit(solution)/shard_map/ppermute | solution.py:448
  195.8 16.5 %copy-start.10 = (f32[64,2,1024]{2,1,0:T(2,128)S(1)}, f32[64,2,1024]{2,1,0:T(2,128)}, u32[]{:S(2)}) copy-start(f32[64,2,1024]{2,1,0:T(2,128)} %moment1.1) | copy-start | bytes 1572868
  195.8 16.5 %copy-start.21 = (s32[3]{0:T(128)S(1)}, s32[3]{0:T(128)}, u32[]{:S(2)}) copy-start(s32[3]{0:T(128)} %copy-done.20) | copy-start | bytes 40
  (7 other events, 6.7 us)
Sparse Core Ops, SparseCore 0:
  10.4 41.6 all-gather.1

commit v3 on v2

--- a/solution.py
+++ b/solution.py
@@ -263,7 +263,7 @@
     count = len(ids)
     blocks, refs = refs[: count * halves], refs[count * halves :]
     hid_own, hid_other = refs[:2]
-    refs = refs[2:] if first else refs[4:]
+    refs = refs[2:] if first else refs[3:]
     partial, cot_other, block_v, hid_v, out_v, block_sem, hid_sem, out_sem, cot_sem = refs
     tokens, features = hid_own.shape
     rows = HD // halves
@@ -279,7 +279,7 @@
         for i, block in enumerate(blocks):
             at = pl.ds(i * rows, rows)
             loads.append(pltpu.make_async_copy(block, block_v.at[at], block_sem.at[i]))
-            part = cot_other.at[ids[i // halves], pl.ds(i % halves * rows, rows)]
+            part = cot_other.at[i // halves, pl.ds(i % halves * rows, rows)]
             stores.append(
                 pltpu.make_async_copy(block.at[:, pl.ds(tokens, tokens)], part, cot_sem.at[i])
             )
@@ -303,7 +303,7 @@
             store.wait()
 
 
-def product(place, ids, blocks, hid_own, hid_other, before=()):
+def product(place, ids, blocks, hid_own, hid_other, *before):
     first = not before
     tokens, features = hid_own.shape
     operands = (place, *blocks, hid_own, hid_other, *before)
@@ -317,9 +317,9 @@
         out_specs=[pl.BlockSpec(memory_space=pl.ANY)] * 2,
         out_shape=[
             jax.ShapeDtypeStruct((N_TP, HD, features), jnp.bfloat16),
-            jax.ShapeDtypeStruct((N_TP, HD, tokens), jnp.bfloat16),
+            jax.ShapeDtypeStruct((len(ids), HD, tokens), jnp.bfloat16),
         ],
-        input_output_aliases={} if first else {len(operands) - 2: 0, len(operands) - 1: 1},
+        input_output_aliases={} if first else {len(operands) - 1: 0},
         scratch_shapes=[
             pltpu.VMEM((rows, 2 * tokens), jnp.bfloat16),
             pltpu.VMEM((2 * tokens, features), jnp.bfloat16),
@@ -395,26 +395,25 @@
     up, down = after(up, h_up, h_down), after(down, h_up, h_down)
     hids += [h_up, h_down]
     h_up, h_down = along_z(h_up, 1, 1), along_z(h_down, 1, -1)
+    far_up, far_down = along_z(up[:64], 0, 2), along_z(down[64:], 0, -2)
     up, down = along_z(up, 0, 1), along_z(down, 0, -1)
     cots += [up, down]
-    sums = product(place, (0, 1, 2, 3, 4), cots[:5], rows_in, hid_other)
-    up, down = after(up, sums[0]), after(down, sums[0])
-    up, down = along_z(up[:64], 0, 1), along_z(down[64:], 0, -1)
-    sums = product(place, (5, 6), cots[5:], rows_in, hid_other, sums)
+    partial, others = product(place, (0, 1, 2, 3, 4), cots[:5], rows_in, hid_other)
+    partial, more = product(place, (5, 6), cots[5:], rows_in, hid_other, partial)
     old = jnp.transpose(master, (1, 0, 2)).astype(jnp.bfloat16).reshape(128, features)
     old = lax.all_gather(old, "fsdp", axis=0)
-    sums = (after(sums[0], up, down, old), sums[1])
-    partial, cot_other = product(place, (7,), (up, down), rows_in, hid_other, sums)
+    partial, up, down, old = lax.optimization_barrier((partial, far_up, far_down, old))
+    partial, last = product(place, (7,), (up, down), rows_in, hid_other, partial)
     cots += [up, down]
     gathered = lax.all_to_all(partial, "fsdp", 0, 0, axis_index_groups=SAME_CORE)
-    gathered, h_up, h_down = lax.optimization_barrier((gathered, h_up, h_down))
+    gradient = jnp.sum(gathered.astype(jnp.float32), axis=0) * scale
+    gradient = jnp.transpose(gradient.reshape(2, 64, features), (1, 0, 2))
+
+    serving = jnp.transpose(adam(gradient, master, moment1, moment2)[0], (1, 0, 2)).astype(jnp.bfloat16)
+    serving = serving.reshape(128, features)
+    serving, h_up, h_down = lax.optimization_barrier((serving, h_up, h_down))
     hids += [h_up, h_down]
     h_up, h_down = along_z(h_up, 1, 1), along_z(h_down, 1, -1)
-    gradient = jnp.sum(gathered.astype(jnp.float32), axis=0) * scale
-    gradient = jnp.transpose(gradient.reshape(2, 64, features), (1, 0, 2))
-
-    serving = jnp.transpose(adam(gradient, master, moment1, moment2)[0], (1, 0, 2)).astype(jnp.bfloat16)
-    serving = serving.reshape(128, features)
 
     def across(rows, flip):
         pairs = [
@@ -429,7 +428,8 @@
     hids += [h_up, h_down]
     far_first, far_second = along_z(h_up[:half], 1, 1), along_z(h_down[half:], 1, -1)
     hids += [far_first, far_second]
-    cot_other = after(cot_other, keys)
+    cot_other = jnp.concatenate([others, more, last], axis=0)
+    keys, values, cot_other = lax.optimization_barrier((keys, values, cot_other))
     pieces = jnp.concatenate([keys, values], axis=0)
     w = lax.all_to_all(
         jnp.broadcast_to(pieces[None], (8,) + pieces.shape),
@@ -441,8 +441,8 @@
     cot_other = sibling(cot_other, 0)
     reach_of = jnp.repeat(lengths.astype(jnp.float32).reshape(-1, 8), STEPS, axis=1)
     reach_of = jnp.tile(reach_of, (1, queries.shape[1] // HD))
-    w, reach_of, gradient, far_first, far_second = lax.optimization_barrier(
-        (w, reach_of, gradient, far_first, far_second)
+    w, reach_of, gradient, far_first, far_second, cot_other = lax.optimization_barrier(
+        (w, reach_of, gradient, far_first, far_second, cot_other)
     )
     hids[-2:] = [far_first, far_second]
     mirrored = lax.ppermute(gradient, "group", [(0, 1)])

time: 223 us -> 217 us (0.973)
  local copies, waits for them, and re-layouts: 16.5 us -> 12.3 us
  waiting for transfers between devices: 96.9 us -> 94.6 us
    ppermute x16, waiting for transfers between devices: 73.1 us -> 49.6 us  [along_z(): return lax.ppermute(block, ('group', 'tp'), pairs)]
    all_to_all x1, waiting for transfers between devices: 0.01 us -> 20.5 us  [on_device(): lax.all_to_all(partial, 'fsdp', 0, 0, axis_index_groups=SAME_CORE)]
    unnamed x62 -> x48, local copies, waits for them, and re-layouts: 8.34 us -> 5.31 us
  transfers between devices with their start and end apart: 26 -> 26, of which waited for: 9 -> 10; matrix products, arithmetic and copies ran while one was open for 4% -> 5% of each run, Pallas kernels for 8% -> 8%
where the time goes in v3:
time: 217 us; the launch traced here: 216 us
  waiting for transfers between devices  94.6 us (44%)
  starting transfers between devices  67.2 us (31%)
  Pallas kernels  20.5 us (9%)
  between operations  14.7 us (7%)
  local copies, waits for them, and re-layouts  12.3 us (6%)
  other arithmetic  6.5 us (3%)
    ppermute x16, waiting for transfers between devices, along_z(): return lax.ppermute(block, ('group', 'tp'), pairs)  49.6 us
    ppermute x16, starting transfers between devices, along_z(): return lax.ppermute(block, ('group', 'tp'), pairs)  31.1 us
    all_to_all x1, starting transfers between devices, on_device(): lax.all_to_all(jnp.broadcast_to(pieces[None], (8,) + pieces.shape), 'fsdp...  20.9 us
    all_to_all x1, waiting for transfers between devices, on_device(): lax.all_to_all(partial, 'fsdp', 0, 0, axis_index_groups=SAME_CORE)  20.5 us
    pallas_call x1, Pallas kernels, final(): pl.pallas_call(final_kernel, in_specs=in_specs, out_specs=anywhere, out_s...  16.2 us
    all_to_all x1, waiting for transfers between devices, on_device(): lax.all_to_all(jnp.broadcast_to(pieces[None], (8,) + pieces.shape), 'fsdp...  11.8 us
    ppermute x2, waiting for transfers between devices, across(): return lax.ppermute(rows, ('group', 'fsdp', 'tp'), pairs)  10.5 us
    unnamed x48, local copies, waits for them, and re-layouts  5.31 us
  transfers between devices with their start and end apart: 26, of which 10 were waited for; matrix products, arithmetic and copies ran while one was open for 5% of the time, Pallas kernels for 8%

profile of v3, /device:TPU:121, one launch (start us, length us, event | category | flops | bytes accessed | tf_op | source)
XLA Modules:
  0.0 215.8 jit_solution(9585731350966910191)
XLA Ops:
  7.2 1.3 convert_bitcast_fusion
  8.5 0.7 copy.26
  10.8 0.7 collective-permute-start.1
  11.5 0.7 collective-permute-start.6
  12.2 4.8 %collective-permute-start.3 = (bf16[768,1024]{1,0:T(8,128)(2,1)S(1)}, bf16[768,1024]{1,0:T(8,128)(2,1)}, u32[]{:S(2)}, u32[]{:S(2)}) collective-permute-start(bf16[768,1024]{1,0:T(8,128)(2,1)S(1)} %bitcast.24), channel_id=1, source_target_pairs={{128,129},{129,130},{130,131},{131,132},{132,133},{133,134},{134,1... | collective-permute-start | bytes 4718600 | tf_op jit(solution)/shard_map/ppermute | solution.py:41
  16.9 1.9 collective-permute-start.4
  18.9 0.8 collective-permute-start.9
  19.7 0.7 collective-permute-start.7
  20.4 0.7 collective-permute-start.2
  21.1 28.9 %collective-permute-done.3.refs_1_ = bf16[768,1024]{1,0:T(8,128)(2,1)} collective-permute-done((bf16[768,1024]{1,0:T(8,128)(2,1)S(1)}, bf16[768,1024]{1,0:T(8,128)(2,1)}, u32[]{:S(2)}, u32[]{:S(2)}) %collective-permute-start.3) | collective-permute-done | bytes 1572896 | tf_op jit(solution)/shard_map/ppermute | solution.py:41
  50.0 5.1 %collective-permute-done.4.refs_2_ = bf16[768,1024]{1,0:T(8,128)(2,1)} collective-permute-done((bf16[768,1024]{1,0:T(8,128)(2,1)S(1)}, bf16[768,1024]{1,0:T(8,128)(2,1)}, u32[]{:S(2)}, u32[]{:S(2)}) %collective-permute-start.4) | collective-permute-done | bytes 1572896 | tf_op jit(solution)/shard_map/ppermute | solution.py:41
  55.8 0.7 collective-permute-start.5
  57.9 0.7 shard_map.112
  58.7 0.9 copy-done.6
  60.5 0.8 copy-done.17
  61.9 0.7 copy-done.13
  62.6 0.9 copy-done.12
  63.6 0.9 copy-done.14
  65.1 5.2 %all-to-all-start = ((bf16[8,128,1024]{2,1,0:T(8,128)(2,1)}), bf16[8,128,1024]{2,1,0:T(8,128)(2,1)}, u32[]{:S(2)}, u32[]{:S(2)}) async-start(bf16[8,128,1024]{2,1,0:T(8,128)(2,1)} %get-tuple-element.48), calls=%async_computation | async-start | bytes 4194304 | tf_op jit(solution)/shard_map/all_to_all | solution.py:408
  70.3 2.1 collective-permute-start.12
  72.4 3.4 %collective-permute-start.13 = (bf16[768,1024]{1,0:T(8,128)(2,1)}, bf16[768,1024]{1,0:T(8,128)(2,1)}, u32[]{:S(2)}, u32[]{:S(2)}) collective-permute-start(bf16[768,1024]{1,0:T(8,128)(2,1)} %collective-permute-done.4.refs_2_), channel_id=1, source_target_pairs={{128,135},{129,128},{130,129},{131,130},{132,131},{133,132},{134,1... | collective-permute-start | bytes 4718600 | tf_op jit(solution)/shard_map/ppermute | solution.py:41
  75.8 20.5 %all-to-all-done = bf16[8,128,1024]{2,1,0:T(8,128)(2,1)} async-done(((bf16[8,128,1024]{2,1,0:T(8,128)(2,1)}), bf16[8,128,1024]{2,1,0:T(8,128)(2,1)}, u32[]{:S(2)}, u32[]{:S(2)}) %all-to-all-start) | async-done | bytes 2097184 | tf_op jit(solution)/shard_map/all_to_all | solution.py:408
  96.3 2.0 convert_reduce_fusion
  98.4 1.7 fusion.3
  100.2 5.9 %collective-permute-done.12.refs_3_ = bf16[768,1024]{1,0:T(8,128)(2,1)} collective-permute-done((bf16[768,1024]{1,0:T(8,128)(2,1)}, bf16[768,1024]{1,0:T(8,128)(2,1)}, u32[]{:S(2)}, u32[]{:S(2)}) %collective-permute-start.12) | collective-permute-done | bytes 1572896 | tf_op jit(solution)/shard_map/ppermute | solution.py:41
  106.1 3.1 %collective-permute-done.13.refs_4_ = bf16[768,1024]{1,0:T(8,128)(2,1)} collective-permute-done((bf16[768,1024]{1,0:T(8,128)(2,1)}, bf16[768,1024]{1,0:T(8,128)(2,1)}, u32[]{:S(2)}, u32[]{:S(2)}) %collective-permute-start.13) | collective-permute-done | bytes 1572896 | tf_op jit(solution)/shard_map/ppermute | solution.py:41
  109.3 1.9 collective-permute-start.16
  111.2 3.4 %collective-permute-start.18 = (bf16[768,1024]{1,0:T(8,128)(2,1)}, bf16[768,1024]{1,0:T(8,128)(2,1)}, u32[]{:S(2)}, u32[]{:S(2)}) collective-permute-start(bf16[768,1024]{1,0:T(8,128)(2,1)} %collective-permute-done.13.refs_4_), channel_id=1, source_target_pairs={{128,135},{129,128},{130,129},{131,130},{132,131},{133,132},{134,1... | collective-permute-start | bytes 4718600 | tf_op jit(solution)/shard_map/ppermute | solution.py:41
  114.6 1.3 collective-permute-start.14
  115.9 1.3 collective-permute-start.15
  117.2 1.3 pad_maximum_fusion
  118.6 7.9 %collective-permute-done.14 = bf16[64,1024]{1,0:T(8,128)(2,1)S(1)} collective-permute-done((bf16[64,1024]{1,0:T(8,128)(2,1)S(1)}, bf16[64,1024]{1,0:T(8,128)(2,1)S(1)}, u32[]{:S(2)}, u32[]{:S(2)}) %collective-permute-start.14) | collective-permute-done | bytes 131104 | tf_op jit(solution)/shard_map/ppermute | solution.py:425
  126.4 2.6 %collective-permute-done.15 = bf16[64,1024]{1,0:T(8,128)(2,1)S(1)} collective-permute-done((bf16[64,1024]{1,0:T(8,128)(2,1)S(1)}, bf16[64,1024]{1,0:T(8,128)(2,1)S(1)}, u32[]{:S(2)}, u32[]{:S(2)}) %collective-permute-start.15) | collective-permute-done | bytes 131104 | tf_op jit(solution)/shard_map/ppermute | solution.py:425
  129.1 1.6 broadcast_in_dim.12
  130.7 20.9 %all-to-all-start.1 = ((bf16[8,128,1024]{2,1,0:T(8,128)(2,1)}), bf16[8,128,1024]{2,1,0:T(8,128)(2,1)}, u32[]{:S(2)}, u32[]{:S(2)}) async-start(bf16[8,128,1024]{2,1,0:T(8,128)(2,1)} %broadcast_in_dim.12), calls=%async_computation.1 | async-start | bytes 4194304 | tf_op jit(solution)/shard_map/all_to_all | solution.py:434
  151.6 1.9 collective-permute-start.20
  153.6 1.2 slice.24
  154.8 6.4 %collective-permute-start.17 = (bf16[384,1024]{1,0:T(8,128)(2,1)S(1)}, bf16[384,1024]{1,0:T(8,128)(2,1)}, u32[]{:S(2)}, u32[]{:S(2)}) collective-permute-start(bf16[384,1024]{1,0:T(8,128)(2,1)S(1)} %slice.24), channel_id=1, source_target_pairs={{128,129},{129,130},{130,131},{131,132},{132,133},{133,134},{134,1... | collective-permute-start | bytes 2359304 | tf_op jit(solution)/shard_map/ppermute | solution.py:41
  161.2 2.1 slice.25
  163.3 1.9 collective-permute-start.19
  165.8 11.8 %all-to-all-done.1.refs_9_ = bf16[8,128,1024]{2,1,0:T(8,128)(2,1)} async-done(((bf16[8,128,1024]{2,1,0:T(8,128)(2,1)}), bf16[8,128,1024]{2,1,0:T(8,128)(2,1)}, u32[]{:S(2)}, u32[]{:S(2)}) %all-to-all-start.1) | async-done | bytes 2097184 | tf_op jit(solution)/shard_map/all_to_all | solution.py:434
  177.6 6.5 %collective-permute-done.19.refs_8_ = bf16[384,1024]{1,0:T(8,128)(2,1)} collective-permute-done((bf16[384,1024]{1,0:T(8,128)(2,1)}, bf16[384,1024]{1,0:T(8,128)(2,1)}, u32[]{:S(2)}, u32[]{:S(2)}) %collective-permute-start.19) | collective-permute-done | bytes 786464 | tf_op jit(solution)/shard_map/ppermute | solution.py:41
  184.1 2.6 %collective-permute-start.22 = (bf16[8,128,1024]{2,1,0:T(8,128)(2,1)}, bf16[8,128,1024]{2,1,0:T(8,128)(2,1)}, u32[]{:S(2)}, u32[]{:S(2)}) collective-permute-start(bf16[8,128,1024]{2,1,0:T(8,128)(2,1)} %all-to-all-done.1.refs_9_), channel_id=1, source_target_pairs={{0,8},{8,0},{16,24},{24,16},{32,40},{40,32},{48,56},{56,48},{64,72... | collective-permute-start | bytes 6291464 | tf_op jit(solution)/shard_map/ppermute | solution.py:449
  186.8 1.3 collective-permute-start.21
  188.1 0.7 copy.30.refs_13_
  188.7 2.2 %collective-permute-done.22.refs_10_ = bf16[8,128,1024]{2,1,0:T(8,128)(2,1)} collective-permute-done((bf16[8,128,1024]{2,1,0:T(8,128)(2,1)}, bf16[8,128,1024]{2,1,0:T(8,128)(2,1)}, u32[]{:S(2)}, u32[]{:S(2)}) %collective-permute-start.22) | collective-permute-done | bytes 2097184 | tf_op jit(solution)/shard_map/ppermute | solution.py:449
  190.9 16.2 %shard_map.115 = bf16[768,1024]{1,0:T(8,128)(2,1)} custom-call(s32[3]{0:T(128)} %copy-done.19, bf16[768,1024]{1,0:T(8,128)(2,1)} %bitcast.23, bf16[768,1024]{1,0:T(8,128)(2,1)} %collective-permute-done.3.refs_1_, bf16[768,1024]{1,0:T(8,128)(2,1)} %collective-permute-done.4.refs_2_, bf16[768,1024]{1,0:T(8,128)(2,1)} %collective-permute-done.12.refs_3_, ...), custom_call_target="tpu_custom_call" | custom-call | flops 3221225472 | bytes 25165824 | tf_op jit(solution)/shard_map/pallas_call | solution.py:206
  207.1 1.9 shard_map.116
  (82 shorter events, 6.5 us)
Async XLA Ops:
  7.2 2.1 copy-start.21
  7.2 55.5 %all-gather.2.cloned.1.call-start = ((), (), s32[]{:S(2)}) async-start(), calls=%async_computation.2 | async-start | bytes 4456448 | tf_op jit(solution)/shard_map/all_gather | solution.py:404
  8.5 3.7 %copy-start = (bf16[1,768,1024]{2,1,0:T(8,128)(2,1)S(1)}, bf16[1,768,1024]{2,1,0:T(8,128)(2,1)}, u32[]{:S(2)}) copy-start(bf16[1,768,1024]{2,1,0:T(8,128)(2,1)} %param.8) | copy-start | bytes 4718596
  9.4 53.2 %copy-start.19 = (s32[3]{0:T(128)}, s32[3]{0:T(128)S(1)}, u32[]{:S(2)}) copy-start(s32[3]{0:T(128)S(1)} %pad_add_fusion.place) | copy-start | bytes 40
  10.0 0.7 collective-permute-start
  10.7 47.9 %copy-start.10 = (bf16[128,1536]{1,0:T(8,128)(2,1)}, bf16[128,1536]{1,0:T(8,128)(2,1)S(1)}, u32[]{:S(2)}) copy-start(bf16[128,1536]{1,0:T(8,128)(2,1)S(1)} %constant_dynamic-update-slice_fusion.refs_0_.refs_14_) | copy-start | bytes 1179652
  10.8 8.1 %collective-permute-start.1 = (bf16[128,1536]{1,0:T(8,128)(2,1)S(1)}, bf16[128,1536]{1,0:T(8,128)(2,1)S(1)}, u32[]{:S(2)}, u32[]{:S(2)}) collective-permute-start(bf16[128,1536]{1,0:T(8,128)(2,1)S(1)} %constant_dynamic-update-slice_fusion.refs_0_.refs_14_), channel_id=1, source_target_pairs={{0,1},{1,2},{2,3},{3,4},{4,5},{5,6},{6,7},{7,0},{8,9},{9,10},{10,1... | collective-permute-start | bytes 1179656 | tf_op jit(solution)/shard_map/ppermute | solution.py:41
  11.5 7.4 %collective-permute-start.6 = (bf16[128,1536]{1,0:T(8,128)(2,1)S(1)}, bf16[128,1536]{1,0:T(8,128)(2,1)S(1)}, u32[]{:S(2)}, u32[]{:S(2)}) collective-permute-start(bf16[128,1536]{1,0:T(8,128)(2,1)S(1)} %constant_dynamic-update-slice_fusion.refs_0_.refs_14_), channel_id=1, source_target_pairs={{0,7},{1,0},{2,1},{3,2},{4,3},{5,4},{6,5},{7,6},{8,15},{9,8},{10,9... | collective-permute-start | bytes 1179656 | tf_op jit(solution)/shard_map/ppermute | solution.py:41
  12.2 37.8 %collective-permute-start.3 = (bf16[768,1024]{1,0:T(8,128)(2,1)S(1)}, bf16[768,1024]{1,0:T(8,128)(2,1)}, u32[]{:S(2)}, u32[]{:S(2)}) collective-permute-start(bf16[768,1024]{1,0:T(8,128)(2,1)S(1)} %bitcast.24), channel_id=1, source_target_pairs={{128,129},{129,130},{130,131},{131,132},{132,133},{133,134},{134,1... | collective-permute-start | bytes 4718600 | tf_op jit(solution)/shard_map/ppermute | solution.py:41
  16.9 38.2 %collective-permute-start.4 = (bf16[768,1024]{1,0:T(8,128)(2,1)S(1)}, bf16[768,1024]{1,0:T(8,128)(2,1)}, u32[]{:S(2)}, u32[]{:S(2)}) collective-permute-start(bf16[768,1024]{1,0:T(8,128)(2,1)S(1)} %bitcast.25), channel_id=1, source_target_pairs={{128,135},{129,128},{130,129},{131,130},{132,131},{133,132},{134,1... | collective-permute-start | bytes 4718600 | tf_op jit(solution)/shard_map/ppermute | solution.py:41
  18.9 39.8 %copy-start.15 = (bf16[128,1536]{1,0:T(8,128)(2,1)}, bf16[128,1536]{1,0:T(8,128)(2,1)S(1)}, u32[]{:S(2)}) copy-start(bf16[128,1536]{1,0:T(8,128)(2,1)S(1)} %collective-permute-done.1.refs_1_.refs_15_) | copy-start | bytes 1179652
  18.9 39.7 %copy-start.16 = (bf16[128,1536]{1,0:T(8,128)(2,1)}, bf16[128,1536]{1,0:T(8,128)(2,1)S(1)}, u32[]{:S(2)}) copy-start(bf16[128,1536]{1,0:T(8,128)(2,1)S(1)} %collective-permute-done.6.refs_2_.refs_16_) | copy-start | bytes 1179652
  18.9 39.0 %collective-permute-start.9 = (bf16[768,1024]{1,0:T(8,128)(2,1)S(1)}, bf16[768,1024]{1,0:T(8,128)(2,1)S(1)}, u32[]{:S(2)}, u32[]{:S(2)}) collective-permute-start(bf16[768,1024]{1,0:T(8,128)(2,1)S(1)} %bitcast.26), channel_id=1, source_target_pairs={{0,8},{8,0},{16,24},{24,16},{32,40},{40,32},{48,56},{56,48},{64,72... | collective-permute-start | bytes 4718600 | tf_op jit(solution)/shard_map/ppermute | solution.py:36
  19.7 1.4 collective-permute-start.7
  20.4 35.4 %collective-permute-start.2 = (bf16[128,1536]{1,0:T(8,128)(2,1)S(1)}, bf16[128,1536]{1,0:T(8,128)(2,1)S(1)}, u32[]{:S(2)}, u32[]{:S(2)}) collective-permute-start(bf16[128,1536]{1,0:T(8,128)(2,1)S(1)} %collective-permute-done.1.refs_1_.refs_15_), channel_id=1, source_target_pairs={{0,1},{1,2},{2,3},{3,4},{4,5},{5,6},{6,7},{7,0},{8,9},{9,10},{10,1... | collective-permute-start | bytes 1179656 | tf_op jit(solution)/shard_map/ppermute | solution.py:41
  21.1 37.6 %copy-start.8 = (bf16[128,1536]{1,0:T(8,128)(2,1)}, bf16[128,1536]{1,0:T(8,128)(2,1)S(1)}, u32[]{:S(2)}) copy-start(bf16[128,1536]{1,0:T(8,128)(2,1)S(1)} %collective-permute-done.7.refs_4_.refs_18_) | copy-start | bytes 1179652
  55.1 4.5 %collective-permute-start.8 = (bf16[128,1536]{1,0:T(8,128)(2,1)S(1)}, bf16[128,1536]{1,0:T(8,128)(2,1)S(1)}, u32[]{:S(2)}, u32[]{:S(2)}) collective-permute-start(bf16[128,1536]{1,0:T(8,128)(2,1)S(1)} %collective-permute-done.7.refs_4_.refs_18_), channel_id=1, source_target_pairs={{0,7},{1,0},{2,1},{3,2},{4,3},{5,4},{6,5},{7,6},{8,15},{9,8},{10,9... | collective-permute-start | bytes 1179656 | tf_op jit(solution)/shard_map/ppermute | solution.py:41
  55.8 2.9 %copy-start.9 = (bf16[128,1536]{1,0:T(8,128)(2,1)}, bf16[128,1536]{1,0:T(8,128)(2,1)S(1)}, u32[]{:S(2)}) copy-start(bf16[128,1536]{1,0:T(8,128)(2,1)S(1)} %collective-permute-done.2.refs_3_.refs_17_) | copy-start | bytes 1179652
  55.8 3.8 %collective-permute-start.5 = (bf16[128,1536]{1,0:T(8,128)(2,1)S(1)}, bf16[128,1536]{1,0:T(8,128)(2,1)S(1)}, u32[]{:S(2)}, u32[]{:S(2)}) collective-permute-start(bf16[128,1536]{1,0:T(8,128)(2,1)S(1)} %collective-permute-done.2.refs_3_.refs_17_), channel_id=1, source_target_pairs={{0,1},{1,2},{2,3},{3,4},{4,5},{5,6},{6,7},{7,0},{8,9},{9,10},{10,1... | collective-permute-start | bytes 1179656 | tf_op jit(solution)/shard_map/ppermute | solution.py:41
  56.5 4.8 %collective-permute-start.11 = (bf16[64,1536]{1,0:T(8,128)(2,1)S(1)}, bf16[64,1536]{1,0:T(8,128)(2,1)S(1)}, u32[]{:S(2)}, u32[]{:S(2)}) collective-permute-start(bf16[64,1536]{1,0:T(8,128)(2,1)S(1)} %slice.19), channel_id=1, source_target_pairs={{0,6},{1,7},{2,0},{3,1},{4,2},{5,3},{6,4},{7,5},{8,14},{9,15},{10,... | collective-permute-start | bytes 589832 | tf_op jit(solution)/shard_map/ppermute | solution.py:41
  57.2 4.7 %collective-permute-start.10 = (bf16[64,1536]{1,0:T(8,128)(2,1)S(1)}, bf16[64,1536]{1,0:T(8,128)(2,1)S(1)}, u32[]{:S(2)}, u32[]{:S(2)}) collective-permute-start(bf16[64,1536]{1,0:T(8,128)(2,1)S(1)} %slice.18), channel_id=1, source_target_pairs={{0,2},{1,3},{2,4},{3,5},{4,6},{5,7},{6,0},{7,1},{8,10},{9,11},{10,... | collective-permute-start | bytes 589832 | tf_op jit(solution)/shard_map/ppermute | solution.py:41
  58.7 0.9 copy-start.6
  59.6 0.8 copy-start.4
  59.6 0.9 copy-start.5
  60.5 0.8 copy-start.17
  61.9 0.7 copy-start.13
  62.6 0.9 copy-start.12
  63.6 0.9 copy-start.14
  65.1 31.2 %all-to-all-start = ((bf16[8,128,1024]{2,1,0:T(8,128)(2,1)}), bf16[8,128,1024]{2,1,0:T(8,128)(2,1)}, u32[]{:S(2)}, u32[]{:S(2)}) async-start(bf16[8,128,1024]{2,1,0:T(8,128)(2,1)} %get-tuple-element.48), calls=%async_computation | async-start | bytes 4194304 | tf_op jit(solution)/shard_map/all_to_all | solution.py:408
  70.3 28.0 %copy-start.1 = (f32[64,2,1024]{2,1,0:T(2,128)S(1)}, f32[64,2,1024]{2,1,0:T(2,128)}, u32[]{:S(2)}) copy-start(f32[64,2,1024]{2,1,0:T(2,128)} %master.1) | copy-start | bytes 1572868
  70.3 28.1 %copy-start.2 = (f32[64,2,1024]{2,1,0:T(2,128)S(1)}, f32[64,2,1024]{2,1,0:T(2,128)}, u32[]{:S(2)}) copy-start(f32[64,2,1024]{2,1,0:T(2,128)} %moment2.1) | copy-start | bytes 1572868
  70.3 28.1 %copy-start.3 = (f32[64,2,1024]{2,1,0:T(2,128)S(1)}, f32[64,2,1024]{2,1,0:T(2,128)}, u32[]{:S(2)}) copy-start(f32[64,2,1024]{2,1,0:T(2,128)} %moment1.1) | copy-start | bytes 1572868
  70.3 35.8 %collective-permute-start.12 = (bf16[768,1024]{1,0:T(8,128)(2,1)}, bf16[768,1024]{1,0:T(8,128)(2,1)}, u32[]{:S(2)}, u32[]{:S(2)}) collective-permute-start(bf16[768,1024]{1,0:T(8,128)(2,1)} %collective-permute-done.3.refs_1_), channel_id=1, source_target_pairs={{128,129},{129,130},{130,131},{131,132},{132,133},{133,134},{134,1... | collective-permute-start | bytes 4718600 | tf_op jit(solution)/shard_map/ppermute | solution.py:41
  72.4 36.9 %collective-permute-start.13 = (bf16[768,1024]{1,0:T(8,128)(2,1)}, bf16[768,1024]{1,0:T(8,128)(2,1)}, u32[]{:S(2)}, u32[]{:S(2)}) collective-permute-start(bf16[768,1024]{1,0:T(8,128)(2,1)} %collective-permute-done.4.refs_2_), channel_id=1, source_target_pairs={{128,135},{129,128},{130,129},{131,130},{132,131},{133,132},{134,1... | collective-permute-start | bytes 4718600 | tf_op jit(solution)/shard_map/ppermute | solution.py:41
  98.4 18.8 %copy-start.7 = (bf16[5,128,768]{2,1,0:T(8,128)(2,1)S(1)}, bf16[5,128,768]{2,1,0:T(8,128)(2,1)}, u32[]{:S(2)}) copy-start(bf16[5,128,768]{2,1,0:T(8,128)(2,1)} %copy-done.6) | copy-start | bytes 2949124
  98.4 18.8 %copy-start.18 = (bf16[2,128,768]{2,1,0:T(8,128)(2,1)S(1)}, bf16[2,128,768]{2,1,0:T(8,128)(2,1)}, u32[]{:S(2)}) copy-start(bf16[2,128,768]{2,1,0:T(8,128)(2,1)} %copy-done.17) | copy-start | bytes 1179652
  109.3 44.3 %collective-permute-start.16 = (bf16[768,1024]{1,0:T(8,128)(2,1)}, bf16[768,1024]{1,0:T(8,128)(2,1)}, u32[]{:S(2)}, u32[]{:S(2)}) collective-permute-start(bf16[768,1024]{1,0:T(8,128)(2,1)} %collective-permute-done.12.refs_3_), channel_id=1, source_target_pairs={{128,129},{129,130},{130,131},{131,132},{132,133},{133,134},{134,1... | collective-permute-start | bytes 4718600 | tf_op jit(solution)/shard_map/ppermute | solution.py:41
  111.2 50.0 %collective-permute-start.18 = (bf16[768,1024]{1,0:T(8,128)(2,1)}, bf16[768,1024]{1,0:T(8,128)(2,1)}, u32[]{:S(2)}, u32[]{:S(2)}) collective-permute-start(bf16[768,1024]{1,0:T(8,128)(2,1)} %collective-permute-done.13.refs_4_), channel_id=1, source_target_pairs={{128,135},{129,128},{130,129},{131,130},{132,131},{133,132},{134,1... | collective-permute-start | bytes 4718600 | tf_op jit(solution)/shard_map/ppermute | solution.py:41
  114.6 11.8 %collective-permute-start.14 = (bf16[64,1024]{1,0:T(8,128)(2,1)S(1)}, bf16[64,1024]{1,0:T(8,128)(2,1)S(1)}, u32[]{:S(2)}, u32[]{:S(2)}) collective-permute-start(bf16[64,1024]{1,0:T(8,128)(2,1)S(1)} %get-tuple-element.71), channel_id=1, source_target_pairs={{0,128},{1,144},{2,160},{3,176},{4,192},{5,208},{6,224},{7,240},{8... | collective-permute-start | bytes 393224 | tf_op jit(solution)/shard_map/ppermute | solution.py:425
  115.9 13.1 %collective-permute-start.15 = (bf16[64,1024]{1,0:T(8,128)(2,1)S(1)}, bf16[64,1024]{1,0:T(8,128)(2,1)S(1)}, u32[]{:S(2)}, u32[]{:S(2)}) collective-permute-start(bf16[64,1024]{1,0:T(8,128)(2,1)S(1)} %get-tuple-element.70), channel_id=1, source_target_pairs={{0,192},{1,208},{2,224},{3,240},{4,128},{5,144},{6,160},{7,176},{8... | collective-permute-start | bytes 393224 | tf_op jit(solution)/shard_map/ppermute | solution.py:425
  130.7 46.9 %all-to-all-start.1 = ((bf16[8,128,1024]{2,1,0:T(8,128)(2,1)}), bf16[8,128,1024]{2,1,0:T(8,128)(2,1)}, u32[]{:S(2)}, u32[]{:S(2)}) async-start(bf16[8,128,1024]{2,1,0:T(8,128)(2,1)} %broadcast_in_dim.12), calls=%async_computation.1 | async-start | bytes 4194304 | tf_op jit(solution)/shard_map/all_to_all | solution.py:434
  151.6 13.6 %copy-start.22 = (s32[384]{0:T(512)S(1)}, s32[384]{0:T(512)}, u32[]{:S(2)}) copy-start(s32[384]{0:T(512)} %param.12) | copy-start | bytes 4612
  151.6 14.2 %collective-permute-start.20 = (bf16[8,128,768]{2,1,0:T(8,128)(2,1)}, bf16[8,128,768]{2,1,0:T(8,128)(2,1)}, u32[]{:S(2)}, u32[]{:S(2)}) collective-permute-start(bf16[8,128,768]{2,1,0:T(8,128)(2,1)} %pad_maximum_fusion), channel_id=1, source_target_pairs={{0,8},{8,0},{16,24},{24,16},{32,40},{40,32},{48,56},{56,48},{64,72... | collective-permute-start | bytes 4718600 | tf_op jit(solution)/shard_map/ppermute | solution.py:36
  154.8 22.8 %collective-permute-start.17 = (bf16[384,1024]{1,0:T(8,128)(2,1)S(1)}, bf16[384,1024]{1,0:T(8,128)(2,1)}, u32[]{:S(2)}, u32[]{:S(2)}) collective-permute-start(bf16[384,1024]{1,0:T(8,128)(2,1)S(1)} %slice.24), channel_id=1, source_target_pairs={{128,129},{129,130},{130,131},{131,132},{132,133},{133,134},{134,1... | collective-permute-start | bytes 2359304 | tf_op jit(solution)/shard_map/ppermute | solution.py:41
  163.3 20.8 %collective-permute-start.19 = (bf16[384,1024]{1,0:T(8,128)(2,1)}, bf16[384,1024]{1,0:T(8,128)(2,1)}, u32[]{:S(2)}, u32[]{:S(2)}) collective-permute-start(bf16[384,1024]{1,0:T(8,128)(2,1)} %slice.25), channel_id=1, source_target_pairs={{128,135},{129,128},{130,129},{131,130},{132,131},{133,132},{134,1... | collective-permute-start | bytes 2359304 | tf_op jit(solution)/shard_map/ppermute | solution.py:41
  184.1 6.8 %collective-permute-start.22 = (bf16[8,128,1024]{2,1,0:T(8,128)(2,1)}, bf16[8,128,1024]{2,1,0:T(8,128)(2,1)}, u32[]{:S(2)}, u32[]{:S(2)}) collective-permute-start(bf16[8,128,1024]{2,1,0:T(8,128)(2,1)} %all-to-all-done.1.refs_9_), channel_id=1, source_target_pairs={{0,8},{8,0},{16,24},{24,16},{32,40},{40,32},{48,56},{56,48},{64,72... | collective-permute-start | bytes 6291464 | tf_op jit(solution)/shard_map/ppermute | solution.py:449
  186.8 20.3 %collective-permute-start.21 = (f32[64,2,1024]{2,1,0:T(2,128)S(1)}, f32[64,2,1024]{2,1,0:T(2,128)S(1)}, u32[]{:S(2)}, u32[]{:S(2)}) collective-permute-start(f32[64,2,1024]{2,1,0:T(2,128)S(1)} %bitcast.30), channel_id=1, source_target_pairs={{0,128},{1,129},{2,130},{3,131},{4,132},{5,133},{6,134},{7,135},{8... | collective-permute-start | bytes 1572872 | tf_op jit(solution)/shard_map/ppermute | solution.py:448
  188.7 18.3 %copy-start.20 = (s32[3]{0:T(128)S(1)}, s32[3]{0:T(128)}, u32[]{:S(2)}) copy-start(s32[3]{0:T(128)} %copy-done.19) | copy-start | bytes 40
  (1 other events, 0.7 us)
Sparse Core Ops, SparseCore 0:
  9.9 41.5 all-gather.1

commit v4 on v3

--- a/solution.py
+++ b/solution.py
@@ -48,7 +48,7 @@
     cots, refs = refs[5 : 5 + count], refs[5 + count :]
     cot_other, old, out = refs[:3]
     (
-        hid_v, w_v, q_v, c_v, fresh_v, out_v, limit_v, cot_v, old_v,
+        hid_v, w_v, q_v, c_v, fresh_v, out_v, limit_v, score_v, cot_v, old_v,
         hid_sem, w_sem, q_sem, c_sem, out_sem, cot_sem, old_sem,
     ) = refs[3:]
     tokens, features = q_v.shape
@@ -110,9 +110,38 @@
             loads.append(pltpu.make_async_copy(hids[i], to, hid_sem.at[i]))
         loads.append(pltpu.make_async_copy(queries, q_v, q_sem))
         loads.append(pltpu.make_async_copy(cache, c_v, c_sem))
-        started = 5
-        for load in loads[:started]:
+        *loads, query_load, cache_load = loads
+        started = 6
+        for load in (query_load, cache_load, *loads[:started]):
             load.start()
+        query_load.wait()
+        cache_load.wait()
+
+        width = 128 + SPAN
+        root = 1.0 / math.sqrt(HD)
+        key_at = lax.broadcasted_iota(jnp.int32, (width, heads * SPAN), 0)
+        token = lax.broadcasted_iota(jnp.int32, (width, heads * SPAN), 1) % SPAN
+        new = key_at - 128
+        owner = jnp.where(key_at < 128, key_at // 16, new // STEPS)
+        limit = jnp.where(key_at < 128, key_at % 16, 0)
+        limit = jnp.where(owner == token // STEPS, jnp.where(new <= token, limit, 99), 99)
+        limit_v[...] = limit.astype(jnp.float32)
+
+        def query_of(i):
+            at = slice(i * SPAN, (i + 1) * SPAN)
+            return jnp.concatenate(
+                [q_v[at, h * HD : (h + 1) * HD] for h in range(heads)], axis=0
+            )
+
+        def scores_of(i, keys, low, high):
+            score = lax.dot_general(
+                keys, query_of(i), (((1,), (1,)), ((), ())), preferred_element_type=jnp.float32
+            )
+            return jnp.where(limit_v[low:high] < reach_of[i : i + 1, :], score * root, MASKED)
+
+        for i in range(tokens // SPAN):
+            keys = c_v[i * 8 : (i + 1) * 8, 0].reshape(128, HD)
+            score_v[i] = scores_of(i, keys, 0, 128)
 
         total = None
         arrived = -1
@@ -145,39 +174,16 @@
                 jnp.concatenate([own, other], axis=1),
                 jnp.concatenate([other, own], axis=1),
             ).astype(jnp.bfloat16)
-        loads[-2].wait()
-        loads[-1].wait()
-
-        width = 128 + SPAN
-        root = 1.0 / math.sqrt(HD)
-        key_at = lax.broadcasted_iota(jnp.int32, (width, heads * SPAN), 0)
-        token = lax.broadcasted_iota(jnp.int32, (width, heads * SPAN), 1) % SPAN
-        new = key_at - 128
-        owner = jnp.where(key_at < 128, key_at // 16, new // STEPS)
-        limit = jnp.where(key_at < 128, key_at % 16, 0)
-        limit = jnp.where(owner == token // STEPS, jnp.where(new <= token, limit, 99), 99)
-        limit_v[...] = limit.astype(jnp.float32)
-
         stores = []
         for first in range(0, tokens // SPAN, per):
             ids = range(first, first + per)
             scores = []
             for i in ids:
-                at = slice(i * SPAN, (i + 1) * SPAN)
-                query = jnp.concatenate(
-                    [q_v[at, h * HD : (h + 1) * HD] for h in range(heads)], axis=0
-                )
-                keys = c_v[i * 8 : (i + 1) * 8, 0].reshape(128, HD)
-                keys = jnp.concatenate([keys, fresh_v[0, at]], axis=0)
-                scores.append(
-                    lax.dot_general(
-                        keys, query, (((1,), (1,)), ((), ())), preferred_element_type=jnp.float32
-                    )
-                )
+                keys = fresh_v[0, i * SPAN : (i + 1) * SPAN]
+                scores.append(scores_of(i, keys, 128, width))
             probs = []
             for i, score in zip(ids, scores):
-                seen = limit_v[...] < reach_of[i : i + 1, :]
-                score = jnp.where(seen, score * root, MASKED)
+                score = jnp.concatenate([score_v[i], score], axis=0)
                 score = jnp.exp(score - jnp.max(score, axis=0, keepdims=True))
                 inverse = 1.0 / jnp.sum(score, axis=0, keepdims=True)
                 probs.append((score * inverse).astype(jnp.bfloat16))
@@ -216,6 +222,7 @@
             pltpu.VMEM((2, tokens, HD), jnp.bfloat16),
             pltpu.VMEM((tokens, features), jnp.bfloat16),
             pltpu.VMEM((128 + SPAN, 128), jnp.float32),
+            pltpu.VMEM((tokens // SPAN, 128, 128), jnp.float32),
             pltpu.VMEM((N_TP, 2 * HD, tokens), jnp.bfloat16),
             pltpu.VMEM(old.shape, jnp.bfloat16),
             pltpu.SemaphoreType.DMA((len(HID_PARTS),)),

time: 217 us -> 219 us (level)
  transfers between devices with their start and end apart: 26 -> 26, of which waited for: 10 -> 10; matrix products, arithmetic and copies ran while one was open for 5% -> 5% of each run, Pallas kernels for 8% -> 9%
where the time goes in v4:
time: 219 us; the launch traced here: 218 us
  waiting for transfers between devices  94.6 us (43%)
  starting transfers between devices  67.2 us (31%)
  Pallas kernels  22.4 us (10%)
  between operations  14.7 us (7%)
  local copies, waits for them, and re-layouts  12.3 us (6%)
  other arithmetic  6.5 us (3%)
    ppermute x16, waiting for transfers between devices, along_z(): return lax.ppermute(block, ('group', 'tp'), pairs)  49.6 us
    ppermute x16, starting transfers between devices, along_z(): return lax.ppermute(block, ('group', 'tp'), pairs)  31.1 us
    all_to_all x1, starting transfers between devices, on_device(): lax.all_to_all(jnp.broadcast_to(pieces[None], (8,) + pieces.shape), 'fsdp...  20.9 us
    all_to_all x1, waiting for transfers between devices, on_device(): lax.all_to_all(partial, 'fsdp', 0, 0, axis_index_groups=SAME_CORE)  20.5 us
    pallas_call x1, Pallas kernels, final(): pl.pallas_call(final_kernel, in_specs=in_specs, out_specs=anywhere, out_s...  18 us
    all_to_all x1, waiting for transfers between devices, on_device(): lax.all_to_all(jnp.broadcast_to(pieces[None], (8,) + pieces.shape), 'fsdp...  11.8 us
    ppermute x2, waiting for transfers between devices, across(): return lax.ppermute(rows, ('group', 'fsdp', 'tp'), pairs)  10.5 us
    unnamed x48, local copies, waits for them, and re-layouts  5.31 us
  transfers between devices with their start and end apart: 26, of which 10 were waited for; matrix products, arithmetic and copies ran while one was open for 5% of the time, Pallas kernels for 9%

profile of v4, /device:TPU:121, one launch (start us, length us, event | category | flops | bytes accessed | tf_op | source)
XLA Modules:
  0.0 217.7 jit_solution(2867776625168080098)
XLA Ops:
  7.2 1.3 convert_bitcast_fusion
  8.5 0.7 copy.26
  10.8 0.7 collective-permute-start.1
  11.5 0.7 collective-permute-start.6
  12.2 4.8 %collective-permute-start.3 = (bf16[768,1024]{1,0:T(8,128)(2,1)S(1)}, bf16[768,1024]{1,0:T(8,128)(2,1)}, u32[]{:S(2)}, u32[]{:S(2)}) collective-permute-start(bf16[768,1024]{1,0:T(8,128)(2,1)S(1)} %bitcast.24), channel_id=1, source_target_pairs={{128,129},{129,130},{130,131},{131,132},{132,133},{133,134},{134,1... | collective-permute-start | bytes 4718600 | tf_op jit(solution)/shard_map/ppermute | solution.py:41
  16.9 1.9 collective-permute-start.4
  18.9 0.8 collective-permute-start.9
  19.7 0.7 collective-permute-start.7
  20.4 0.7 collective-permute-start.2
  21.1 28.9 %collective-permute-done.3.refs_1_ = bf16[768,1024]{1,0:T(8,128)(2,1)} collective-permute-done((bf16[768,1024]{1,0:T(8,128)(2,1)S(1)}, bf16[768,1024]{1,0:T(8,128)(2,1)}, u32[]{:S(2)}, u32[]{:S(2)}) %collective-permute-start.3) | collective-permute-done | bytes 1572896 | tf_op jit(solution)/shard_map/ppermute | solution.py:41
  50.0 5.1 %collective-permute-done.4.refs_2_ = bf16[768,1024]{1,0:T(8,128)(2,1)} collective-permute-done((bf16[768,1024]{1,0:T(8,128)(2,1)S(1)}, bf16[768,1024]{1,0:T(8,128)(2,1)}, u32[]{:S(2)}, u32[]{:S(2)}) %collective-permute-start.4) | collective-permute-done | bytes 1572896 | tf_op jit(solution)/shard_map/ppermute | solution.py:41
  55.8 0.7 collective-permute-start.5
  57.9 0.7 shard_map.112
  58.7 0.9 copy-done.6
  60.5 0.8 copy-done.17
  61.9 0.7 copy-done.13
  62.6 0.9 copy-done.12
  63.6 0.9 copy-done.14
  65.1 5.2 %all-to-all-start = ((bf16[8,128,1024]{2,1,0:T(8,128)(2,1)}), bf16[8,128,1024]{2,1,0:T(8,128)(2,1)}, u32[]{:S(2)}, u32[]{:S(2)}) async-start(bf16[8,128,1024]{2,1,0:T(8,128)(2,1)} %get-tuple-element.48), calls=%async_computation | async-start | bytes 4194304 | tf_op jit(solution)/shard_map/all_to_all | solution.py:415
  70.3 2.1 collective-permute-start.12
  72.4 3.4 %collective-permute-start.13 = (bf16[768,1024]{1,0:T(8,128)(2,1)}, bf16[768,1024]{1,0:T(8,128)(2,1)}, u32[]{:S(2)}, u32[]{:S(2)}) collective-permute-start(bf16[768,1024]{1,0:T(8,128)(2,1)} %collective-permute-done.4.refs_2_), channel_id=1, source_target_pairs={{128,135},{129,128},{130,129},{131,130},{132,131},{133,132},{134,1... | collective-permute-start | bytes 4718600 | tf_op jit(solution)/shard_map/ppermute | solution.py:41
  75.8 20.5 %all-to-all-done = bf16[8,128,1024]{2,1,0:T(8,128)(2,1)} async-done(((bf16[8,128,1024]{2,1,0:T(8,128)(2,1)}), bf16[8,128,1024]{2,1,0:T(8,128)(2,1)}, u32[]{:S(2)}, u32[]{:S(2)}) %all-to-all-start) | async-done | bytes 2097184 | tf_op jit(solution)/shard_map/all_to_all | solution.py:415
  96.3 2.0 convert_reduce_fusion
  98.4 1.7 fusion.3
  100.2 5.9 %collective-permute-done.12.refs_3_ = bf16[768,1024]{1,0:T(8,128)(2,1)} collective-permute-done((bf16[768,1024]{1,0:T(8,128)(2,1)}, bf16[768,1024]{1,0:T(8,128)(2,1)}, u32[]{:S(2)}, u32[]{:S(2)}) %collective-permute-start.12) | collective-permute-done | bytes 1572896 | tf_op jit(solution)/shard_map/ppermute | solution.py:41
  106.1 3.1 %collective-permute-done.13.refs_4_ = bf16[768,1024]{1,0:T(8,128)(2,1)} collective-permute-done((bf16[768,1024]{1,0:T(8,128)(2,1)}, bf16[768,1024]{1,0:T(8,128)(2,1)}, u32[]{:S(2)}, u32[]{:S(2)}) %collective-permute-start.13) | collective-permute-done | bytes 1572896 | tf_op jit(solution)/shard_map/ppermute | solution.py:41
  109.3 1.9 collective-permute-start.16
  111.2 3.4 %collective-permute-start.18 = (bf16[768,1024]{1,0:T(8,128)(2,1)}, bf16[768,1024]{1,0:T(8,128)(2,1)}, u32[]{:S(2)}, u32[]{:S(2)}) collective-permute-start(bf16[768,1024]{1,0:T(8,128)(2,1)} %collective-permute-done.13.refs_4_), channel_id=1, source_target_pairs={{128,135},{129,128},{130,129},{131,130},{132,131},{133,132},{134,1... | collective-permute-start | bytes 4718600 | tf_op jit(solution)/shard_map/ppermute | solution.py:41
  114.6 1.3 collective-permute-start.14
  115.9 1.3 collective-permute-start.15
  117.2 1.3 pad_maximum_fusion
  118.6 7.9 %collective-permute-done.14 = bf16[64,1024]{1,0:T(8,128)(2,1)S(1)} collective-permute-done((bf16[64,1024]{1,0:T(8,128)(2,1)S(1)}, bf16[64,1024]{1,0:T(8,128)(2,1)S(1)}, u32[]{:S(2)}, u32[]{:S(2)}) %collective-permute-start.14) | collective-permute-done | bytes 131104 | tf_op jit(solution)/shard_map/ppermute | solution.py:432
  126.4 2.6 %collective-permute-done.15 = bf16[64,1024]{1,0:T(8,128)(2,1)S(1)} collective-permute-done((bf16[64,1024]{1,0:T(8,128)(2,1)S(1)}, bf16[64,1024]{1,0:T(8,128)(2,1)S(1)}, u32[]{:S(2)}, u32[]{:S(2)}) %collective-permute-start.15) | collective-permute-done | bytes 131104 | tf_op jit(solution)/shard_map/ppermute | solution.py:432
  129.1 1.6 broadcast_in_dim.12
  130.7 20.9 %all-to-all-start.1 = ((bf16[8,128,1024]{2,1,0:T(8,128)(2,1)}), bf16[8,128,1024]{2,1,0:T(8,128)(2,1)}, u32[]{:S(2)}, u32[]{:S(2)}) async-start(bf16[8,128,1024]{2,1,0:T(8,128)(2,1)} %broadcast_in_dim.12), calls=%async_computation.1 | async-start | bytes 4194304 | tf_op jit(solution)/shard_map/all_to_all | solution.py:441
  151.6 1.9 collective-permute-start.20
  153.6 1.2 slice.24
  154.8 6.4 %collective-permute-start.17 = (bf16[384,1024]{1,0:T(8,128)(2,1)S(1)}, bf16[384,1024]{1,0:T(8,128)(2,1)}, u32[]{:S(2)}, u32[]{:S(2)}) collective-permute-start(bf16[384,1024]{1,0:T(8,128)(2,1)S(1)} %slice.24), channel_id=1, source_target_pairs={{128,129},{129,130},{130,131},{131,132},{132,133},{133,134},{134,1... | collective-permute-start | bytes 2359304 | tf_op jit(solution)/shard_map/ppermute | solution.py:41
  161.2 2.1 slice.25
  163.3 1.9 collective-permute-start.19
  165.8 11.8 %all-to-all-done.1.refs_9_ = bf16[8,128,1024]{2,1,0:T(8,128)(2,1)} async-done(((bf16[8,128,1024]{2,1,0:T(8,128)(2,1)}), bf16[8,128,1024]{2,1,0:T(8,128)(2,1)}, u32[]{:S(2)}, u32[]{:S(2)}) %all-to-all-start.1) | async-done | bytes 2097184 | tf_op jit(solution)/shard_map/all_to_all | solution.py:441
  177.6 6.5 %collective-permute-done.19.refs_8_ = bf16[384,1024]{1,0:T(8,128)(2,1)} collective-permute-done((bf16[384,1024]{1,0:T(8,128)(2,1)}, bf16[384,1024]{1,0:T(8,128)(2,1)}, u32[]{:S(2)}, u32[]{:S(2)}) %collective-permute-start.19) | collective-permute-done | bytes 786464 | tf_op jit(solution)/shard_map/ppermute | solution.py:41
  184.1 2.6 %collective-permute-start.22 = (bf16[8,128,1024]{2,1,0:T(8,128)(2,1)}, bf16[8,128,1024]{2,1,0:T(8,128)(2,1)}, u32[]{:S(2)}, u32[]{:S(2)}) collective-permute-start(bf16[8,128,1024]{2,1,0:T(8,128)(2,1)} %all-to-all-done.1.refs_9_), channel_id=1, source_target_pairs={{0,8},{8,0},{16,24},{24,16},{32,40},{40,32},{48,56},{56,48},{64,72... | collective-permute-start | bytes 6291464 | tf_op jit(solution)/shard_map/ppermute | solution.py:456
  186.8 1.3 collective-permute-start.21
  188.1 0.7 copy.30.refs_13_
  188.7 2.2 collective-permute-done.22.refs_10_
  190.9 18.0 %shard_map.115 = bf16[768,1024]{1,0:T(8,128)(2,1)} custom-call(s32[3]{0:T(128)} %copy-done.19, bf16[768,1024]{1,0:T(8,128)(2,1)} %bitcast.23, bf16[768,1024]{1,0:T(8,128)(2,1)} %collective-permute-done.3.refs_1_, bf16[768,1024]{1,0:T(8,128)(2,1)} %collective-permute-done.4.refs_2_, bf16[768,1024]{1,0:T(8,128)(2,1)} %collective-permute-done.12.refs_3_, ...), custom_call_target="tpu_custom_call" | custom-call | flops 3221225472 | bytes 25165824 | tf_op jit(solution)/shard_map/pallas_call | solution.py:212
  208.9 1.9 shard_map.116
  (82 shorter events, 6.5 us)
Async XLA Ops:
  7.2 2.1 copy-start.21
  7.2 55.5 %all-gather.2.cloned.1.call-start = ((), (), s32[]{:S(2)}) async-start(), calls=%async_computation.2 | async-start | bytes 4456448 | tf_op jit(solution)/shard_map/all_gather | solution.py:411
  8.5 3.7 %copy-start = (bf16[1,768,1024]{2,1,0:T(8,128)(2,1)S(1)}, bf16[1,768,1024]{2,1,0:T(8,128)(2,1)}, u32[]{:S(2)}) copy-start(bf16[1,768,1024]{2,1,0:T(8,128)(2,1)} %param.8) | copy-start | bytes 4718596
  9.4 53.2 %copy-start.19 = (s32[3]{0:T(128)}, s32[3]{0:T(128)S(1)}, u32[]{:S(2)}) copy-start(s32[3]{0:T(128)S(1)} %pad_add_fusion.place) | copy-start | bytes 40
  10.0 0.7 collective-permute-start
  10.7 47.9 %copy-start.10 = (bf16[128,1536]{1,0:T(8,128)(2,1)}, bf16[128,1536]{1,0:T(8,128)(2,1)S(1)}, u32[]{:S(2)}) copy-start(bf16[128,1536]{1,0:T(8,128)(2,1)S(1)} %constant_dynamic-update-slice_fusion.refs_0_.refs_14_) | copy-start | bytes 1179652
  10.8 8.1 %collective-permute-start.1 = (bf16[128,1536]{1,0:T(8,128)(2,1)S(1)}, bf16[128,1536]{1,0:T(8,128)(2,1)S(1)}, u32[]{:S(2)}, u32[]{:S(2)}) collective-permute-start(bf16[128,1536]{1,0:T(8,128)(2,1)S(1)} %constant_dynamic-update-slice_fusion.refs_0_.refs_14_), channel_id=1, source_target_pairs={{0,1},{1,2},{2,3},{3,4},{4,5},{5,6},{6,7},{7,0},{8,9},{9,10},{10,1... | collective-permute-start | bytes 1179656 | tf_op jit(solution)/shard_map/ppermute | solution.py:41
  11.5 7.4 %collective-permute-start.6 = (bf16[128,1536]{1,0:T(8,128)(2,1)S(1)}, bf16[128,1536]{1,0:T(8,128)(2,1)S(1)}, u32[]{:S(2)}, u32[]{:S(2)}) collective-permute-start(bf16[128,1536]{1,0:T(8,128)(2,1)S(1)} %constant_dynamic-update-slice_fusion.refs_0_.refs_14_), channel_id=1, source_target_pairs={{0,7},{1,0},{2,1},{3,2},{4,3},{5,4},{6,5},{7,6},{8,15},{9,8},{10,9... | collective-permute-start | bytes 1179656 | tf_op jit(solution)/shard_map/ppermute | solution.py:41
  12.2 37.8 %collective-permute-start.3 = (bf16[768,1024]{1,0:T(8,128)(2,1)S(1)}, bf16[768,1024]{1,0:T(8,128)(2,1)}, u32[]{:S(2)}, u32[]{:S(2)}) collective-permute-start(bf16[768,1024]{1,0:T(8,128)(2,1)S(1)} %bitcast.24), channel_id=1, source_target_pairs={{128,129},{129,130},{130,131},{131,132},{132,133},{133,134},{134,1... | collective-permute-start | bytes 4718600 | tf_op jit(solution)/shard_map/ppermute | solution.py:41
  16.9 38.2 %collective-permute-start.4 = (bf16[768,1024]{1,0:T(8,128)(2,1)S(1)}, bf16[768,1024]{1,0:T(8,128)(2,1)}, u32[]{:S(2)}, u32[]{:S(2)}) collective-permute-start(bf16[768,1024]{1,0:T(8,128)(2,1)S(1)} %bitcast.25), channel_id=1, source_target_pairs={{128,135},{129,128},{130,129},{131,130},{132,131},{133,132},{134,1... | collective-permute-start | bytes 4718600 | tf_op jit(solution)/shard_map/ppermute | solution.py:41
  18.9 39.8 %copy-start.15 = (bf16[128,1536]{1,0:T(8,128)(2,1)}, bf16[128,1536]{1,0:T(8,128)(2,1)S(1)}, u32[]{:S(2)}) copy-start(bf16[128,1536]{1,0:T(8,128)(2,1)S(1)} %collective-permute-done.1.refs_1_.refs_15_) | copy-start | bytes 1179652
  18.9 39.7 %copy-start.16 = (bf16[128,1536]{1,0:T(8,128)(2,1)}, bf16[128,1536]{1,0:T(8,128)(2,1)S(1)}, u32[]{:S(2)}) copy-start(bf16[128,1536]{1,0:T(8,128)(2,1)S(1)} %collective-permute-done.6.refs_2_.refs_16_) | copy-start | bytes 1179652
  18.9 39.0 %collective-permute-start.9 = (bf16[768,1024]{1,0:T(8,128)(2,1)S(1)}, bf16[768,1024]{1,0:T(8,128)(2,1)S(1)}, u32[]{:S(2)}, u32[]{:S(2)}) collective-permute-start(bf16[768,1024]{1,0:T(8,128)(2,1)S(1)} %bitcast.26), channel_id=1, source_target_pairs={{0,8},{8,0},{16,24},{24,16},{32,40},{40,32},{48,56},{56,48},{64,72... | collective-permute-start | bytes 4718600 | tf_op jit(solution)/shard_map/ppermute | solution.py:36
  19.7 1.4 collective-permute-start.7
  20.4 35.4 %collective-permute-start.2 = (bf16[128,1536]{1,0:T(8,128)(2,1)S(1)}, bf16[128,1536]{1,0:T(8,128)(2,1)S(1)}, u32[]{:S(2)}, u32[]{:S(2)}) collective-permute-start(bf16[128,1536]{1,0:T(8,128)(2,1)S(1)} %collective-permute-done.1.refs_1_.refs_15_), channel_id=1, source_target_pairs={{0,1},{1,2},{2,3},{3,4},{4,5},{5,6},{6,7},{7,0},{8,9},{9,10},{10,1... | collective-permute-start | bytes 1179656 | tf_op jit(solution)/shard_map/ppermute | solution.py:41
  21.1 37.6 %copy-start.8 = (bf16[128,1536]{1,0:T(8,128)(2,1)}, bf16[128,1536]{1,0:T(8,128)(2,1)S(1)}, u32[]{:S(2)}) copy-start(bf16[128,1536]{1,0:T(8,128)(2,1)S(1)} %collective-permute-done.7.refs_4_.refs_18_) | copy-start | bytes 1179652
  55.1 4.5 %collective-permute-start.8 = (bf16[128,1536]{1,0:T(8,128)(2,1)S(1)}, bf16[128,1536]{1,0:T(8,128)(2,1)S(1)}, u32[]{:S(2)}, u32[]{:S(2)}) collective-permute-start(bf16[128,1536]{1,0:T(8,128)(2,1)S(1)} %collective-permute-done.7.refs_4_.refs_18_), channel_id=1, source_target_pairs={{0,7},{1,0},{2,1},{3,2},{4,3},{5,4},{6,5},{7,6},{8,15},{9,8},{10,9... | collective-permute-start | bytes 1179656 | tf_op jit(solution)/shard_map/ppermute | solution.py:41
  55.8 2.9 %copy-start.9 = (bf16[128,1536]{1,0:T(8,128)(2,1)}, bf16[128,1536]{1,0:T(8,128)(2,1)S(1)}, u32[]{:S(2)}) copy-start(bf16[128,1536]{1,0:T(8,128)(2,1)S(1)} %collective-permute-done.2.refs_3_.refs_17_) | copy-start | bytes 1179652
  55.8 3.8 %collective-permute-start.5 = (bf16[128,1536]{1,0:T(8,128)(2,1)S(1)}, bf16[128,1536]{1,0:T(8,128)(2,1)S(1)}, u32[]{:S(2)}, u32[]{:S(2)}) collective-permute-start(bf16[128,1536]{1,0:T(8,128)(2,1)S(1)} %collective-permute-done.2.refs_3_.refs_17_), channel_id=1, source_target_pairs={{0,1},{1,2},{2,3},{3,4},{4,5},{5,6},{6,7},{7,0},{8,9},{9,10},{10,1... | collective-permute-start | bytes 1179656 | tf_op jit(solution)/shard_map/ppermute | solution.py:41
  56.5 4.8 %collective-permute-start.11 = (bf16[64,1536]{1,0:T(8,128)(2,1)S(1)}, bf16[64,1536]{1,0:T(8,128)(2,1)S(1)}, u32[]{:S(2)}, u32[]{:S(2)}) collective-permute-start(bf16[64,1536]{1,0:T(8,128)(2,1)S(1)} %slice.19), channel_id=1, source_target_pairs={{0,6},{1,7},{2,0},{3,1},{4,2},{5,3},{6,4},{7,5},{8,14},{9,15},{10,... | collective-permute-start | bytes 589832 | tf_op jit(solution)/shard_map/ppermute | solution.py:41
  57.2 4.7 %collective-permute-start.10 = (bf16[64,1536]{1,0:T(8,128)(2,1)S(1)}, bf16[64,1536]{1,0:T(8,128)(2,1)S(1)}, u32[]{:S(2)}, u32[]{:S(2)}) collective-permute-start(bf16[64,1536]{1,0:T(8,128)(2,1)S(1)} %slice.18), channel_id=1, source_target_pairs={{0,2},{1,3},{2,4},{3,5},{4,6},{5,7},{6,0},{7,1},{8,10},{9,11},{10,... | collective-permute-start | bytes 589832 | tf_op jit(solution)/shard_map/ppermute | solution.py:41
  58.7 0.9 copy-start.6
  59.6 0.8 copy-start.4
  59.6 0.9 copy-start.5
  60.5 0.8 copy-start.17
  61.9 0.7 copy-start.13
  62.6 0.9 copy-start.12
  63.6 0.9 copy-start.14
  65.1 31.2 %all-to-all-start = ((bf16[8,128,1024]{2,1,0:T(8,128)(2,1)}), bf16[8,128,1024]{2,1,0:T(8,128)(2,1)}, u32[]{:S(2)}, u32[]{:S(2)}) async-start(bf16[8,128,1024]{2,1,0:T(8,128)(2,1)} %get-tuple-element.48), calls=%async_computation | async-start | bytes 4194304 | tf_op jit(solution)/shard_map/all_to_all | solution.py:415
  70.3 28.0 %copy-start.1 = (f32[64,2,1024]{2,1,0:T(2,128)S(1)}, f32[64,2,1024]{2,1,0:T(2,128)}, u32[]{:S(2)}) copy-start(f32[64,2,1024]{2,1,0:T(2,128)} %master.1) | copy-start | bytes 1572868
  70.3 28.1 %copy-start.2 = (f32[64,2,1024]{2,1,0:T(2,128)S(1)}, f32[64,2,1024]{2,1,0:T(2,128)}, u32[]{:S(2)}) copy-start(f32[64,2,1024]{2,1,0:T(2,128)} %moment2.1) | copy-start | bytes 1572868
  70.3 28.1 %copy-start.3 = (f32[64,2,1024]{2,1,0:T(2,128)S(1)}, f32[64,2,1024]{2,1,0:T(2,128)}, u32[]{:S(2)}) copy-start(f32[64,2,1024]{2,1,0:T(2,128)} %moment1.1) | copy-start | bytes 1572868
  70.3 35.8 %collective-permute-start.12 = (bf16[768,1024]{1,0:T(8,128)(2,1)}, bf16[768,1024]{1,0:T(8,128)(2,1)}, u32[]{:S(2)}, u32[]{:S(2)}) collective-permute-start(bf16[768,1024]{1,0:T(8,128)(2,1)} %collective-permute-done.3.refs_1_), channel_id=1, source_target_pairs={{128,129},{129,130},{130,131},{131,132},{132,133},{133,134},{134,1... | collective-permute-start | bytes 4718600 | tf_op jit(solution)/shard_map/ppermute | solution.py:41
  72.4 36.9 %collective-permute-start.13 = (bf16[768,1024]{1,0:T(8,128)(2,1)}, bf16[768,1024]{1,0:T(8,128)(2,1)}, u32[]{:S(2)}, u32[]{:S(2)}) collective-permute-start(bf16[768,1024]{1,0:T(8,128)(2,1)} %collective-permute-done.4.refs_2_), channel_id=1, source_target_pairs={{128,135},{129,128},{130,129},{131,130},{132,131},{133,132},{134,1... | collective-permute-start | bytes 4718600 | tf_op jit(solution)/shard_map/ppermute | solution.py:41
  98.4 18.8 %copy-start.7 = (bf16[5,128,768]{2,1,0:T(8,128)(2,1)S(1)}, bf16[5,128,768]{2,1,0:T(8,128)(2,1)}, u32[]{:S(2)}) copy-start(bf16[5,128,768]{2,1,0:T(8,128)(2,1)} %copy-done.6) | copy-start | bytes 2949124
  98.4 18.8 %copy-start.18 = (bf16[2,128,768]{2,1,0:T(8,128)(2,1)S(1)}, bf16[2,128,768]{2,1,0:T(8,128)(2,1)}, u32[]{:S(2)}) copy-start(bf16[2,128,768]{2,1,0:T(8,128)(2,1)} %copy-done.17) | copy-start | bytes 1179652
  109.3 44.3 %collective-permute-start.16 = (bf16[768,1024]{1,0:T(8,128)(2,1)}, bf16[768,1024]{1,0:T(8,128)(2,1)}, u32[]{:S(2)}, u32[]{:S(2)}) collective-permute-start(bf16[768,1024]{1,0:T(8,128)(2,1)} %collective-permute-done.12.refs_3_), channel_id=1, source_target_pairs={{128,129},{129,130},{130,131},{131,132},{132,133},{133,134},{134,1... | collective-permute-start | bytes 4718600 | tf_op jit(solution)/shard_map/ppermute | solution.py:41
  111.2 50.0 %collective-permute-start.18 = (bf16[768,1024]{1,0:T(8,128)(2,1)}, bf16[768,1024]{1,0:T(8,128)(2,1)}, u32[]{:S(2)}, u32[]{:S(2)}) collective-permute-start(bf16[768,1024]{1,0:T(8,128)(2,1)} %collective-permute-done.13.refs_4_), channel_id=1, source_target_pairs={{128,135},{129,128},{130,129},{131,130},{132,131},{133,132},{134,1... | collective-permute-start | bytes 4718600 | tf_op jit(solution)/shard_map/ppermute | solution.py:41
  114.6 11.8 %collective-permute-start.14 = (bf16[64,1024]{1,0:T(8,128)(2,1)S(1)}, bf16[64,1024]{1,0:T(8,128)(2,1)S(1)}, u32[]{:S(2)}, u32[]{:S(2)}) collective-permute-start(bf16[64,1024]{1,0:T(8,128)(2,1)S(1)} %get-tuple-element.71), channel_id=1, source_target_pairs={{0,128},{1,144},{2,160},{3,176},{4,192},{5,208},{6,224},{7,240},{8... | collective-permute-start | bytes 393224 | tf_op jit(solution)/shard_map/ppermute | solution.py:432
  115.9 13.1 %collective-permute-start.15 = (bf16[64,1024]{1,0:T(8,128)(2,1)S(1)}, bf16[64,1024]{1,0:T(8,128)(2,1)S(1)}, u32[]{:S(2)}, u32[]{:S(2)}) collective-permute-start(bf16[64,1024]{1,0:T(8,128)(2,1)S(1)} %get-tuple-element.70), channel_id=1, source_target_pairs={{0,192},{1,208},{2,224},{3,240},{4,128},{5,144},{6,160},{7,176},{8... | collective-permute-start | bytes 393224 | tf_op jit(solution)/shard_map/ppermute | solution.py:432
  130.7 46.9 %all-to-all-start.1 = ((bf16[8,128,1024]{2,1,0:T(8,128)(2,1)}), bf16[8,128,1024]{2,1,0:T(8,128)(2,1)}, u32[]{:S(2)}, u32[]{:S(2)}) async-start(bf16[8,128,1024]{2,1,0:T(8,128)(2,1)} %broadcast_in_dim.12), calls=%async_computation.1 | async-start | bytes 4194304 | tf_op jit(solution)/shard_map/all_to_all | solution.py:441
  151.6 13.6 %copy-start.22 = (s32[384]{0:T(512)S(1)}, s32[384]{0:T(512)}, u32[]{:S(2)}) copy-start(s32[384]{0:T(512)} %param.12) | copy-start | bytes 4612
  151.6 14.2 %collective-permute-start.20 = (bf16[8,128,768]{2,1,0:T(8,128)(2,1)}, bf16[8,128,768]{2,1,0:T(8,128)(2,1)}, u32[]{:S(2)}, u32[]{:S(2)}) collective-permute-start(bf16[8,128,768]{2,1,0:T(8,128)(2,1)} %pad_maximum_fusion), channel_id=1, source_target_pairs={{0,8},{8,0},{16,24},{24,16},{32,40},{40,32},{48,56},{56,48},{64,72... | collective-permute-start | bytes 4718600 | tf_op jit(solution)/shard_map/ppermute | solution.py:36
  154.8 22.8 %collective-permute-start.17 = (bf16[384,1024]{1,0:T(8,128)(2,1)S(1)}, bf16[384,1024]{1,0:T(8,128)(2,1)}, u32[]{:S(2)}, u32[]{:S(2)}) collective-permute-start(bf16[384,1024]{1,0:T(8,128)(2,1)S(1)} %slice.24), channel_id=1, source_target_pairs={{128,129},{129,130},{130,131},{131,132},{132,133},{133,134},{134,1... | collective-permute-start | bytes 2359304 | tf_op jit(solution)/shard_map/ppermute | solution.py:41
  163.3 20.8 %collective-permute-start.19 = (bf16[384,1024]{1,0:T(8,128)(2,1)}, bf16[384,1024]{1,0:T(8,128)(2,1)}, u32[]{:S(2)}, u32[]{:S(2)}) collective-permute-start(bf16[384,1024]{1,0:T(8,128)(2,1)} %slice.25), channel_id=1, source_target_pairs={{128,135},{129,128},{130,129},{131,130},{132,131},{133,132},{134,1... | collective-permute-start | bytes 2359304 | tf_op jit(solution)/shard_map/ppermute | solution.py:41
  184.1 6.8 %collective-permute-start.22 = (bf16[8,128,1024]{2,1,0:T(8,128)(2,1)}, bf16[8,128,1024]{2,1,0:T(8,128)(2,1)}, u32[]{:S(2)}, u32[]{:S(2)}) collective-permute-start(bf16[8,128,1024]{2,1,0:T(8,128)(2,1)} %all-to-all-done.1.refs_9_), channel_id=1, source_target_pairs={{0,8},{8,0},{16,24},{24,16},{32,40},{40,32},{48,56},{56,48},{64,72... | collective-permute-start | bytes 6291464 | tf_op jit(solution)/shard_map/ppermute | solution.py:456
  186.8 22.2 %collective-permute-start.21 = (f32[64,2,1024]{2,1,0:T(2,128)S(1)}, f32[64,2,1024]{2,1,0:T(2,128)S(1)}, u32[]{:S(2)}, u32[]{:S(2)}) collective-permute-start(f32[64,2,1024]{2,1,0:T(2,128)S(1)} %bitcast.30), channel_id=1, source_target_pairs={{0,128},{1,129},{2,130},{3,131},{4,132},{5,133},{6,134},{7,135},{8... | collective-permute-start | bytes 1572872 | tf_op jit(solution)/shard_map/ppermute | solution.py:455
  188.7 20.2 %copy-start.20 = (s32[3]{0:T(128)S(1)}, s32[3]{0:T(128)}, u32[]{:S(2)}) copy-start(s32[3]{0:T(128)} %copy-done.19) | copy-start | bytes 40
  (1 other events, 0.7 us)
Sparse Core Ops, SparseCore 0:
  9.9 41.5 all-gather.1
